TPU v7x, 32 devices: a whole 2x2x4 slice. The times are simulated.
32 devices in a mesh: gx: 4 (over z), gy: 8 (over y, x, core).
Axes of the slice: x: 2, y: 2, z: 4, core: 2. Of those that a mesh axis runs over, the one named last changes fastest.
Arguments:
- center_points: float32 [3, 8192], P(None, ('gx', 'gy')), may hold values from 0 to 1
- displacements: float32 [3, 8192], P(None, ('gx', 'gy')), may hold values from -24 to 24
- edge_points: float32 [3, 32768], P(None, ('gx', 'gy')), may hold values from 0 to 1
- send_list: int32 [32, 8, 6], P(('gx', 'gy')), may hold values from -1 to 15, as said below
- block_tiles: int32 [128, 12], P(('gx', 'gy')), may hold values from 0 to 47, as said below
- block_count: int32 [32], P(('gx', 'gy')), may hold values from 1 to 4, as said below
Outputs:
- coefficients: float32 [3, 8192], P(None, ('gx', 'gy'))
- block_motion: float32 [128, 3, 64, 4096], P(('gx', 'gy'))
Inputs may be any that keep to these rules, and one draw needn't show every extreme that they name: `send_list`: A zone is the 8 devices that share a gx index. Entry [s, r, c] names the local edge that device s sends to device r of its zone in position c, or -1 where that position carries nothing. Every position that a live block slot names carries an edge. `block_tiles`: the entry for a block slot and edge is the position s * 6 + c, in the tiles that reach the block's device, of the tile sent by device s of its zone in position c; the 48 entries of one device are all distinct, so a device with 4 live blocks receives 6 tiles from every device of its zone. `block_count`: the live slots of a device are its first ones; in every zone some device holds 4 blocks.
All inputs are finite; a program needn't handle non-finite values.
Results may differ from a plain program's by a relative error of at most 0.0003.
Values sent between devices are 32-bit elements; how exact they have to be, the bound alone decides.
No kernel may reach another device: no remote copies, remote signals or barrier semaphores. Data moves between devices by JAX's collectives and lax.ppermute only.
A program may use at most 128 MiB of HBM per device.

v0:
```python
import math

import jax
import jax.numpy as jnp
from jax import lax
from jax.sharding import PartitionSpec as P

S = 64
ITERS = 3
SLOTS = 4
EDGE_DEV = 16


RADIUS = 0.25
SHIFT = 0.1
HIGHEST_PREC = lax.Precision.HIGHEST


def pair_distance(left_points, right_points):
    squared = (left_points[0][:, None] - right_points[0][None, :]) ** 2
    squared = squared + (left_points[1][:, None] - right_points[1][None, :]) ** 2
    squared = squared + (left_points[2][:, None] - right_points[2][None, :]) ** 2
    return squared


def wendland(squared):
    radial = jnp.sqrt(squared) / RADIUS
    remain = jnp.maximum(1.0 - radial, 0.0)
    return remain**4 * (4.0 * radial + 1.0)


def transfinite(edge_tiles):
    extent = edge_tiles.shape[2]
    fraction = jnp.arange(extent).astype(jnp.float32) / (extent - 1)
    blends = jnp.stack([1.0 - fraction, fraction])
    pair_weight = (blends[None, :, :, None] * blends[:, None, None, :]).reshape(4, extent, extent)
    first_dir = edge_tiles[:, 0:4]
    second_dir = edge_tiles[:, 4:8]
    third_dir = edge_tiles[:, 8:12]
    straight = (
        blends[0][None, None, :] * first_dir[:, :, 0:1]
        + blends[1][None, None, :] * first_dir[:, :, extent - 1 : extent]
    )
    result = jnp.einsum(
        "cei,ejk->cijk", first_dir - 2.0 * straight, pair_weight, precision=HIGHEST_PREC
    )
    result = result + jnp.einsum("cej,eik->cijk", second_dir, pair_weight, precision=HIGHEST_PREC)
    result = result + jnp.einsum("cek,eij->cijk", third_dir, pair_weight, precision=HIGHEST_PREC)
    return result.reshape(3, extent, extent * extent)


def conjugate(right_side, matvec, global_sum):
    norm_start = global_sum(jnp.sum(right_side * right_side, axis=1, keepdims=True))

    def cg_turn(iteration, cg_state):
        iterate, remain, search, norm_now = cg_state
        applied = matvec(search)
        step_size = norm_now / global_sum(jnp.sum(search * applied, axis=1, keepdims=True))
        iterate = iterate + step_size * search
        remain = remain - step_size * applied
        norm_next = global_sum(jnp.sum(remain * remain, axis=1, keepdims=True))
        search = remain + norm_next / norm_now * search
        return (iterate, remain, search, norm_next)

    cg_state = lax.fori_loop(
        0, ITERS, cg_turn, (jnp.zeros_like(right_side), right_side, right_side, norm_start)
    )
    return cg_state[0]


def row_product(full_search, kernel):
    return lax.dot_general(full_search, kernel, (((1,), (1,)), ((), ())), precision=HIGHEST_PREC)


def make_fold(points, all_centers, running, portion):
    extent = portion.shape[1]
    step_cols = math.gcd(extent, 2048)

    def add_block(number, summed):
        first_col = number * step_cols
        part_coef = lax.dynamic_slice_in_dim(portion, first_col, step_cols, 1)
        part_cent = lax.dynamic_slice_in_dim(all_centers, first_col, step_cols, 1)
        weights = wendland(pair_distance(points, part_cent))
        return summed + row_product(part_coef, weights)

    return lax.fori_loop(0, extent // step_cols, add_block, running)


def shards(center_points, displacements, edge_points, send_list, block_tiles, block_count):
    shard_cols = center_points.shape[1]
    empty_motion = jnp.zeros((3, edge_points.shape[1]), jnp.float32)
    zone_centers, zone_shifts = (
        lax.all_gather(center_points, "gx", axis=1, tiled=True),
        lax.all_gather(displacements, "gx", axis=1, tiled=True),
    )
    all_centers = lax.all_gather(zone_centers, "gy", axis=1, tiled=True)
    kernel = wendland(pair_distance(zone_centers, all_centers))

    def matvec(search):
        full_search = lax.all_gather(search, "gy", axis=1, tiled=True)
        return row_product(full_search, kernel) + SHIFT * search

    def global_sum(partial_value):
        return lax.psum(partial_value, "gy")

    zone_coefs = conjugate(zone_shifts, matvec, global_sum)
    motion = make_fold(
        edge_points, all_centers, empty_motion, lax.all_gather(zone_coefs, "gy", axis=1, tiled=True)
    )
    coefficients = lax.dynamic_slice_in_dim(
        zone_coefs, lax.axis_index("gx") * shard_cols, shard_cols, 1
    )
    group_size = lax.axis_size("gy")
    capacity = send_list.shape[2]
    motion_tiles = motion.reshape(3, EDGE_DEV, S)
    wanted = send_list[0].reshape(group_size * capacity)
    picked = jnp.take(motion_tiles, jnp.maximum(wanted, 0), axis=1)
    picked = jnp.where((wanted >= 0)[None, :, None], picked, 0.0)
    arrived = lax.all_to_all(
        picked.reshape(3, group_size * capacity * S), "gy", split_axis=1, concat_axis=1, tiled=True
    )
    arrived = arrived.reshape(3, group_size * capacity, S)
    live_blocks = block_count[0]

    def fill_block(position, result):
        edge_tiles = jnp.take(arrived, block_tiles[position], axis=1)
        return lax.dynamic_update_index_in_dim(result, transfinite(edge_tiles), position, 0)

    block_motion = lax.fori_loop(
        0, live_blocks, fill_block, jnp.zeros((SLOTS, 3, S, S * S), jnp.float32)
    )
    return (coefficients, block_motion)


def solution(mesh):
    return jax.shard_map(
        shards,
        mesh=mesh,
        in_specs=(
            P(None, ("gx", "gy")),
            P(None, ("gx", "gy")),
            P(None, ("gx", "gy")),
            P(("gx", "gy"), None, None),
            P(("gx", "gy"), None),
            P(("gx", "gy")),
        ),
        out_specs=(P(None, ("gx", "gy")), P(("gx", "gy"), None, None, None)),
        check_vma=False,
    )
```

profile of v0, /device:TPU:17, one launch (start us, length us, event | category | flops | bytes accessed | tf_op | source)
XLA Modules:
  0.0 580.2 jit_solution(12650299831458198588)
XLA Ops:
  1.4 8.6 %all_gather.15 = f32[3,1024]{1,0:T(4,128)S(1)} all-gather(f32[3,256]{1,0:T(4,128)} %param.13), channel_id=1, replica_groups=mesh['gx'=4,'gy'=8] {'gx'}, dimensions={1}, use_global_device_ids=true | all-gather | bytes 15360 | tf_op jit(solution)/shard_map/all_gather | solution.py:94
  10.6 10.4 %all_gather.16 = f32[3,1024]{1,0:T(4,128)S(1)} all-gather(f32[3,256]{1,0:T(4,128)} %param.12), channel_id=1, replica_groups=mesh['gx'=4,'gy'=8] {'gx'}, dimensions={1}, use_global_device_ids=true | all-gather | bytes 15360 | tf_op jit(solution)/shard_map/all_gather | solution.py:93
  21.0 15.5 %all_gather.17 = f32[3,8192]{1,0:T(4,128)S(1)} all-gather(f32[3,1024]{1,0:T(4,128)S(1)} %all_gather.16), channel_id=1, replica_groups=mesh['gx'=4,'gy'=8] {'gy'}, dimensions={1}, use_global_device_ids=true | all-gather | bytes 110592 | tf_op jit(solution)/shard_map/all_gather | solution.py:96
  38.7 11.3 %psum.21 = f32[3,1]{0,1:T(1,128)S(1)} all-reduce(f32[3,1]{0,1:T(1,128)S(1)} %bitcast.135), channel_id=1, replica_groups=mesh['gx'=4,'gy'=8] {'gy'}, use_global_device_ids=true, to_apply=%region_1.0 | all-reduce | flops 3 | bytes 24 | tf_op jit(solution)/shard_map/psum | solution.py:104
  50.1 243.9 %while.44 = (s32[]{:T(128)}, f32[3,1024]{1,0:T(4,128)S(1)}, f32[3,1024]{1,0:T(4,128)}, f32[3,1024]{1,0:T(4,128)S(1)}, f32[3,1]{0,1:T(1,128)S(1)}, /*index=5*/f32...) while((s32[]{:T(128)}, f32[3,1024]{1,0:T(4,128)S(1)}, ...), condition=%wide.region_7.0_spmd.clone, body=%wide.region_2.0_spmd.clone.sunk | while | flops 436247552 | bytes 541067 | solution.py:65
  50.1 11.1 %all_gather.21 = f32[3,8192]{1,0:T(4,128)S(1)} all-gather(f32[3,1024]{1,0:T(4,128)S(1)} %get-tuple-element.524), channel_id=1, replica_groups=mesh['gx'=4,'gy'=8] {'gy'}, dimensions={1}, use_global_device_ids=true | all-gather | bytes 110592 | tf_op jit(solution)/shard_map/while/body/eval_jaxpr/all_gather | solution.py:100
  61.2 46.5 %multiply_reduce_fusion.5 = (f32[3]{0:T(128)S(1)}, f32[3,1024]{1,0:T(4,128)S(1)}) fusion(f32[3,1024]{1,0:T(4,128)S(1)} %get-tuple-element.524, f32[3,8192]{1,0:T(4,128)S(1)} %all_gather.21, f32[8192]{0:T(1024)S(1)} %get-tuple-element.543, f32[1024]{0:T(1024)S(1)} %get-tuple-element.544, f32[8192]{0:T(1024)S(1)} %get-tuple-element.541, ...), kind=kOutput, calls=%fused_computation.36.clone.1 | convolution fusion | flops 436219904 | bytes 233484 | tf_op jit(solution)/shard_map/while/body/eval_jaxpr/dot_general | solution.py:72
  107.7 11.3 %psum.26 = f32[3,1]{0,1:T(1,128)S(1)} all-reduce(f32[3,1]{0,1:T(1,128)S(1)} %bitcast.136), channel_id=1, replica_groups=mesh['gx'=4,'gy'=8] {'gy'}, use_global_device_ids=true, to_apply=%region_4.0 | all-reduce | flops 3 | bytes 24 | tf_op jit(solution)/shard_map/while/body/eval_jaxpr/psum | solution.py:104
  119.2 13.2 %psum.27 = f32[3,1]{0,1:T(1,128)S(1)} all-reduce(f32[3,1]{0,1:T(1,128)S(1)} %bitcast.131), channel_id=1, replica_groups=mesh['gx'=4,'gy'=8] {'gy'}, use_global_device_ids=true, to_apply=%region_6.0 | all-reduce | flops 3 | bytes 24 | tf_op jit(solution)/shard_map/while/body/eval_jaxpr/psum | solution.py:104
  132.6 8.7 %all_gather.21 = f32[3,8192]{1,0:T(4,128)S(1)} all-gather(f32[3,1024]{1,0:T(4,128)S(1)} %get-tuple-element.524), channel_id=1, replica_groups=mesh['gx'=4,'gy'=8] {'gy'}, dimensions={1}, use_global_device_ids=true | all-gather | bytes 110592 | tf_op jit(solution)/shard_map/while/body/eval_jaxpr/all_gather | solution.py:100
  141.3 46.5 %multiply_reduce_fusion.5 = (f32[3]{0:T(128)S(1)}, f32[3,1024]{1,0:T(4,128)S(1)}) fusion(f32[3,1024]{1,0:T(4,128)S(1)} %get-tuple-element.524, f32[3,8192]{1,0:T(4,128)S(1)} %all_gather.21, f32[8192]{0:T(1024)S(1)} %get-tuple-element.543, f32[1024]{0:T(1024)S(1)} %get-tuple-element.544, f32[8192]{0:T(1024)S(1)} %get-tuple-element.541, ...), kind=kOutput, calls=%fused_computation.36.clone.1 | convolution fusion | flops 436219904 | bytes 233484 | tf_op jit(solution)/shard_map/while/body/eval_jaxpr/dot_general | solution.py:72
  187.8 11.3 %psum.26 = f32[3,1]{0,1:T(1,128)S(1)} all-reduce(f32[3,1]{0,1:T(1,128)S(1)} %bitcast.136), channel_id=1, replica_groups=mesh['gx'=4,'gy'=8] {'gy'}, use_global_device_ids=true, to_apply=%region_4.0 | all-reduce | flops 3 | bytes 24 | tf_op jit(solution)/shard_map/while/body/eval_jaxpr/psum | solution.py:104
  199.3 13.2 %psum.27 = f32[3,1]{0,1:T(1,128)S(1)} all-reduce(f32[3,1]{0,1:T(1,128)S(1)} %bitcast.131), channel_id=1, replica_groups=mesh['gx'=4,'gy'=8] {'gy'}, use_global_device_ids=true, to_apply=%region_6.0 | all-reduce | flops 3 | bytes 24 | tf_op jit(solution)/shard_map/while/body/eval_jaxpr/psum | solution.py:104
  212.7 9.7 %all_gather.21 = f32[3,8192]{1,0:T(4,128)S(1)} all-gather(f32[3,1024]{1,0:T(4,128)S(1)} %get-tuple-element.524), channel_id=1, replica_groups=mesh['gx'=4,'gy'=8] {'gy'}, dimensions={1}, use_global_device_ids=true | all-gather | bytes 110592 | tf_op jit(solution)/shard_map/while/body/eval_jaxpr/all_gather | solution.py:100
  222.4 46.5 %multiply_reduce_fusion.5 = (f32[3]{0:T(128)S(1)}, f32[3,1024]{1,0:T(4,128)S(1)}) fusion(f32[3,1024]{1,0:T(4,128)S(1)} %get-tuple-element.524, f32[3,8192]{1,0:T(4,128)S(1)} %all_gather.21, f32[8192]{0:T(1024)S(1)} %get-tuple-element.543, f32[1024]{0:T(1024)S(1)} %get-tuple-element.544, f32[8192]{0:T(1024)S(1)} %get-tuple-element.541, ...), kind=kOutput, calls=%fused_computation.36.clone.1 | convolution fusion | flops 436219904 | bytes 233484 | tf_op jit(solution)/shard_map/while/body/eval_jaxpr/dot_general | solution.py:72
  268.9 11.3 %psum.26 = f32[3,1]{0,1:T(1,128)S(1)} all-reduce(f32[3,1]{0,1:T(1,128)S(1)} %bitcast.136), channel_id=1, replica_groups=mesh['gx'=4,'gy'=8] {'gy'}, use_global_device_ids=true, to_apply=%region_4.0 | all-reduce | flops 3 | bytes 24 | tf_op jit(solution)/shard_map/while/body/eval_jaxpr/psum | solution.py:104
  280.4 13.2 %psum.27 = f32[3,1]{0,1:T(1,128)S(1)} all-reduce(f32[3,1]{0,1:T(1,128)S(1)} %bitcast.131), channel_id=1, replica_groups=mesh['gx'=4,'gy'=8] {'gy'}, use_global_device_ids=true, to_apply=%region_6.0 | all-reduce | flops 3 | bytes 24 | tf_op jit(solution)/shard_map/while/body/eval_jaxpr/psum | solution.py:104
  294.0 8.7 %all_gather.18 = f32[3,8192]{1,0:T(4,128)S(1)} all-gather(f32[3,1024]{1,0:T(4,128)S(1)} %get-tuple-element.194), channel_id=1, replica_groups=mesh['gx'=4,'gy'=8] {'gy'}, dimensions={1}, use_global_device_ids=true | all-gather | bytes 110592 | tf_op jit(solution)/shard_map/all_gather | solution.py:108
  302.7 54.1 %while.45 = (s32[]{:T(128)}, f32[3,1024]{1,0:T(4,128)S(1)}, f32[3,8192]{1,0:T(4,128)S(1)}, f32[3,1024]{1,0:T(4,128)S(1)}, f32[3,8192]{1,0:T(4,128)}, /*index=5*/...) while((s32[]{:T(128)}, f32[3,1024]{1,0:T(4,128)S(1)}, ...), condition=%wide.region_9.0_spmd.clone, body=%wide.region_8.0_spmd.clone.sunk | while | flops 109058056 | bytes 172245 | solution.py:86
  303.7 12.5 %fusion.128 = f32[3,1024]{1,0:T(4,128)S(1)} fusion(f32[2048]{0:T(1024)S(1)} %bitcast.123, f32[1024]{0:T(1024)S(1)} %bitcast.126, f32[2048]{0:T(1024)S(1)} %bitcast.122, f32[1024]{0:T(1024)S(1)} %bitcast.127, f32[2048]{0:T(1024)S(1)} %bitcast.121, f32[1024]{0:T(1024)S(1)} %bitcast.125, f32[3,8192]{1,0:T(4,128)S(1)} %get-tuple-element.571, ...), kind=kOutput, calls=%fused_computation.71.clone.1 | convolution fusion | flops 109058048 | bytes 98309 | tf_op jit(solution)/shard_map/while/body/eval_jaxpr/dot_general | solution.py:72
  317.3 12.5 %fusion.128 = f32[3,1024]{1,0:T(4,128)S(1)} fusion(f32[2048]{0:T(1024)S(1)} %bitcast.123, f32[1024]{0:T(1024)S(1)} %bitcast.126, f32[2048]{0:T(1024)S(1)} %bitcast.122, f32[1024]{0:T(1024)S(1)} %bitcast.127, f32[2048]{0:T(1024)S(1)} %bitcast.121, f32[1024]{0:T(1024)S(1)} %bitcast.125, f32[3,8192]{1,0:T(4,128)S(1)} %get-tuple-element.571, ...), kind=kOutput, calls=%fused_computation.71.clone.1 | convolution fusion | flops 109058048 | bytes 98309 | tf_op jit(solution)/shard_map/while/body/eval_jaxpr/dot_general | solution.py:72
  330.8 12.5 %fusion.128 = f32[3,1024]{1,0:T(4,128)S(1)} fusion(f32[2048]{0:T(1024)S(1)} %bitcast.123, f32[1024]{0:T(1024)S(1)} %bitcast.126, f32[2048]{0:T(1024)S(1)} %bitcast.122, f32[1024]{0:T(1024)S(1)} %bitcast.127, f32[2048]{0:T(1024)S(1)} %bitcast.121, f32[1024]{0:T(1024)S(1)} %bitcast.125, f32[3,8192]{1,0:T(4,128)S(1)} %get-tuple-element.571, ...), kind=kOutput, calls=%fused_computation.71.clone.1 | convolution fusion | flops 109058048 | bytes 98309 | tf_op jit(solution)/shard_map/while/body/eval_jaxpr/dot_general | solution.py:72
  344.3 12.5 %fusion.128 = f32[3,1024]{1,0:T(4,128)S(1)} fusion(f32[2048]{0:T(1024)S(1)} %bitcast.123, f32[1024]{0:T(1024)S(1)} %bitcast.126, f32[2048]{0:T(1024)S(1)} %bitcast.122, f32[1024]{0:T(1024)S(1)} %bitcast.127, f32[2048]{0:T(1024)S(1)} %bitcast.121, f32[1024]{0:T(1024)S(1)} %bitcast.125, f32[3,8192]{1,0:T(4,128)S(1)} %get-tuple-element.571, ...), kind=kOutput, calls=%fused_computation.71.clone.1 | convolution fusion | flops 109058048 | bytes 98309 | tf_op jit(solution)/shard_map/while/body/eval_jaxpr/dot_general | solution.py:72
  366.1 6.3 %broadcast_in_dim.60 = f32[4,3,64,4096]{3,2,1,0:T(8,128)} broadcast(f32[]{:T(128)} %constant.153.clone.1), dimensions={} | broadcast | bytes 12582916 | tf_op jit(solution)/shard_map/broadcast_in_dim | solution.py:130
  372.5 206.7 %while.43 = (s32[]{:T(128)}, f32[4,3,64,4096]{3,2,1,0:T(8,128)}, s32[]{:T(128)}, s32[4,12]{1,0:T(4,128)S(1)}, f32[3,48,64]{2,0,1:T(4,128)S(1)}, /*index=5*/s32[]{:T(128)}, s32[]{:T(128)}, s32[]{:T(128)}) while((s32[]{:T(128)}, f32[4,3,64,4096]{3,2,1,0:T(8,128)}, s32[]{:T(128)}, s32[4,12]{1,0:T(4,128)S(1)}, f32[3,48,64]{2,0,1:T(4,128)S(1)}, ...), condition=%wide.region_11.12_spmd, body=%wide.region_10.11_spmd.sunk | while | flops 114876016 | bytes 41366100 | solution.py:129
  385.2 7.1 %fusion.122 = f32[3,64,64,64]{3,1,2,0:T(8,128)} fusion(f32[4,64,64]{2,0,1:T(4,128)S(1)} %copy.66, f32[3,12,64]{2,1,0:T(8,128)S(1)} %fusion.121, f32[3,4]{1,0:T(4,128)S(1)} %get-tuple-element.476, f32[64]{0:T(128)S(1)} %get-tuple-element.477, f32[3,4]{1,0:T(4,128)S(1)} %get-tuple-element.478, f32[64]{0:T(128)S(1)} %get-tuple-element.479), kind=kOutput, calls=%fused_computation.84.clone.1 | convolution fusion | flops 37752576 | bytes 3288064 | tf_op jit(solution)/shard_map/while/body/cei,ejk->cijk/dot_general | solution.py:44
  392.3 8.9 %fusion.123 = f32[64,64,3,64]{3,0,2,1:T(8,128)} fusion(f32[4,64]{0,1:T(8,128)S(1)} %copy.65, f32[4,64]{1,0:T(4,128)S(1)} %bitcast.118, f32[3,12,64]{2,1,0:T(8,128)S(1)} %fusion.121), kind=kOutput, calls=%fused_computation.81.clone.1 | convolution fusion | flops 37765120 | bytes 3186688 | tf_op jit(solution)/shard_map/while/body/cej,eik->cijk/dot_general | solution.py:47
  401.2 7.7 %copy.67 = f32[64,64,3,64]{1,0,3,2:T(8,128)} copy(f32[64,64,3,64]{3,0,2,1:T(8,128)} %fusion.123) | data formatting | bytes 6291456 | tf_op jit(solution)/shard_map/while/body/cej,eik->cijk/dot_general | solution.py:47
  408.9 10.4 %bitcast_add_fusion.3 = f32[3,64,64,64]{3,1,2,0:T(8,128)S(1)} fusion(f32[3,64,64,64]{3,1,2,0:T(8,128)} %fusion.122, f32[64,64,3,64]{1,0,3,2:T(8,128)} %copy.67, f32[4,64]{0,1:T(8,128)S(1)} %copy.65, f32[4,64]{1,0:T(4,128)S(1)} %bitcast.119, f32[3,12,64]{2,1,0:T(8,128)S(1)} %fusion.121), kind=kOutput, calls=%fused_computation.79.clone.1 | convolution fusion | flops 39337984 | bytes 9478144 | tf_op jit(solution)/shard_map/while/body/cek,eij->cijk/dot_general | solution.py:48
  419.4 6.3 %copy.68 = f32[3,64,64,64]{3,2,1,0:T(8,128)} copy(f32[3,64,64,64]{3,1,2,0:T(8,128)S(1)} %bitcast_add_fusion.3) | data formatting | bytes 6291456 | tf_op jit(solution)/shard_map/while/body/add | solution.py:48
  425.7 4.5 broadcast_in_dim.76
  433.9 7.1 %fusion.122 = f32[3,64,64,64]{3,1,2,0:T(8,128)} fusion(f32[4,64,64]{2,0,1:T(4,128)S(1)} %copy.66, f32[3,12,64]{2,1,0:T(8,128)S(1)} %fusion.121, f32[3,4]{1,0:T(4,128)S(1)} %get-tuple-element.476, f32[64]{0:T(128)S(1)} %get-tuple-element.477, f32[3,4]{1,0:T(4,128)S(1)} %get-tuple-element.478, f32[64]{0:T(128)S(1)} %get-tuple-element.479), kind=kOutput, calls=%fused_computation.84.clone.1 | convolution fusion | flops 37752576 | bytes 3288064 | tf_op jit(solution)/shard_map/while/body/cei,ejk->cijk/dot_general | solution.py:44
  441.1 8.9 %fusion.123 = f32[64,64,3,64]{3,0,2,1:T(8,128)} fusion(f32[4,64]{0,1:T(8,128)S(1)} %copy.65, f32[4,64]{1,0:T(4,128)S(1)} %bitcast.118, f32[3,12,64]{2,1,0:T(8,128)S(1)} %fusion.121), kind=kOutput, calls=%fused_computation.81.clone.1 | convolution fusion | flops 37765120 | bytes 3186688 | tf_op jit(solution)/shard_map/while/body/cej,eik->cijk/dot_general | solution.py:47
  450.0 7.7 %copy.67 = f32[64,64,3,64]{1,0,3,2:T(8,128)} copy(f32[64,64,3,64]{3,0,2,1:T(8,128)} %fusion.123) | data formatting | bytes 6291456 | tf_op jit(solution)/shard_map/while/body/cej,eik->cijk/dot_general | solution.py:47
  457.7 10.4 %bitcast_add_fusion.3 = f32[3,64,64,64]{3,1,2,0:T(8,128)S(1)} fusion(f32[3,64,64,64]{3,1,2,0:T(8,128)} %fusion.122, f32[64,64,3,64]{1,0,3,2:T(8,128)} %copy.67, f32[4,64]{0,1:T(8,128)S(1)} %copy.65, f32[4,64]{1,0:T(4,128)S(1)} %bitcast.119, f32[3,12,64]{2,1,0:T(8,128)S(1)} %fusion.121), kind=kOutput, calls=%fused_computation.79.clone.1 | convolution fusion | flops 39337984 | bytes 9478144 | tf_op jit(solution)/shard_map/while/body/cek,eij->cijk/dot_general | solution.py:48
  468.1 6.3 %copy.68 = f32[3,64,64,64]{3,2,1,0:T(8,128)} copy(f32[3,64,64,64]{3,1,2,0:T(8,128)S(1)} %bitcast_add_fusion.3) | data formatting | bytes 6291456 | tf_op jit(solution)/shard_map/while/body/add | solution.py:48
  474.4 4.5 broadcast_in_dim.76
  482.7 7.1 %fusion.122 = f32[3,64,64,64]{3,1,2,0:T(8,128)} fusion(f32[4,64,64]{2,0,1:T(4,128)S(1)} %copy.66, f32[3,12,64]{2,1,0:T(8,128)S(1)} %fusion.121, f32[3,4]{1,0:T(4,128)S(1)} %get-tuple-element.476, f32[64]{0:T(128)S(1)} %get-tuple-element.477, f32[3,4]{1,0:T(4,128)S(1)} %get-tuple-element.478, f32[64]{0:T(128)S(1)} %get-tuple-element.479), kind=kOutput, calls=%fused_computation.84.clone.1 | convolution fusion | flops 37752576 | bytes 3288064 | tf_op jit(solution)/shard_map/while/body/cei,ejk->cijk/dot_general | solution.py:44
  489.8 8.9 %fusion.123 = f32[64,64,3,64]{3,0,2,1:T(8,128)} fusion(f32[4,64]{0,1:T(8,128)S(1)} %copy.65, f32[4,64]{1,0:T(4,128)S(1)} %bitcast.118, f32[3,12,64]{2,1,0:T(8,128)S(1)} %fusion.121), kind=kOutput, calls=%fused_computation.81.clone.1 | convolution fusion | flops 37765120 | bytes 3186688 | tf_op jit(solution)/shard_map/while/body/cej,eik->cijk/dot_general | solution.py:47
  498.7 7.7 %copy.67 = f32[64,64,3,64]{1,0,3,2:T(8,128)} copy(f32[64,64,3,64]{3,0,2,1:T(8,128)} %fusion.123) | data formatting | bytes 6291456 | tf_op jit(solution)/shard_map/while/body/cej,eik->cijk/dot_general | solution.py:47
  506.5 10.4 %bitcast_add_fusion.3 = f32[3,64,64,64]{3,1,2,0:T(8,128)S(1)} fusion(f32[3,64,64,64]{3,1,2,0:T(8,128)} %fusion.122, f32[64,64,3,64]{1,0,3,2:T(8,128)} %copy.67, f32[4,64]{0,1:T(8,128)S(1)} %copy.65, f32[4,64]{1,0:T(4,128)S(1)} %bitcast.119, f32[3,12,64]{2,1,0:T(8,128)S(1)} %fusion.121), kind=kOutput, calls=%fused_computation.79.clone.1 | convolution fusion | flops 39337984 | bytes 9478144 | tf_op jit(solution)/shard_map/while/body/cek,eij->cijk/dot_general | solution.py:48
  516.9 6.3 %copy.68 = f32[3,64,64,64]{3,2,1,0:T(8,128)} copy(f32[3,64,64,64]{3,1,2,0:T(8,128)S(1)} %bitcast_add_fusion.3) | data formatting | bytes 6291456 | tf_op jit(solution)/shard_map/while/body/add | solution.py:48
  523.2 4.5 broadcast_in_dim.76
  531.5 7.1 %fusion.122 = f32[3,64,64,64]{3,1,2,0:T(8,128)} fusion(f32[4,64,64]{2,0,1:T(4,128)S(1)} %copy.66, f32[3,12,64]{2,1,0:T(8,128)S(1)} %fusion.121, f32[3,4]{1,0:T(4,128)S(1)} %get-tuple-element.476, f32[64]{0:T(128)S(1)} %get-tuple-element.477, f32[3,4]{1,0:T(4,128)S(1)} %get-tuple-element.478, f32[64]{0:T(128)S(1)} %get-tuple-element.479), kind=kOutput, calls=%fused_computation.84.clone.1 | convolution fusion | flops 37752576 | bytes 3288064 | tf_op jit(solution)/shard_map/while/body/cei,ejk->cijk/dot_general | solution.py:44
  538.6 8.9 %fusion.123 = f32[64,64,3,64]{3,0,2,1:T(8,128)} fusion(f32[4,64]{0,1:T(8,128)S(1)} %copy.65, f32[4,64]{1,0:T(4,128)S(1)} %bitcast.118, f32[3,12,64]{2,1,0:T(8,128)S(1)} %fusion.121), kind=kOutput, calls=%fused_computation.81.clone.1 | convolution fusion | flops 37765120 | bytes 3186688 | tf_op jit(solution)/shard_map/while/body/cej,eik->cijk/dot_general | solution.py:47
  547.5 7.7 %copy.67 = f32[64,64,3,64]{1,0,3,2:T(8,128)} copy(f32[64,64,3,64]{3,0,2,1:T(8,128)} %fusion.123) | data formatting | bytes 6291456 | tf_op jit(solution)/shard_map/while/body/cej,eik->cijk/dot_general | solution.py:47
  555.2 10.4 %bitcast_add_fusion.3 = f32[3,64,64,64]{3,1,2,0:T(8,128)S(1)} fusion(f32[3,64,64,64]{3,1,2,0:T(8,128)} %fusion.122, f32[64,64,3,64]{1,0,3,2:T(8,128)} %copy.67, f32[4,64]{0,1:T(8,128)S(1)} %copy.65, f32[4,64]{1,0:T(4,128)S(1)} %bitcast.119, f32[3,12,64]{2,1,0:T(8,128)S(1)} %fusion.121), kind=kOutput, calls=%fused_computation.79.clone.1 | convolution fusion | flops 39337984 | bytes 9478144 | tf_op jit(solution)/shard_map/while/body/cek,eij->cijk/dot_general | solution.py:48
  565.7 6.3 %copy.68 = f32[3,64,64,64]{3,2,1,0:T(8,128)} copy(f32[3,64,64,64]{3,1,2,0:T(8,128)S(1)} %bitcast_add_fusion.3) | data formatting | bytes 6291456 | tf_op jit(solution)/shard_map/while/body/add | solution.py:48
  (138 shorter events, 34.6 us)
Async XLA Ops:
  10.0 0.6 copy-start
  36.5 13.6 %copy-start.3 = (f32[3,8192]{1,0:T(4,128)}, f32[3,8192]{1,0:T(4,128)S(1)}, u32[]{:S(2)}) copy-start(f32[3,8192]{1,0:T(4,128)S(1)} %all_gather.17) | copy-start | bytes 294916
  50.1 252.6 %copy-start.4 = (f32[3,1024]{1,0:T(4,128)S(1)}, f32[3,1024]{1,0:T(4,128)}, u32[]{:S(2)}) copy-start(f32[3,1024]{1,0:T(4,128)} %param.14) | copy-start | bytes 36868
  50.1 252.6 %copy-start.5 = (f32[3,1024]{1,0:T(4,128)S(1)}, f32[3,1024]{1,0:T(4,128)}, u32[]{:S(2)}) copy-start(f32[3,1024]{1,0:T(4,128)} %custom-call.1) | copy-start | bytes 36868
  61.2 57.8 %copy-start.1 = (f32[3,1024]{1,0:T(4,128)S(1)}, f32[3,1024]{1,0:T(4,128)}, u32[]{:S(2)}) copy-start(f32[3,1024]{1,0:T(4,128)} %get-tuple-element.523) | copy-start | bytes 36868 | tf_op jit(solution)/shard_map/while
  119.2 13.3 %copy-start.2 = (f32[3,1024]{1,0:T(4,128)}, f32[3,1024]{1,0:T(4,128)S(1)}, u32[]{:S(2)}) copy-start(f32[3,1024]{1,0:T(4,128)S(1)} %get-tuple-element.536) | copy-start | bytes 36868 | tf_op jit(solution)/shard_map/while
  141.3 57.8 %copy-start.1 = (f32[3,1024]{1,0:T(4,128)S(1)}, f32[3,1024]{1,0:T(4,128)}, u32[]{:S(2)}) copy-start(f32[3,1024]{1,0:T(4,128)} %get-tuple-element.523) | copy-start | bytes 36868 | tf_op jit(solution)/shard_map/while
  199.3 13.3 %copy-start.2 = (f32[3,1024]{1,0:T(4,128)}, f32[3,1024]{1,0:T(4,128)S(1)}, u32[]{:S(2)}) copy-start(f32[3,1024]{1,0:T(4,128)S(1)} %get-tuple-element.536) | copy-start | bytes 36868 | tf_op jit(solution)/shard_map/while
  222.4 57.8 %copy-start.1 = (f32[3,1024]{1,0:T(4,128)S(1)}, f32[3,1024]{1,0:T(4,128)}, u32[]{:S(2)}) copy-start(f32[3,1024]{1,0:T(4,128)} %get-tuple-element.523) | copy-start | bytes 36868 | tf_op jit(solution)/shard_map/while
  280.4 13.3 %copy-start.2 = (f32[3,1024]{1,0:T(4,128)}, f32[3,1024]{1,0:T(4,128)S(1)}, u32[]{:S(2)}) copy-start(f32[3,1024]{1,0:T(4,128)S(1)} %get-tuple-element.536) | copy-start | bytes 36868 | tf_op jit(solution)/shard_map/while
  302.7 55.1 %copy-start.6 = (pred[8,384]{1,0:T(8,128)(4,1)S(1)}, pred[8,384]{1,0:T(8,128)(4,1)}, u32[]{:S(2)}) copy-start(pred[8,384]{1,0:T(8,128)(4,1)} %broadcast_in_dim.62) | copy-start | bytes 9220
  302.7 55.1 %copy-start.7 = (pred[8,384]{1,0:T(8,128)(4,1)S(1)}, pred[8,384]{1,0:T(8,128)(4,1)}, u32[]{:S(2)}) copy-start(pred[8,384]{1,0:T(8,128)(4,1)} %broadcast_in_dim.65) | copy-start | bytes 9220
  356.8 15.7 %copy-start.8 = (s32[4,12]{1,0:T(4,128)S(1)}, s32[4,12]{1,0:T(4,128)}, u32[]{:S(2)}) copy-start(s32[4,12]{1,0:T(4,128)} %param.16) | copy-start | bytes 580
  358.4 7.5 %all-to-all-start = ((f32[3,8,384]{2,0,1:T(4,128)}), f32[3,8,384]{2,0,1:T(4,128)S(1)}, u32[]{:S(2)}, u32[]{:S(2)}) async-start(f32[3,8,384]{2,0,1:T(4,128)} %copy.50), calls=%async_computation | async-start | bytes 98304 | tf_op jit(solution)/shard_map/all_to_all | solution.py:119
where the time goes:
time: 587 us; the launch traced here: 580 us
  matrix products  295 us (50%)
  blocking collectives  158 us (27%)
  local copies, waits for them, and re-layouts  101 us (17%)
  loops' own time  15.2 us (3%)
    dot_general x7, matrix products, row_product(): lax.dot_general(full_search, kernel, (((1,), (1,)), ((), ())), precision=...  190 us
    psum x7, blocking collectives, global_sum(): return lax.psum(partial_value, 'gy')  84.8 us
    dot_general x4, matrix products, transfinite(): jnp.einsum('cek,eij->cijk', third_dir, pair_weight, precision=HIGHEST_PREC)  41.7 us
    dot_general x4, matrix products, transfinite(): jnp.einsum('cej,eik->cijk', second_dir, pair_weight, precision=HIGHEST_PREC)  35.7 us
    dot_general x4, local copies, waits for them, and re-layouts, transfinite(): jnp.einsum('cej,eik->cijk', second_dir, pair_weight, precision=HIGHEST_PREC)  30.9 us
    all_gather x3, blocking collectives, matvec(): full_search = lax.all_gather(search, 'gy', axis=1, tiled=True)  29.5 us
    dot_general x4, matrix products, transfinite(): jnp.einsum('cei,ejk->cijk', first_dir - 2.0 * straight, pair_weight, prec...  28.4 us
    add x4, local copies, waits for them, and re-layouts, transfinite(): result + jnp.einsum('cek,eij->cijk', third_dir, pair_weight, precision=HI...  25.2 us
  transfers between devices with their start and end apart: 1, of which 1 were waited for; matrix products, arithmetic and copies ran while one was open for 0% of the time, Pallas kernels for 0%

commit v1 on v0

v1 whole, which is shorter than its diff:
```python
import functools

import jax
import jax.numpy as jnp
from jax import lax
from jax.experimental import pallas as pl
from jax.experimental.pallas import tpu as pltpu
from jax.sharding import PartitionSpec as P

S = 64
SHIFT = 0.1
INV_RADIUS = 4.0
TINY = 1e-12
BOTH = ("gx", "gy")
F32, BF16 = jnp.float32, jnp.bfloat16
VMEM = pl.BlockSpec(memory_space=pltpu.VMEM)
SMEM = pl.BlockSpec(memory_space=pltpu.SMEM)
PLAIN = (((1,), (0,)), ((), ()))
LEFT_T = (((0,), (0,)), ((), ()))


def dot(left, right, dims=PLAIN):
    return lax.dot_general(left, right, dims, preferred_element_type=F32)


def split2(value):
    high = value.astype(BF16)
    return high, (value - high.astype(F32)).astype(BF16)


def split3(value):
    high = value.astype(BF16).astype(F32)
    rest = value - high
    middle = rest.astype(BF16).astype(F32)
    return high, middle, rest - middle


def features(points, is_left):
    row = lax.broadcasted_iota(jnp.int32, points.shape, 0)
    is_point = (row >= 4) & (row < 7)
    scaled = jnp.where(is_point, (points - 0.5) * INV_RADIUS, 0.0)
    norm = jnp.sum(scaled * scaled, axis=0, keepdims=True)
    own_row, other_row = (0, 1) if is_left else (1, 0)
    if is_left:
        scaled = -2.0 * scaled
    high, middle, low = split3(scaled)

    def with_norm(part, norm_part):
        return jnp.where(row == own_row, norm_part, jnp.where(row == other_row, 1.0, part))

    norms = split3(norm)
    if is_left:
        parts = [with_norm(high, n) for n in norms] + [middle, middle, low]
    else:
        parts = [with_norm(p, n) for p, n in zip((high, middle, low), norms)] + [high, middle, high]
    return jnp.concatenate(parts, axis=0).astype(BF16)


def quarter_phi(squared):
    squared = jnp.maximum(squared, TINY)
    radial = squared * lax.rsqrt(squared)
    remain = jnp.maximum(1.0 - radial, 0.0)
    remain2 = remain * remain
    return (remain2 * remain2) * (radial + 0.25)


def stack_split(vector):
    high, low = split2(vector)
    return jnp.concatenate([high, low], axis=0), high


def split_product(stacked, high, weights_high, weights_low):
    both = dot(stacked, weights_high)
    rows = high.shape[0]
    return both[:rows] + both[rows:] + dot(high, weights_low)


def pack_kernel(centers, shifts, out):
    out[...] = jnp.zeros_like(out)
    out[:, 0:3, :] = jnp.broadcast_to(shifts[...][None], (out.shape[0],) + shifts.shape)
    out[:, 4:7, :] = jnp.broadcast_to(centers[...][None], (out.shape[0],) + centers.shape)


def lead_rows(value, count):
    row = lax.broadcasted_iota(jnp.int32, value.shape, value.ndim - 2)
    return jnp.where(row < count, value, 0.0)


def build_kernel(me, every, high_ref, low_ref, applied_out, left_ref):
    parts = every.shape[0]
    mine = every[me[0]]
    left_ref[...] = features(mine, True)

    def block(number, total):
        there = every[number]
        right = features(there, False)
        weights = quarter_phi(dot(right, left_ref[...], LEFT_T))
        weights_high, weights_low = split2(weights)
        high_ref[number] = weights_high
        low_ref[number] = weights_low
        stacked, high = stack_split(4.0 * lead_rows(there, 3))
        return total + split_product(stacked, high, weights_high, weights_low)

    total = lax.fori_loop(0, parts, block, jnp.zeros(mine.shape, F32))
    applied = total + SHIFT * lead_rows(mine, 3)
    applied_out[...] = jnp.broadcast_to(applied[0:4][None], applied_out.shape)


def matvec(vector_ref, high_ref, low_ref):
    parts, rows, width = vector_ref.shape

    def block(number, total):
        stacked, high = stack_split(4.0 * vector_ref[number])
        return total + split_product(stacked, high, high_ref[number], low_ref[number])

    return lax.fori_loop(0, parts, block, jnp.zeros((rows, width), F32))


def whole_sum(value):
    return jnp.sum(jnp.sum(value, axis=0), axis=1, keepdims=True)


def ratio(top, bottom):
    row = lax.broadcasted_iota(jnp.int32, top.shape, 0)
    return jnp.where(row < 3, top / jnp.where(row < 3, bottom, 1.0), 0.0)


def turn_one_kernel(me, every, applied, high_ref, low_ref, applied_out, search_out, remain_out, numbers_out):
    start = lead_rows(every[:, 0:4, :], 3)
    got = applied[...]
    norm = whole_sum(start * start)
    step = ratio(norm, whole_sum(start * got))
    remain = start - step[None] * got
    following = whole_sum(remain * remain)
    search = remain + ratio(following, norm)[None] * start
    search_out[:, 0:4, :] = search
    search_out[:, 4:8, :] = jnp.zeros_like(search)
    remain_out[...] = remain
    numbers_out[0] = jnp.broadcast_to(step, numbers_out.shape[1:])
    numbers_out[1] = jnp.broadcast_to(following, numbers_out.shape[1:])
    product = matvec(search_out, high_ref, low_ref)
    product = product[0:4] + SHIFT * search_out[me[0]][0:4]
    applied_out[...] = jnp.broadcast_to(product[None], applied_out.shape)


def turn_two_kernel(me, every, applied, search_in, remain_in, numbers, high_ref, low_ref, partial_out, pair_out, norm_out):
    start = lead_rows(every[:, 0:4, :], 3)
    got = applied[...]
    search = search_in[:, 0:4, :]
    norm = numbers[1][:, 0:1]
    step = ratio(norm, whole_sum(search * got))
    iterate = numbers[0][:, 0:1][None] * start + step[None] * search
    remain = remain_in[...] - step[None] * got
    following = whole_sum(remain * remain)
    search = remain + ratio(following, norm)[None] * search
    pair_out[:, 0:4, :] = search
    pair_out[:, 4:8, :] = iterate
    norm_out[...] = jnp.broadcast_to(following, norm_out.shape)
    product = matvec(pair_out, high_ref, low_ref)
    mine = pair_out[me[0]][0:4]
    product = product[0:4] + SHIFT * mine
    partial = jnp.sum(mine * product, axis=1, keepdims=True)
    partial_out[...] = jnp.broadcast_to(partial[None], partial_out.shape)


def edge_kernel(every, points, pair, out, left_ref):
    parts = every.shape[0]
    width = out.shape[1]
    piece = min(width, 256)
    left_ref[...] = features(points[...], True)
    out[...] = jnp.zeros_like(out)

    def block(number, carry):
        right = features(every[number], False).T
        stacked, high = stack_split(4.0 * pair[number])
        for first in range(0, width, piece):
            cols = slice(first, first + piece)
            weights = quarter_phi(dot(right, left_ref[:, cols]))
            out[:, cols] += split_product(stacked, high, *split2(weights))
        return carry

    lax.fori_loop(0, parts, block, 0)


def pick_kernel(me, send_list, partials, norm, pair, motions, coefficients_out, tiles_out, edge_ref):
    total = jnp.sum(partials[...], axis=0)[:, 0:1]
    step = ratio(norm[:, 0:1], total)
    mine = pair[me[0]]
    coefficients_out[...] = (mine[4:8] + step * mine[0:4])[0:3]
    motion = motions[4:8, :] + step * motions[0:4, :]
    for edge in range(edge_ref.shape[0]):
        edge_ref[edge] = motion[:, edge * S : (edge + 1) * S]
    for place in range(tiles_out.shape[0]):
        for position in range(tiles_out.shape[1]):
            tiles_out[place, position] = edge_ref[jnp.maximum(send_list[place, position], 0)]


def blend(index):
    fraction = index.astype(F32) / (S - 1)
    return 1.0 - fraction, fraction


def six_products(left, right):
    lh, lm, ll = split3(left)
    rh, rm, rl = split3(right)
    lefts = jnp.concatenate([lh, lh, lm, lh, ll, lm], axis=0).astype(BF16)
    rights = jnp.concatenate([rh, rm, rh, rl, rh, rm], axis=0).astype(BF16)
    return dot(lefts, rights, LEFT_T)


def block_kernel(block_tiles, count, tiles, out, tile_ref, spread_ref, weight_ref):
    slot = pl.program_id(0)
    cells = S * S

    @pl.when(slot == 0)
    def _():
        index = lax.broadcasted_iota(jnp.int32, (2 * S, cells), 0)
        cell = lax.broadcasted_iota(jnp.int32, (2 * S, cells), 1)
        wanted = jnp.where(index < S, cell // S, cell % S + S)
        spread_ref[...] = jnp.where(index == wanted, 1.0, 0.0).astype(BF16)
        row = lax.broadcasted_iota(jnp.int32, (8, cells), 0)
        cell = lax.broadcasted_iota(jnp.int32, (8, cells), 1)
        j_low, j_high = blend(cell // S)
        k_low, k_high = blend(cell % S)
        j_weight = jnp.where(row % 2 == 0, j_low, j_high)
        k_weight = jnp.where(row // 2 == 0, k_low, k_high)
        weight_ref[0] = jnp.where(row < 4, j_weight * k_weight, 0.0)
        side = row % 4 // 2 == 0
        weight_ref[1] = jnp.where(row < 4, jnp.where(side, k_low, k_high), jnp.where(side, j_low, j_high))

    @pl.when(slot < count[0])
    def _():
        for edge in range(12):
            tile = tiles[block_tiles[slot, edge]]
            for coordinate in range(3):
                tile_ref[coordinate, edge : edge + 1, :] = tile[coordinate : coordinate + 1, :]
        along_low, along_high = blend(lax.broadcasted_iota(jnp.int32, (8, S), 1))
        row = lax.broadcasted_iota(jnp.int32, (8, S), 0)
        side = jnp.where(row % 2 == 0, along_low, along_high)
        for coordinate in range(3):
            first = tile_ref[coordinate, 0:8, :]
            straight = along_low * first[:, 0:1] + along_high * first[:, S - 1 : S]
            bent = jnp.where(row < 4, first - 2.0 * straight, 0.0)
            others = tile_ref[coordinate, 4:12, :]
            zero = jnp.zeros_like(others)
            placed = jnp.concatenate(
                [jnp.where(row < 4, others, zero), jnp.where(row < 4, zero, others)], axis=1
            )
            spread = dot(jnp.concatenate(split3(placed), axis=0).astype(BF16), spread_ref[...])
            spread = (spread[0:8] + spread[8:16]) + spread[16:24]
            lefts = jnp.concatenate([bent, side], axis=0)
            rights = jnp.concatenate([weight_ref[0], spread * weight_ref[1]], axis=0)
            out[0, coordinate] = six_products(lefts, rights)

    @pl.when(slot >= count[0])
    def _():
        out[...] = jnp.zeros_like(out)


def call(kernel, name, outs, specs, scratch=(), **more):
    shapes = tuple(jax.ShapeDtypeStruct(shape, dtype) for shape, dtype in outs)
    return pl.pallas_call(
        kernel,
        out_shape=shapes,
        in_specs=specs,
        out_specs=tuple(VMEM for _ in shapes),
        scratch_shapes=scratch,
        compiler_params=pltpu.CompilerParams(vmem_limit_bytes=48 << 20),
        name=name,
        **more,
    )


def shards(total, center_points, displacements, edge_points, send_list, block_tiles, block_count):
    width = center_points.shape[1]
    edge_width = edge_points.shape[1]
    group = send_list.shape[1]
    capacity = send_list.shape[2]
    slots = block_tiles.shape[0]
    me = (lax.axis_index("gx") * lax.axis_size("gy") + lax.axis_index("gy")).reshape(1)

    def spread_out(copies, axes):
        return lax.all_to_all(copies, axes, split_axis=0, concat_axis=0, tiled=True)

    (packed,) = call(pack_kernel, "pack", [((total, 8, width), F32)], [VMEM] * 2)(center_points, displacements)
    every = spread_out(packed, BOTH)
    matrix = ((total, width, width), BF16)
    thin = ((total, 4, width), F32)
    wide = ((total, 8, width), F32)
    high, low, applied = call(
        build_kernel, "build", [matrix, matrix, thin], [SMEM, VMEM], [pltpu.VMEM((48, width), BF16)]
    )(me, every)
    applied = spread_out(applied, BOTH)
    applied, search, remain, numbers = call(
        turn_one_kernel, "turn_one", [thin, wide, thin, ((2, 4, 128), F32)], [SMEM] + [VMEM] * 4
    )(me, every, applied, high, low)
    applied = spread_out(applied, BOTH)
    partials, pair, norm = call(
        turn_two_kernel, "turn_two", [((total, 4, 128), F32), wide, ((4, 128), F32)], [SMEM] + [VMEM] * 7
    )(me, every, applied, search, remain, numbers, high, low)
    partials = spread_out(partials, BOTH)
    points = jnp.concatenate([jnp.zeros((4, edge_width), F32), edge_points, jnp.zeros((1, edge_width), F32)])
    (motions,) = call(
        edge_kernel, "edges", [((8, edge_width), F32)], [VMEM] * 3, [pltpu.VMEM((48, edge_width), BF16)]
    )(every, points, pair)
    coefficients, tiles = call(
        pick_kernel,
        "pick",
        [((3, width), F32), ((group, capacity, 4, S), F32)],
        [SMEM] * 2 + [VMEM] * 4,
        [pltpu.VMEM((edge_width // S, 4, S), F32)],
    )(me, send_list[0], partials, norm, pair, motions)
    tiles = spread_out(tiles, "gy").reshape(group * capacity, 4, S)
    block_motion = pl.pallas_call(
        block_kernel,
        out_shape=jax.ShapeDtypeStruct((slots, 3, S, S * S), F32),
        grid=(slots,),
        in_specs=[SMEM, SMEM, VMEM],
        out_specs=pl.BlockSpec((1, 3, S, S * S), lambda slot: (slot, 0, 0, 0)),
        scratch_shapes=[
            pltpu.VMEM((3, 12, S), F32),
            pltpu.VMEM((2 * S, S * S), BF16),
            pltpu.VMEM((2, 8, S * S), F32),
        ],
        compiler_params=pltpu.CompilerParams(vmem_limit_bytes=48 << 20),
        name="blocks",
    )(block_tiles, block_count, tiles)
    return coefficients, block_motion


def solution(mesh):
    total = mesh.shape["gx"] * mesh.shape["gy"]
    split = P(None, BOTH)
    return jax.shard_map(
        functools.partial(shards, total),
        mesh=mesh,
        in_specs=(split, split, split, P(BOTH, None, None), P(BOTH, None), P(BOTH)),
        out_specs=(split, P(BOTH, None, None, None)),
        check_vma=False,
    )
```

time: 587 us -> 125 us (0.21)
  the two profiles are of different devices: /device:TPU:17 before, /device:TPU:0 now
where the time goes in v1:
time: 125 us; the launch traced here: 124 us
  Pallas kernels  67.4 us (54%)
  waiting for transfers between devices  22.9 us (18%)
  starting transfers between devices  16.3 us (13%)
  blocking collectives  10.4 us (8%)
  local copies, waits for them, and re-layouts  5.09 us (4%)
  between operations  1.36 us (1%)
    pallas_call x1, Pallas kernels, shards(): call(edge_kernel, 'edges', [((8, edge_width), F32)], [VMEM] * 3, [pltpu.V...  24.8 us
    all_to_all x4, waiting for transfers between devices, spread_out(): return lax.all_to_all(copies, axes, split_axis=0, concat_axis=0, tiled=True)  22.9 us
    all_to_all x4, starting transfers between devices, spread_out(): return lax.all_to_all(copies, axes, split_axis=0, concat_axis=0, tiled=True)  16.3 us
    pallas_call x1, Pallas kernels, shards(): call(build_kernel, 'build', [matrix, matrix, thin], [SMEM, VMEM], [pltpu....  16.1 us
    all_to_all x1, blocking collectives, spread_out(): return lax.all_to_all(copies, axes, split_axis=0, concat_axis=0, tiled=True)  10.4 us
    pallas_call x1, Pallas kernels, shards(): call(turn_two_kernel, 'turn_two', [((total, 4, 128), F32), wide, ((4, 128...  8.58 us
    pallas_call x1, Pallas kernels, shards(): call(turn_one_kernel, 'turn_one', [thin, wide, thin, ((2, 4, 128), F32)],...  8.4 us
    pallas_call x1, Pallas kernels, shards(): pl.pallas_call(block_kernel, out_shape=jax.ShapeDtypeStruct((slots, 3, S,...  7.41 us
  transfers between devices with their start and end apart: 4, of which 3 were waited for; matrix products, arithmetic and copies ran while one was open for 0% of the time, Pallas kernels for 20%

profile of v1, /device:TPU:0, one launch (start us, length us, event | category | flops | bytes accessed | tf_op | source)
XLA Modules:
  0.0 124.3 jit_solution(10874512913596311798)
XLA Ops:
  0.6 0.0 copy-start.2
  0.6 0.7 copy-done.2
  1.3 0.0 copy-start.3
  1.3 0.7 copy-done.3
  2.0 0.8 pack.1
  2.8 7.3 %all-to-all-start = ((f32[32,8,256]{2,1,0:T(8,128)}), f32[32,8,256]{2,1,0:T(8,128)S(1)}, u32[]{:S(2)}, u32[]{:S(2)}) async-start(f32[32,8,256]{2,1,0:T(8,128)} %pack.1), calls=%async_computation | async-start | bytes 524288 | tf_op jit(solution)/shard_map/all_to_all | solution.py:283
  10.1 10.6 %all-to-all-done.every = f32[32,8,256]{2,1,0:T(8,128)S(1)} async-done(((f32[32,8,256]{2,1,0:T(8,128)}), f32[32,8,256]{2,1,0:T(8,128)S(1)}, u32[]{:S(2)}, u32[]{:S(2)}) %all-to-all-start) | async-done | bytes 262176 | tf_op jit(solution)/shard_map/all_to_all | solution.py:283
  20.7 16.1 %build.1 = (bf16[32,256,256]{2,1,0:T(8,128)(2,1)S(1)}, bf16[32,256,256]{2,1,0:T(8,128)(2,1)}, f32[32,4,256]{2,1,0:T(4,128)S(1)}) custom-call(s32[1]{0:T(128)} %bitcast.me, f32[32,8,256]{2,1,0:T(8,128)S(1)} %all-to-all-done.every), custom_call_target="tpu_custom_call" | custom-call | tf_op jit(solution)/shard_map/build/pallas_call | solution.py:290
  36.8 0.0 copy-start
  36.8 10.4 %all_to_all.25.applied = f32[32,4,256]{2,1,0:T(4,128)S(1)} all-to-all(f32[32,4,256]{2,1,0:T(4,128)S(1)} %get-tuple-element.14), channel_id=1, replica_groups=mesh['gx'=4,'gy'=8] {'gx','gy'}, dimensions={0} | all-to-all | bytes 262144 | tf_op jit(solution)/shard_map/all_to_all | solution.py:283
  47.2 0.0 copy-start.6
  47.2 8.4 %turn_one.1 = (f32[32,4,256]{2,1,0:T(4,128)}, f32[32,8,256]{2,1,0:T(8,128)S(1)}, f32[32,4,256]{2,1,0:T(4,128)S(1)}, f32[2,4,128]{2,1,0:T(4,128)S(1)}) custom-call(s32[1]{0:T(128)} %bitcast.me, f32[32,8,256]{2,1,0:T(8,128)S(1)} %all-to-all-done.every, f32[32,4,256]{2,1,0:T(4,128)S(1)} %all_to_all.25.applied, ...), custom_call_target="tpu_custom_call" | custom-call | tf_op jit(solution)/shard_map/turn_one/pallas_call | solution.py:294
  55.6 0.0 copy-done
  55.6 2.6 %all-to-all-start.2 = ((f32[32,4,256]{2,1,0:T(4,128)}), f32[32,4,256]{2,1,0:T(4,128)S(1)}, u32[]{:S(2)}, u32[]{:S(2)}) async-start(f32[32,4,256]{2,1,0:T(4,128)} %get-tuple-element.17), calls=%async_computation.2 | async-start | bytes 262144 | tf_op jit(solution)/shard_map/all_to_all | solution.py:283
  58.2 0.1 pad.2.clone
  58.3 0.0 copy-done.6
  58.3 0.1 copy.8
  58.4 8.1 %all-to-all-done.2.applied = f32[32,4,256]{2,1,0:T(4,128)S(1)} async-done(((f32[32,4,256]{2,1,0:T(4,128)}), f32[32,4,256]{2,1,0:T(4,128)S(1)}, u32[]{:S(2)}, u32[]{:S(2)}) %all-to-all-start.2) | async-done | bytes 131104 | tf_op jit(solution)/shard_map/all_to_all | solution.py:283
  66.4 0.0 copy-start.1
  66.4 2.2 %copy-done.1 = bf16[32,256,256]{2,1,0:T(8,128)(2,1)S(1)} copy-done((bf16[32,256,256]{2,1,0:T(8,128)(2,1)S(1)}, bf16[32,256,256]{2,1,0:T(8,128)(2,1)}, u32[]{:S(2)}) %copy-start.1) | copy-done | bytes 4194328
  68.6 0.0 copy-start.5
  68.6 0.0 copy-start.4
  68.6 8.6 %turn_two.1 = (f32[32,4,128]{2,1,0:T(4,128)}, f32[32,8,256]{2,1,0:T(8,128)S(1)}, f32[4,128]{1,0:T(4,128)S(1)}) custom-call(s32[1]{0:T(128)} %bitcast.me, f32[32,8,256]{2,1,0:T(8,128)S(1)} %all-to-all-done.every, f32[32,4,256]{2,1,0:T(4,128)S(1)} %all-to-all-done.2.applied, f32[32,8,256]{2,1,0:T(8,128)S(1)} %get-tuple-element.18.search_in, ...), custom_call_target="tpu_custom_call" | custom-call | tf_op jit(solution)/shard_map/turn_two/pallas_call | solution.py:298
  77.2 2.6 %all-to-all-start.3 = ((f32[32,4,128]{2,1,0:T(4,128)}), f32[32,4,128]{2,1,0:T(4,128)S(1)}, u32[]{:S(2)}, u32[]{:S(2)}) async-start(f32[32,4,128]{2,1,0:T(4,128)} %get-tuple-element.21), calls=%async_computation.3 | async-start | bytes 131072 | tf_op jit(solution)/shard_map/all_to_all | solution.py:283
  79.8 0.0 copy-done.5
  79.8 0.1 maximum_maximum_fusion.points
  79.9 24.8 %edges.1.motions = f32[8,1024]{1,0:T(8,128)S(1)} custom-call(f32[32,8,256]{2,1,0:T(8,128)S(1)} %all-to-all-done.every, f32[8,1024]{1,0:T(8,128)S(1)} %maximum_maximum_fusion.points, f32[32,8,256]{2,1,0:T(8,128)S(1)} %get-tuple-element.23.pair), custom_call_target="tpu_custom_call" | custom-call | tf_op jit(solution)/shard_map/edges/pallas_call | solution.py:303
  104.7 0.0 all-to-all-done.3.partials
  104.7 1.3 %pick.1 = (f32[3,256]{1,0:T(4,128)}, f32[8,6,4,64]{3,2,1,0:T(4,128)S(1)}) custom-call(s32[1]{0:T(128)} %bitcast.me, s32[8,6]{1,0:T(8,128)S(1)} %bitcast.5, f32[32,4,128]{2,1,0:T(4,128)S(1)} %all-to-all-done.3.partials, f32[4,128]{1,0:T(4,128)S(1)} %get-tuple-element.22.norm, f32[32,8,256]{2,1,0:T(8,128)S(1)} %get-tuple-element.23.pair, ...), custom_call_target="tpu_custom_call" | custom-call | tf_op jit(solution)/shard_map/pick/pallas_call | solution.py:306
  106.0 0.7 reshape.13
  106.8 3.8 %all-to-all-start.4 = ((f32[8,1,1536]{2,1,0:T(1,128)}), f32[8,1,1536]{2,1,0:T(1,128)S(1)}, u32[]{:S(2)}, u32[]{:S(2)}) async-start(f32[8,1,1536]{2,1,0:T(1,128)} %reshape.13), calls=%async_computation.4 | async-start | bytes 98304 | tf_op jit(solution)/shard_map/all_to_all | solution.py:283
  111.3 4.3 %all-to-all-done.4 = f32[8,1,1536]{2,1,0:T(1,128)S(1)} async-done(((f32[8,1,1536]{2,1,0:T(1,128)}), f32[8,1,1536]{2,1,0:T(1,128)S(1)}, u32[]{:S(2)}, u32[]{:S(2)}) %all-to-all-start.4) | async-done | bytes 49184 | tf_op jit(solution)/shard_map/all_to_all | solution.py:283
  115.5 0.5 broadcast.4
  116.0 0.8 reduce
  116.8 0.1 reshape.14
  116.9 0.0 copy-done.4
  116.9 7.4 %blocks.1 = f32[4,3,64,4096]{3,2,1,0:T(8,128)} custom-call(s32[4,12]{1,0:T(4,128)S(1)} %copy-done.4, s32[1]{0:T(128)S(6)} %copy.9.count, f32[48,4,64]{2,1,0:T(4,128)S(1)} %bitcast.4), custom_call_target="tpu_custom_call" | custom-call | tf_op jit(solution)/shard_map/blocks/pallas_call | solution.py:314
  (2 shorter events, 0.0 us)
Async XLA Ops:
  0.6 0.7 copy-start.2
  1.3 0.7 copy-start.3
  2.8 17.9 %all-to-all-start = ((f32[32,8,256]{2,1,0:T(8,128)}), f32[32,8,256]{2,1,0:T(8,128)S(1)}, u32[]{:S(2)}, u32[]{:S(2)}) async-start(f32[32,8,256]{2,1,0:T(8,128)} %pack.1), calls=%async_computation | async-start | bytes 524288 | tf_op jit(solution)/shard_map/all_to_all | solution.py:283
  36.8 18.8 %copy-start = (bf16[32,256,256]{2,1,0:T(8,128)(2,1)}, bf16[32,256,256]{2,1,0:T(8,128)(2,1)S(1)}, u32[]{:S(2)}) copy-start(bf16[32,256,256]{2,1,0:T(8,128)(2,1)S(1)} %get-tuple-element.15.high_ref) | copy-start | bytes 12582916
  47.2 11.1 %copy-start.6 = (s32[1,8,6]{1,0,2:T(1,128)S(1)}, s32[1,8,6]{1,0,2:T(1,128)}, u32[]{:S(2)}) copy-start(s32[1,8,6]{1,0,2:T(1,128)} %param.9) | copy-start | bytes 580
  55.6 10.8 %all-to-all-start.2 = ((f32[32,4,256]{2,1,0:T(4,128)}), f32[32,4,256]{2,1,0:T(4,128)S(1)}, u32[]{:S(2)}, u32[]{:S(2)}) async-start(f32[32,4,256]{2,1,0:T(4,128)} %get-tuple-element.17), calls=%async_computation.2 | async-start | bytes 262144 | tf_op jit(solution)/shard_map/all_to_all | solution.py:283
  66.4 2.2 %copy-start.1 = (bf16[32,256,256]{2,1,0:T(8,128)(2,1)S(1)}, bf16[32,256,256]{2,1,0:T(8,128)(2,1)}, u32[]{:S(2)}) copy-start(bf16[32,256,256]{2,1,0:T(8,128)(2,1)} %copy-done) | copy-start | bytes 12582916
  68.6 11.2 %copy-start.5 = (f32[3,1024]{1,0:T(4,128)S(1)}, f32[3,1024]{1,0:T(4,128)}, u32[]{:S(2)}) copy-start(f32[3,1024]{1,0:T(4,128)} %param.8) | copy-start | bytes 36868
  68.6 48.3 %copy-start.4 = (s32[4,12]{1,0:T(4,128)S(1)}, s32[4,12]{1,0:T(4,128)}, u32[]{:S(2)}) copy-start(s32[4,12]{1,0:T(4,128)} %block_tiles.1) | copy-start | bytes 580
  77.2 27.5 %all-to-all-start.3 = ((f32[32,4,128]{2,1,0:T(4,128)}), f32[32,4,128]{2,1,0:T(4,128)S(1)}, u32[]{:S(2)}, u32[]{:S(2)}) async-start(f32[32,4,128]{2,1,0:T(4,128)} %get-tuple-element.21), calls=%async_computation.3 | async-start | bytes 131072 | tf_op jit(solution)/shard_map/all_to_all | solution.py:283
  106.8 8.8 %all-to-all-start.4 = ((f32[8,1,1536]{2,1,0:T(1,128)}), f32[8,1,1536]{2,1,0:T(1,128)S(1)}, u32[]{:S(2)}, u32[]{:S(2)}) async-start(f32[8,1,1536]{2,1,0:T(1,128)} %reshape.13), calls=%async_computation.4 | async-start | bytes 98304 | tf_op jit(solution)/shard_map/all_to_all | solution.py:283

commit v2 on v1

v2 whole, which is shorter than its diff:
```python
import functools
import math

import jax
import jax.numpy as jnp
from jax import lax
from jax.experimental import pallas as pl
from jax.experimental.pallas import tpu as pltpu
from jax.sharding import PartitionSpec as P

S = 64
SHIFT = 0.1
INV_RADIUS = 4.0
TINY = 1e-12
BOTH = ("gx", "gy")
F32, BF16 = jnp.float32, jnp.bfloat16
VMEM = pl.BlockSpec(memory_space=pltpu.VMEM)
SMEM = pl.BlockSpec(memory_space=pltpu.SMEM)
PLAIN = (((1,), (0,)), ((), ()))
LEFT_T = (((0,), (0,)), ((), ()))


def dot(left, right, dims=PLAIN):
    return lax.dot_general(left, right, dims, preferred_element_type=F32)


def split2(value):
    high = value.astype(BF16)
    return high, (value - high.astype(F32)).astype(BF16)


def split3(value):
    high = value.astype(BF16).astype(F32)
    rest = value - high
    middle = rest.astype(BF16).astype(F32)
    return high, middle, rest - middle


def features(points, is_left):
    row = lax.broadcasted_iota(jnp.int32, points.shape, 0)
    is_point = (row >= 4) & (row < 7)
    scaled = jnp.where(is_point, (points - 0.5) * INV_RADIUS, 0.0)
    norm = jnp.sum(scaled * scaled, axis=0, keepdims=True)
    own_row, other_row = (0, 1) if is_left else (1, 0)
    if is_left:
        scaled = -2.0 * scaled
    high, middle, low = split3(scaled)

    def with_norm(part, norm_part):
        return jnp.where(row == own_row, norm_part, jnp.where(row == other_row, 1.0, part))

    norms = split3(norm)
    if is_left:
        parts = [with_norm(high, n) for n in norms] + [middle, middle, low]
    else:
        parts = [with_norm(p, n) for p, n in zip((high, middle, low), norms)] + [high, middle, high]
    return jnp.concatenate(parts, axis=0).astype(BF16)


def quarter_phi(squared):
    squared = jnp.maximum(squared, TINY)
    radial = squared * lax.rsqrt(squared)
    remain = jnp.maximum(1.0 - radial, 0.0)
    remain2 = remain * remain
    return (remain2 * remain2) * (radial + 0.25)


def stack_split(vector):
    high, low = split2(vector)
    return jnp.concatenate([high, low], axis=0), high


def split_product(stacked, high, weights_high, weights_low):
    both = dot(stacked, weights_high)
    rows = high.shape[0]
    return both[:rows] + both[rows:] + dot(high, weights_low)


def pack_kernel(centers, shifts, out):
    out[...] = jnp.zeros_like(out)
    out[:, 0:3, :] = jnp.broadcast_to(shifts[...][None], (out.shape[0],) + shifts.shape)
    out[:, 4:7, :] = jnp.broadcast_to(centers[...][None], (out.shape[0],) + centers.shape)


def lead_rows(value, count):
    row = lax.broadcasted_iota(jnp.int32, value.shape, value.ndim - 2)
    return jnp.where(row < count, value, 0.0)


def flat(ref):
    return jnp.concatenate([ref[part] for part in range(ref.shape[0])], axis=1)


def fill_weights(right_ref, left_ref, high_ref, low_ref):
    extent = right_ref.shape[0]
    step = math.gcd(extent, 1024)
    for first in range(0, extent, step):
        rows = slice(first, first + step)
        weights = quarter_phi(dot(right_ref[rows, :], left_ref[...]))
        high_ref[rows, :], low_ref[rows, :] = split2(weights)


def matvec(vector, high_ref, low_ref):
    stacked, high = stack_split(4.0 * vector)
    return split_product(stacked, high, high_ref[...], low_ref[...])


def build_kernel(me, every, right_ref, high_ref, low_ref, applied_out, left_ref):
    everything = flat(every)
    mine = every[me[0]]
    left_ref[...] = features(mine, True)
    right_ref[...] = features(everything, False).T
    fill_weights(right_ref, left_ref, high_ref, low_ref)
    applied = matvec(lead_rows(everything, 3), high_ref, low_ref) + SHIFT * lead_rows(mine, 3)
    applied_out[...] = jnp.broadcast_to(applied[0:4][None], applied_out.shape)


def edge_weights_kernel(first, after, right_ref, points, high_ref, low_ref, left_ref, padded_ref):
    padded_ref[...] = jnp.zeros_like(padded_ref)
    padded_ref[4:7, :] = points[:, first : first + left_ref.shape[1]]
    left_ref[...] = features(padded_ref[...], True)
    fill_weights(right_ref, left_ref, high_ref, low_ref)


def edge_motion_kernel(pair, high_ref, low_ref, out):
    out[...] = matvec(pair[...], high_ref, low_ref)


def lane_sum(value):
    return jnp.sum(value, axis=1, keepdims=True)


def ratio(top, bottom):
    row = lax.broadcasted_iota(jnp.int32, top.shape, 0)
    return jnp.where(row < 3, top / jnp.where(row < 3, bottom, 1.0), 0.0)


def own_part(ref, me, width):
    if width % 128 == 0:
        return ref[:, pl.ds(pl.multiple_of(me * width, 128), width)]
    lane = lax.broadcasted_iota(jnp.int32, (ref.shape[1], width), 0)
    column = lax.broadcasted_iota(jnp.int32, (ref.shape[1], width), 1)
    chosen = jnp.where(lane == me * width + column, 1.0, 0.0)
    return lax.dot_general(ref[...], chosen, PLAIN, precision=lax.Precision.HIGHEST, preferred_element_type=F32)


def turn_one_kernel(me, every, applied, high_ref, low_ref, applied_out, search_out, remain_out, numbers_out):
    width = every.shape[2]
    start = lead_rows(flat(every), 3)[0:4]
    got = flat(applied)
    norm = lane_sum(start * start)
    step = ratio(norm, lane_sum(start * got))
    remain = start - step * got
    following = lane_sum(remain * remain)
    search = remain + ratio(following, norm) * start
    search_out[...] = search
    remain_out[...] = remain
    numbers_out[0] = jnp.broadcast_to(step, numbers_out.shape[1:])
    numbers_out[1] = jnp.broadcast_to(following, numbers_out.shape[1:])
    product = matvec(jnp.concatenate([search, jnp.zeros_like(search)], axis=0), high_ref, low_ref)
    product = product[0:4] + SHIFT * own_part(search_out, me[0], width)
    applied_out[...] = jnp.broadcast_to(product[None], applied_out.shape)


def turn_two_kernel(me, every, applied, search_in, remain_in, numbers, high_ref, low_ref, partial_out, pair_out, norm_out):
    width = every.shape[2]
    start = lead_rows(flat(every), 3)[0:4]
    got = flat(applied)
    search = search_in[...]
    norm = numbers[1][:, 0:1]
    step = ratio(norm, lane_sum(search * got))
    iterate = numbers[0][:, 0:1] * start + step * search
    remain = remain_in[...] - step * got
    following = lane_sum(remain * remain)
    search = remain + ratio(following, norm) * search
    pair = jnp.concatenate([search, iterate], axis=0)
    pair_out[...] = pair
    norm_out[...] = jnp.broadcast_to(following, norm_out.shape)
    product = matvec(pair, high_ref, low_ref)
    mine = own_part(pair_out, me[0], width)[0:4]
    product = product[0:4] + SHIFT * mine
    partial_out[...] = jnp.broadcast_to(lane_sum(mine * product)[None], partial_out.shape)


def pick_kernel(me, send_list, partials, norm, pair, *rest):
    motions, (coefficients_out, tiles_out, edge_ref) = rest[:-3], rest[-3:]
    total = jnp.sum(partials[...], axis=0)[:, 0:1]
    step = ratio(norm[:, 0:1], total)
    mine = own_part(pair, me[0], coefficients_out.shape[1])
    coefficients_out[...] = (mine[4:8] + step * mine[0:4])[0:3]
    edge = 0
    for part in motions:
        motion = part[4:8, :] + step * part[0:4, :]
        for first in range(0, motion.shape[1], S):
            edge_ref[edge] = motion[:, first : first + S]
            edge += 1
    group, capacity = tiles_out.shape[0], tiles_out.shape[1] // 4
    for place in range(group):
        for position in range(capacity):
            tile = edge_ref[jnp.maximum(send_list[place, position], 0)]
            tiles_out[place, 4 * position : 4 * position + 4, 0:S] = tile


def blend(index):
    fraction = index.astype(F32) / (S - 1)
    return 1.0 - fraction, fraction


def six_products(left, right):
    lh, lm, ll = split3(left)
    rh, rm, rl = split3(right)
    lefts = jnp.concatenate([lh, lh, lm, lh, ll, lm], axis=0).astype(BF16)
    rights = jnp.concatenate([rh, rm, rh, rl, rh, rm], axis=0).astype(BF16)
    return dot(lefts, rights, LEFT_T)


def block_kernel(block_tiles, count, tiles, out, tile_ref, spread_ref, weight_ref):
    slot = pl.program_id(0)
    cells = S * S
    capacity = tiles.shape[1] // 4

    @pl.when(slot == 0)
    def _():
        index = lax.broadcasted_iota(jnp.int32, (2 * S, cells), 0)
        cell = lax.broadcasted_iota(jnp.int32, (2 * S, cells), 1)
        wanted = jnp.where(index < S, cell // S, cell % S + S)
        spread_ref[...] = jnp.where(index == wanted, 1.0, 0.0).astype(BF16)
        row = lax.broadcasted_iota(jnp.int32, (8, cells), 0)
        cell = lax.broadcasted_iota(jnp.int32, (8, cells), 1)
        j_low, j_high = blend(cell // S)
        k_low, k_high = blend(cell % S)
        j_weight = jnp.where(row % 2 == 0, j_low, j_high)
        k_weight = jnp.where(row // 2 == 0, k_low, k_high)
        weight_ref[0] = jnp.where(row < 4, j_weight * k_weight, 0.0)
        side = row % 4 // 2 == 0
        weight_ref[1] = jnp.where(row < 4, jnp.where(side, k_low, k_high), jnp.where(side, j_low, j_high))

    @pl.when(slot < count[0])
    def _():
        for edge in range(12):
            place = block_tiles[slot, edge]
            tile = tiles[place // capacity, pl.ds(place % capacity * 4, 4), :]
            for coordinate in range(3):
                tile_ref[coordinate, edge : edge + 1, :] = tile[coordinate : coordinate + 1, 0:S]
        along_low, along_high = blend(lax.broadcasted_iota(jnp.int32, (8, S), 1))
        row = lax.broadcasted_iota(jnp.int32, (8, S), 0)
        side = jnp.where(row % 2 == 0, along_low, along_high)
        for coordinate in range(3):
            first = tile_ref[coordinate, 0:8, :]
            straight = along_low * first[:, 0:1] + along_high * first[:, S - 1 : S]
            bent = jnp.where(row < 4, first - 2.0 * straight, 0.0)
            others = tile_ref[coordinate, 4:12, :]
            zero = jnp.zeros_like(others)
            placed = jnp.concatenate(
                [jnp.where(row < 4, others, zero), jnp.where(row < 4, zero, others)], axis=1
            )
            spread = dot(jnp.concatenate(split3(placed), axis=0).astype(BF16), spread_ref[...])
            spread = (spread[0:8] + spread[8:16]) + spread[16:24]
            lefts = jnp.concatenate([bent, side], axis=0)
            rights = jnp.concatenate([weight_ref[0], spread * weight_ref[1]], axis=0)
            out[0, coordinate] = six_products(lefts, rights)

    @pl.when(slot >= count[0])
    def _():
        out[...] = jnp.zeros_like(out)


def call(kernel, name, outs, specs, scratch=(), megabytes=13, work=0):
    shapes = tuple(jax.ShapeDtypeStruct(shape, dtype) for shape, dtype in outs)
    return pl.pallas_call(
        kernel,
        out_shape=shapes,
        in_specs=specs,
        out_specs=tuple(VMEM for _ in shapes),
        scratch_shapes=scratch,
        compiler_params=pltpu.CompilerParams(vmem_limit_bytes=megabytes << 20),
        cost_estimate=pl.CostEstimate(flops=work, bytes_accessed=0, transcendentals=0) if work else None,
        name=name,
    )


def shards(total, center_points, displacements, edge_points, send_list, block_tiles, block_count):
    width = center_points.shape[1]
    extent = total * width
    edge_width = edge_points.shape[1]
    group, capacity = send_list.shape[1:]
    slots = block_tiles.shape[0]
    me = (lax.axis_index("gx") * lax.axis_size("gy") + lax.axis_index("gy")).reshape(1)

    def spread_out(copies, axes):
        return lax.all_to_all(copies, axes, split_axis=0, concat_axis=0, tiled=True)

    (packed,) = call(pack_kernel, "pack", [((total, 8, width), F32)], [VMEM] * 2)(center_points, displacements)
    every = spread_out(packed, BOTH)
    matrix = ((extent, width), BF16)
    thin = ((total, 4, width), F32)
    right, high, low, applied = call(
        build_kernel,
        "build",
        [((extent, 48), BF16), matrix, matrix, thin],
        [SMEM, VMEM],
        [pltpu.VMEM((48, width), BF16)],
        15,
    )(me, every)
    piece = math.gcd(edge_width, 256)
    pieces = edge_width // piece

    def edge_weights(number, after):
        part = ((extent, piece), BF16)
        return call(
            functools.partial(edge_weights_kernel, number * piece),
            "edge_weights",
            [part, part],
            [pl.BlockSpec(memory_space=pl.ANY), VMEM, VMEM],
            [pltpu.VMEM((48, piece), BF16), pltpu.VMEM((8, piece), F32)],
            13,
            extent * piece * 2000,
        )(after, right, edge_points)

    applied_all = spread_out(applied, BOTH)
    weights = [edge_weights(number, me) for number in range(pieces // 2)]
    applied, search, remain, numbers = call(
        turn_one_kernel,
        "turn_one",
        [thin, ((4, extent), F32), ((4, extent), F32), ((2, 4, 128), F32)],
        [SMEM] + [VMEM] * 4,
    )(me, every, applied_all, high, low)
    applied_all = spread_out(applied, BOTH)
    weights += [edge_weights(number, numbers) for number in range(pieces // 2, pieces)]
    partials, pair, norm = call(
        turn_two_kernel,
        "turn_two",
        [((total, 4, 128), F32), ((8, extent), F32), ((4, 128), F32)],
        [SMEM] + [VMEM] * 7,
    )(me, every, applied_all, search, remain, numbers, high, low)
    partials = spread_out(partials, BOTH)
    motions = [
        call(edge_motion_kernel, "edge_motion", [((8, piece), F32)], [VMEM] * 3, (), 13, extent * piece * 1000)(
            pair, *pieces_of
        )[0]
        for pieces_of in weights
    ]
    coefficients, tiles = call(
        pick_kernel,
        "pick",
        [((3, width), F32), ((group, capacity * 4, 128), F32)],
        [SMEM] * 2 + [VMEM] * (3 + pieces),
        [pltpu.VMEM((edge_width // S, 4, S), F32)],
    )(me, send_list[0], partials, norm, pair, *motions)
    tiles = spread_out(tiles, "gy")
    block_motion = pl.pallas_call(
        block_kernel,
        out_shape=jax.ShapeDtypeStruct((slots, 3, S, S * S), F32),
        grid=(slots,),
        in_specs=[SMEM, SMEM, VMEM],
        out_specs=pl.BlockSpec((1, 3, S, S * S), lambda slot: (slot, 0, 0, 0)),
        scratch_shapes=[
            pltpu.VMEM((3, 12, S), F32),
            pltpu.VMEM((2 * S, S * S), BF16),
            pltpu.VMEM((2, 8, S * S), F32),
        ],
        compiler_params=pltpu.CompilerParams(vmem_limit_bytes=24 << 20),
        name="blocks",
    )(block_tiles, block_count, tiles)
    return coefficients, block_motion


def solution(mesh):
    total = mesh.shape["gx"] * mesh.shape["gy"]
    split = P(None, BOTH)
    return jax.shard_map(
        functools.partial(shards, total),
        mesh=mesh,
        in_specs=(split, split, split, P(BOTH, None, None), P(BOTH, None), P(BOTH)),
        out_specs=(split, P(BOTH, None, None, None)),
        check_vma=False,
    )
```

time: 125 us -> 126 us (level)
  local copies, waits for them, and re-layouts: 5.09 us -> 42.8 us
  Pallas kernels: 67.4 us -> 41.8 us
  blocking collectives: 10.4 us -> 0 us
  starting transfers between devices: 16.3 us -> 25.5 us
  waiting for transfers between devices: 22.9 us -> 14.4 us
    unnamed x17 -> x53, local copies, waits for them, and re-layouts: 4.49 us -> 42.8 us
    pallas_call x5 -> x12, Pallas kernels: 59.3 us -> 33.5 us  [the longest x4 16.2 us: edge_weights(): call(functools.partial(edge_weights_kernel, number * piece), 'edge_weight...]
    all_to_all x1 -> x0, blocking collectives: 10.4 us -> none  [spread_out(): return lax.all_to_all(copies, axes, split_axis=0, concat_axis=0, tiled=True)]
    all_to_all x4 -> x5, starting transfers between devices: 16.3 us -> 25.5 us  [spread_out(): return lax.all_to_all(copies, axes, split_axis=0, concat_axis=0, tiled=True)]
    all_to_all x4 -> x5, waiting for transfers between devices: 22.9 us -> 14.4 us  [spread_out(): return lax.all_to_all(copies, axes, split_axis=0, concat_axis=0, tiled=True)]
  transfers between devices with their start and end apart: 4 -> 5, of which waited for: 3 -> 2; matrix products, arithmetic and copies ran while one was open for 0% -> 1% of each run, Pallas kernels for 20% -> 17%
where the time goes in v2:
time: 126 us
  local copies, waits for them, and re-layouts  42.8 us (34%)
  Pallas kernels  41.8 us (33%)
  starting transfers between devices  25.5 us (20%)
  waiting for transfers between devices  14.4 us (11%)
  between operations  1.44 us (1%)
    unnamed x53, local copies, waits for them, and re-layouts  42.8 us
    all_to_all x5, starting transfers between devices, spread_out(): return lax.all_to_all(copies, axes, split_axis=0, concat_axis=0, tiled=True)  25.5 us
    pallas_call x4, Pallas kernels, edge_weights(): call(functools.partial(edge_weights_kernel, number * piece), 'edge_weight...  16.2 us
    all_to_all x5, waiting for transfers between devices, spread_out(): return lax.all_to_all(copies, axes, split_axis=0, concat_axis=0, tiled=True)  14.4 us
    pallas_call x1, Pallas kernels, shards(): pl.pallas_call(block_kernel, out_shape=jax.ShapeDtypeStruct((slots, 3, S,...  7.53 us
    pallas_call x1, Pallas kernels, shards(): call(build_kernel, 'build', [((extent, 48), BF16), matrix, matrix, thin],...  6.53 us
    pallas_call x4, Pallas kernels, shards(): call(edge_motion_kernel, 'edge_motion', [((8, piece), F32)], [VMEM] * 3,...  4.78 us
  transfers between devices with their start and end apart: 5, of which 2 were waited for; matrix products, arithmetic and copies ran while one was open for 1% of the time, Pallas kernels for 17%

profile of v2, /device:TPU:0, one launch (start us, length us, event | category | flops | bytes accessed | tf_op | source)
XLA Modules:
  0.0 125.9 jit_solution(16891407377193391416)
XLA Ops:
  0.6 0.7 copy-done.22
  1.3 0.7 copy-done.23
  2.0 0.8 pack.1
  2.8 7.3 %all-to-all-start = ((f32[32,8,256]{2,1,0:T(8,128)}), f32[32,8,256]{2,1,0:T(8,128)S(1)}, u32[]{:S(2)}, u32[]{:S(2)}) async-start(f32[32,8,256]{2,1,0:T(8,128)} %pack.1), calls=%async_computation | async-start | bytes 524288 | tf_op jit(solution)/shard_map/all_to_all | solution.py:291
  10.1 0.8 copy.8
  10.8 9.8 %all-to-all-done.every = f32[32,8,256]{2,1,0:T(8,128)S(1)} async-done(((f32[32,8,256]{2,1,0:T(8,128)}), f32[32,8,256]{2,1,0:T(8,128)S(1)}, u32[]{:S(2)}, u32[]{:S(2)}) %all-to-all-start) | async-done | bytes 262176 | tf_op jit(solution)/shard_map/all_to_all | solution.py:291
  20.7 6.5 %build.1 = (bf16[8192,48]{1,0:T(8,128)(2,1)S(1)}, bf16[8192,256]{1,0:T(8,128)(2,1)S(1)}, bf16[8192,256]{1,0:T(8,128)(2,1)S(1)}, f32[32,4,256]{2,1,0:T(4,128)}) custom-call(s32[1]{0:T(128)} %bitcast.me.after, f32[32,8,256]{2,1,0:T(8,128)S(1)} %all-to-all-done.every), custom_call_target="tpu_custom_call" | custom-call | tf_op jit(solution)/shard_map/build/pallas_call | solution.py:297
  27.2 2.0 %copy-done = bf16[8192,256]{1,0:T(8,128)(2,1)} copy-done((bf16[8192,256]{1,0:T(8,128)(2,1)}, bf16[8192,256]{1,0:T(8,128)(2,1)S(1)}, u32[]{:S(2)}) %copy-start) | copy-done | bytes 4194328
  29.2 2.0 %copy-done.3 = bf16[8192,256]{1,0:T(8,128)(2,1)} copy-done((bf16[8192,256]{1,0:T(8,128)(2,1)}, bf16[8192,256]{1,0:T(8,128)(2,1)S(1)}, u32[]{:S(2)}) %copy-start.3) | copy-done | bytes 4194328
  31.2 2.7 %all-to-all-start.1 = ((f32[32,4,256]{2,1,0:T(4,128)}), f32[32,4,256]{2,1,0:T(4,128)S(1)}, u32[]{:S(2)}, u32[]{:S(2)}) async-start(f32[32,4,256]{2,1,0:T(4,128)} %get-tuple-element.23), calls=%async_computation.1 | async-start | bytes 262144 | tf_op jit(solution)/shard_map/all_to_all | solution.py:291
  33.9 0.0 copy-start.25
  34.0 0.7 copy-done.25
  34.7 4.1 %edge_weights.5 = (bf16[8192,256]{1,0:T(8,128)(2,1)S(1)}, bf16[8192,256]{1,0:T(8,128)(2,1)S(1)}) custom-call(s32[1]{0:T(128)} %bitcast.me.after, bf16[8192,48]{1,0:T(8,128)(2,1)S(1)} %get-tuple-element.33.right_ref, f32[3,1024]{1,0:T(4,128)S(1)} %copy-done.25), custom_call_target="tpu_custom_call" | custom-call | flops 4194304000 | tf_op jit(solution)/shard_map/edge_weights/pallas_call | solution.py:310
  38.7 2.0 %copy-done.10 = bf16[8192,256]{1,0:T(8,128)(2,1)} copy-done((bf16[8192,256]{1,0:T(8,128)(2,1)}, bf16[8192,256]{1,0:T(8,128)(2,1)S(1)}, u32[]{:S(2)}) %copy-start.10) | copy-done | bytes 4194328
  40.7 1.9 %copy-done.12 = bf16[8192,256]{1,0:T(8,128)(2,1)} copy-done((bf16[8192,256]{1,0:T(8,128)(2,1)}, bf16[8192,256]{1,0:T(8,128)(2,1)S(1)}, u32[]{:S(2)}) %copy-start.12) | copy-done | bytes 4194328
  42.7 4.0 %edge_weights.4 = (bf16[8192,256]{1,0:T(8,128)(2,1)S(1)}, bf16[8192,256]{1,0:T(8,128)(2,1)S(1)}) custom-call(s32[1]{0:T(128)} %bitcast.me.after, bf16[8192,48]{1,0:T(8,128)(2,1)S(1)} %get-tuple-element.33.right_ref, f32[3,1024]{1,0:T(4,128)S(1)} %copy-done.25), custom_call_target="tpu_custom_call" | custom-call | flops 4194304000 | tf_op jit(solution)/shard_map/edge_weights/pallas_call | solution.py:310
  46.7 2.0 %copy-done.6 = bf16[8192,256]{1,0:T(8,128)(2,1)} copy-done((bf16[8192,256]{1,0:T(8,128)(2,1)}, bf16[8192,256]{1,0:T(8,128)(2,1)S(1)}, u32[]{:S(2)}) %copy-start.6) | copy-done | bytes 4194328
  48.7 2.0 %copy-done.8 = bf16[8192,256]{1,0:T(8,128)(2,1)} copy-done((bf16[8192,256]{1,0:T(8,128)(2,1)}, bf16[8192,256]{1,0:T(8,128)(2,1)S(1)}, u32[]{:S(2)}) %copy-start.8) | copy-done | bytes 4194328
  50.7 2.2 %copy-done.1 = bf16[8192,256]{1,0:T(8,128)(2,1)S(1)} copy-done((bf16[8192,256]{1,0:T(8,128)(2,1)S(1)}, bf16[8192,256]{1,0:T(8,128)(2,1)}, u32[]{:S(2)}) %copy-start.1) | copy-done | bytes 4194328
  52.9 2.2 %copy-done.4 = bf16[8192,256]{1,0:T(8,128)(2,1)S(1)} copy-done((bf16[8192,256]{1,0:T(8,128)(2,1)S(1)}, bf16[8192,256]{1,0:T(8,128)(2,1)}, u32[]{:S(2)}) %copy-start.4) | copy-done | bytes 4194328
  55.1 2.2 %turn_one.1 = (f32[32,4,256]{2,1,0:T(4,128)}, f32[4,8192]{1,0:T(4,128)S(1)}, f32[4,8192]{1,0:T(4,128)S(1)}, f32[2,4,128]{2,1,0:T(4,128)S(1)}) custom-call(s32[1]{0:T(128)} %bitcast.me.after, f32[32,8,256]{2,1,0:T(8,128)S(1)} %all-to-all-done.every, f32[32,4,256]{2,1,0:T(4,128)S(1)} %all-to-all-done.1.applied, bf16[8192,256]{1,0:T(8,128)(2,1)S(1)} %copy-done.1, ...), custom_call_target="tpu_custom_call" | custom-call | tf_op jit(solution)/shard_map/turn_one/pallas_call | solution.py:322
  57.3 5.9 %all-to-all-start.2 = ((f32[32,4,256]{2,1,0:T(4,128)}), f32[32,4,256]{2,1,0:T(4,128)S(1)}, u32[]{:S(2)}, u32[]{:S(2)}) async-start(f32[32,4,256]{2,1,0:T(4,128)} %get-tuple-element.26), calls=%async_computation.2 | async-start | bytes 262144 | tf_op jit(solution)/shard_map/all_to_all | solution.py:291
  63.2 4.0 %edge_weights.7 = (bf16[8192,256]{1,0:T(8,128)(2,1)S(1)}, bf16[8192,256]{1,0:T(8,128)(2,1)S(1)}) custom-call(f32[2,4,128]{2,1,0:T(4,128)S(1)} %get-tuple-element.29.numbers.after, bf16[8192,48]{1,0:T(8,128)(2,1)S(1)} %get-tuple-element.33.right_ref, f32[3,1024]{1,0:T(4,128)S(1)} %copy-done.25), custom_call_target="tpu_custom_call" | custom-call | flops 4194304000 | tf_op jit(solution)/shard_map/edge_weights/pallas_call | solution.py:310
  67.2 2.0 %copy-done.18 = bf16[8192,256]{1,0:T(8,128)(2,1)} copy-done((bf16[8192,256]{1,0:T(8,128)(2,1)}, bf16[8192,256]{1,0:T(8,128)(2,1)S(1)}, u32[]{:S(2)}) %copy-start.18) | copy-done | bytes 4194328
  69.2 2.1 %copy-done.20 = bf16[8192,256]{1,0:T(8,128)(2,1)} copy-done((bf16[8192,256]{1,0:T(8,128)(2,1)}, bf16[8192,256]{1,0:T(8,128)(2,1)S(1)}, u32[]{:S(2)}) %copy-start.20) | copy-done | bytes 4194328
  71.3 4.0 %edge_weights.6 = (bf16[8192,256]{1,0:T(8,128)(2,1)S(1)}, bf16[8192,256]{1,0:T(8,128)(2,1)S(1)}) custom-call(f32[2,4,128]{2,1,0:T(4,128)S(1)} %get-tuple-element.29.numbers.after, bf16[8192,48]{1,0:T(8,128)(2,1)S(1)} %get-tuple-element.33.right_ref, f32[3,1024]{1,0:T(4,128)S(1)} %copy-done.25), custom_call_target="tpu_custom_call" | custom-call | flops 4194304000 | tf_op jit(solution)/shard_map/edge_weights/pallas_call | solution.py:310
  75.3 2.0 %copy-done.14 = bf16[8192,256]{1,0:T(8,128)(2,1)} copy-done((bf16[8192,256]{1,0:T(8,128)(2,1)}, bf16[8192,256]{1,0:T(8,128)(2,1)S(1)}, u32[]{:S(2)}) %copy-start.14) | copy-done | bytes 4194328
  77.4 2.0 %copy-done.16 = bf16[8192,256]{1,0:T(8,128)(2,1)} copy-done((bf16[8192,256]{1,0:T(8,128)(2,1)}, bf16[8192,256]{1,0:T(8,128)(2,1)S(1)}, u32[]{:S(2)}) %copy-start.16) | copy-done | bytes 4194328
  79.4 2.2 %copy-done.2 = bf16[8192,256]{1,0:T(8,128)(2,1)S(1)} copy-done((bf16[8192,256]{1,0:T(8,128)(2,1)S(1)}, bf16[8192,256]{1,0:T(8,128)(2,1)}, u32[]{:S(2)}) %copy-start.2) | copy-done | bytes 4194328
  81.6 2.2 %copy-done.5 = bf16[8192,256]{1,0:T(8,128)(2,1)S(1)} copy-done((bf16[8192,256]{1,0:T(8,128)(2,1)S(1)}, bf16[8192,256]{1,0:T(8,128)(2,1)}, u32[]{:S(2)}) %copy-start.5) | copy-done | bytes 4194328
  83.8 2.4 %turn_two.1 = (f32[32,4,128]{2,1,0:T(4,128)}, f32[8,8192]{1,0:T(8,128)S(1)}, f32[4,128]{1,0:T(4,128)S(1)}) custom-call(s32[1]{0:T(128)} %bitcast.me.after, f32[32,8,256]{2,1,0:T(8,128)S(1)} %all-to-all-done.every, f32[32,4,256]{2,1,0:T(4,128)S(1)} %all-to-all-done.2.applied, f32[4,8192]{1,0:T(4,128)S(1)} %get-tuple-element.27.search_in, ...), custom_call_target="tpu_custom_call" | custom-call | tf_op jit(solution)/shard_map/turn_two/pallas_call | solution.py:330
  86.1 5.9 %all-to-all-start.3 = ((f32[32,4,128]{2,1,0:T(4,128)}), f32[32,4,128]{2,1,0:T(4,128)S(1)}, u32[]{:S(2)}, u32[]{:S(2)}) async-start(f32[32,4,128]{2,1,0:T(4,128)} %get-tuple-element.30), calls=%async_computation.3 | async-start | bytes 131072 | tf_op jit(solution)/shard_map/all_to_all | solution.py:291
  92.0 2.2 %copy-done.19 = bf16[8192,256]{1,0:T(8,128)(2,1)S(1)} copy-done((bf16[8192,256]{1,0:T(8,128)(2,1)S(1)}, bf16[8192,256]{1,0:T(8,128)(2,1)}, u32[]{:S(2)}) %copy-start.19) | copy-done | bytes 4194328
  94.2 2.2 %copy-done.21 = bf16[8192,256]{1,0:T(8,128)(2,1)S(1)} copy-done((bf16[8192,256]{1,0:T(8,128)(2,1)S(1)}, bf16[8192,256]{1,0:T(8,128)(2,1)}, u32[]{:S(2)}) %copy-start.21) | copy-done | bytes 4194328
  96.4 1.2 edge_motion.7.rest_3_
  97.6 1.0 copy-done.15
  98.6 1.3 %copy-done.17 = bf16[8192,256]{1,0:T(8,128)(2,1)S(1)} copy-done((bf16[8192,256]{1,0:T(8,128)(2,1)S(1)}, bf16[8192,256]{1,0:T(8,128)(2,1)}, u32[]{:S(2)}) %copy-start.17) | copy-done | bytes 4194328
  99.9 1.2 edge_motion.6.rest_2_
  101.1 1.0 copy-done.11
  102.0 1.3 %copy-done.13 = bf16[8192,256]{1,0:T(8,128)(2,1)S(1)} copy-done((bf16[8192,256]{1,0:T(8,128)(2,1)S(1)}, bf16[8192,256]{1,0:T(8,128)(2,1)}, u32[]{:S(2)}) %copy-start.13) | copy-done | bytes 4194328
  103.3 1.2 edge_motion.5.rest_1_
  104.5 1.0 copy-done.7
  105.5 1.3 %copy-done.9 = bf16[8192,256]{1,0:T(8,128)(2,1)S(1)} copy-done((bf16[8192,256]{1,0:T(8,128)(2,1)S(1)}, bf16[8192,256]{1,0:T(8,128)(2,1)}, u32[]{:S(2)}) %copy-start.9) | copy-done | bytes 4194328
  106.8 1.2 edge_motion.4.rest_0_
  108.0 1.5 %pick.1 = (f32[3,256]{1,0:T(4,128)}, f32[8,24,128]{2,1,0:T(8,128)}) custom-call(s32[1]{0:T(128)} %bitcast.me.after, s32[8,6]{1,0:T(8,128)S(1)} %bitcast.2, f32[32,4,128]{2,1,0:T(4,128)S(1)} %all-to-all-done.3.partials, f32[4,128]{1,0:T(4,128)S(1)} %get-tuple-element.31.norm, f32[8,8192]{1,0:T(8,128)S(1)} %get-tuple-element.32.pair, ...), custom_call_target="tpu_custom_call" | custom-call | tf_op jit(solution)/shard_map/pick/pallas_call | solution.py:343
  109.5 3.7 %all-to-all-start.4 = ((f32[8,24,128]{2,1,0:T(8,128)}), f32[8,24,128]{2,1,0:T(8,128)S(1)}, u32[]{:S(2)}, u32[]{:S(2)}) async-start(f32[8,24,128]{2,1,0:T(8,128)} %get-tuple-element.43), calls=%async_computation.4 | async-start | bytes 196608 | tf_op jit(solution)/shard_map/all_to_all | solution.py:291
  113.8 4.5 %all-to-all-done.4.tiles = f32[8,24,128]{2,1,0:T(8,128)S(1)} async-done(((f32[8,24,128]{2,1,0:T(8,128)}), f32[8,24,128]{2,1,0:T(8,128)S(1)}, u32[]{:S(2)}, u32[]{:S(2)}) %all-to-all-start.4) | async-done | bytes 98336 | tf_op jit(solution)/shard_map/all_to_all | solution.py:291
  118.4 7.5 %blocks.1 = f32[4,3,64,4096]{3,2,1,0:T(8,128)} custom-call(s32[4,12]{1,0:T(4,128)S(1)} %copy-done.24, s32[1]{0:T(128)S(6)} %copy.9.count, f32[8,24,128]{2,1,0:T(8,128)S(1)} %all-to-all-done.4.tiles), custom_call_target="tpu_custom_call" | custom-call | tf_op jit(solution)/shard_map/blocks/pallas_call | solution.py:351
  (29 shorter events, 0.1 us)
Async XLA Ops:
  0.6 0.7 copy-start.22
  1.3 0.7 copy-start.23
  2.8 17.9 %all-to-all-start = ((f32[32,8,256]{2,1,0:T(8,128)}), f32[32,8,256]{2,1,0:T(8,128)S(1)}, u32[]{:S(2)}, u32[]{:S(2)}) async-start(f32[32,8,256]{2,1,0:T(8,128)} %pack.1), calls=%async_computation | async-start | bytes 524288 | tf_op jit(solution)/shard_map/all_to_all | solution.py:291
  27.2 2.0 %copy-start = (bf16[8192,256]{1,0:T(8,128)(2,1)}, bf16[8192,256]{1,0:T(8,128)(2,1)S(1)}, u32[]{:S(2)}) copy-start(bf16[8192,256]{1,0:T(8,128)(2,1)S(1)} %get-tuple-element.24.high_ref) | copy-start | bytes 12582916
  29.2 2.0 %copy-start.3 = (bf16[8192,256]{1,0:T(8,128)(2,1)}, bf16[8192,256]{1,0:T(8,128)(2,1)S(1)}, u32[]{:S(2)}) copy-start(bf16[8192,256]{1,0:T(8,128)(2,1)S(1)} %get-tuple-element.25.low_ref) | copy-start | bytes 12582916
  31.2 19.6 %all-to-all-start.1 = ((f32[32,4,256]{2,1,0:T(4,128)}), f32[32,4,256]{2,1,0:T(4,128)S(1)}, u32[]{:S(2)}, u32[]{:S(2)}) async-start(f32[32,4,256]{2,1,0:T(4,128)} %get-tuple-element.23), calls=%async_computation.1 | async-start | bytes 262144 | tf_op jit(solution)/shard_map/all_to_all | solution.py:291
  33.9 0.7 copy-start.25
  38.7 2.0 %copy-start.10 = (bf16[8192,256]{1,0:T(8,128)(2,1)}, bf16[8192,256]{1,0:T(8,128)(2,1)S(1)}, u32[]{:S(2)}) copy-start(bf16[8192,256]{1,0:T(8,128)(2,1)S(1)} %get-tuple-element.36.high_ref) | copy-start | bytes 12582916
  40.7 1.9 %copy-start.12 = (bf16[8192,256]{1,0:T(8,128)(2,1)}, bf16[8192,256]{1,0:T(8,128)(2,1)S(1)}, u32[]{:S(2)}) copy-start(bf16[8192,256]{1,0:T(8,128)(2,1)S(1)} %get-tuple-element.37.low_ref) | copy-start | bytes 12582916
  46.7 2.0 %copy-start.6 = (bf16[8192,256]{1,0:T(8,128)(2,1)}, bf16[8192,256]{1,0:T(8,128)(2,1)S(1)}, u32[]{:S(2)}) copy-start(bf16[8192,256]{1,0:T(8,128)(2,1)S(1)} %get-tuple-element.34.high_ref) | copy-start | bytes 12582916
  48.7 2.0 %copy-start.8 = (bf16[8192,256]{1,0:T(8,128)(2,1)}, bf16[8192,256]{1,0:T(8,128)(2,1)S(1)}, u32[]{:S(2)}) copy-start(bf16[8192,256]{1,0:T(8,128)(2,1)S(1)} %get-tuple-element.35.low_ref) | copy-start | bytes 12582916
  50.7 2.2 %copy-start.1 = (bf16[8192,256]{1,0:T(8,128)(2,1)S(1)}, bf16[8192,256]{1,0:T(8,128)(2,1)}, u32[]{:S(2)}) copy-start(bf16[8192,256]{1,0:T(8,128)(2,1)} %copy-done) | copy-start | bytes 12582916
  52.9 2.2 %copy-start.4 = (bf16[8192,256]{1,0:T(8,128)(2,1)S(1)}, bf16[8192,256]{1,0:T(8,128)(2,1)}, u32[]{:S(2)}) copy-start(bf16[8192,256]{1,0:T(8,128)(2,1)} %copy-done.3) | copy-start | bytes 12582916
  57.3 22.1 %all-to-all-start.2 = ((f32[32,4,256]{2,1,0:T(4,128)}), f32[32,4,256]{2,1,0:T(4,128)S(1)}, u32[]{:S(2)}, u32[]{:S(2)}) async-start(f32[32,4,256]{2,1,0:T(4,128)} %get-tuple-element.26), calls=%async_computation.2 | async-start | bytes 262144 | tf_op jit(solution)/shard_map/all_to_all | solution.py:291
  67.2 2.0 %copy-start.18 = (bf16[8192,256]{1,0:T(8,128)(2,1)}, bf16[8192,256]{1,0:T(8,128)(2,1)S(1)}, u32[]{:S(2)}) copy-start(bf16[8192,256]{1,0:T(8,128)(2,1)S(1)} %get-tuple-element.40.high_ref) | copy-start | bytes 12582916
  69.2 2.1 %copy-start.20 = (bf16[8192,256]{1,0:T(8,128)(2,1)}, bf16[8192,256]{1,0:T(8,128)(2,1)S(1)}, u32[]{:S(2)}) copy-start(bf16[8192,256]{1,0:T(8,128)(2,1)S(1)} %get-tuple-element.41.low_ref) | copy-start | bytes 12582916
  75.3 2.0 %copy-start.14 = (bf16[8192,256]{1,0:T(8,128)(2,1)}, bf16[8192,256]{1,0:T(8,128)(2,1)S(1)}, u32[]{:S(2)}) copy-start(bf16[8192,256]{1,0:T(8,128)(2,1)S(1)} %get-tuple-element.38.high_ref) | copy-start | bytes 12582916
  77.4 2.0 %copy-start.16 = (bf16[8192,256]{1,0:T(8,128)(2,1)}, bf16[8192,256]{1,0:T(8,128)(2,1)S(1)}, u32[]{:S(2)}) copy-start(bf16[8192,256]{1,0:T(8,128)(2,1)S(1)} %get-tuple-element.39.low_ref) | copy-start | bytes 12582916
  79.4 2.2 %copy-start.2 = (bf16[8192,256]{1,0:T(8,128)(2,1)S(1)}, bf16[8192,256]{1,0:T(8,128)(2,1)}, u32[]{:S(2)}) copy-start(bf16[8192,256]{1,0:T(8,128)(2,1)} %copy-done) | copy-start | bytes 12582916
  81.6 2.2 %copy-start.5 = (bf16[8192,256]{1,0:T(8,128)(2,1)S(1)}, bf16[8192,256]{1,0:T(8,128)(2,1)}, u32[]{:S(2)}) copy-start(bf16[8192,256]{1,0:T(8,128)(2,1)} %copy-done.3) | copy-start | bytes 12582916
  86.1 21.9 %all-to-all-start.3 = ((f32[32,4,128]{2,1,0:T(4,128)}), f32[32,4,128]{2,1,0:T(4,128)S(1)}, u32[]{:S(2)}, u32[]{:S(2)}) async-start(f32[32,4,128]{2,1,0:T(4,128)} %get-tuple-element.30), calls=%async_computation.3 | async-start | bytes 131072 | tf_op jit(solution)/shard_map/all_to_all | solution.py:291
  92.0 2.2 %copy-start.19 = (bf16[8192,256]{1,0:T(8,128)(2,1)S(1)}, bf16[8192,256]{1,0:T(8,128)(2,1)}, u32[]{:S(2)}) copy-start(bf16[8192,256]{1,0:T(8,128)(2,1)} %copy-done.18) | copy-start | bytes 12582916
  94.2 2.2 %copy-start.21 = (bf16[8192,256]{1,0:T(8,128)(2,1)S(1)}, bf16[8192,256]{1,0:T(8,128)(2,1)}, u32[]{:S(2)}) copy-start(bf16[8192,256]{1,0:T(8,128)(2,1)} %copy-done.20) | copy-start | bytes 12582916
  96.4 2.2 %copy-start.15 = (bf16[8192,256]{1,0:T(8,128)(2,1)S(1)}, bf16[8192,256]{1,0:T(8,128)(2,1)}, u32[]{:S(2)}) copy-start(bf16[8192,256]{1,0:T(8,128)(2,1)} %copy-done.14) | copy-start | bytes 12582916
  96.4 3.5 %copy-start.17 = (bf16[8192,256]{1,0:T(8,128)(2,1)S(1)}, bf16[8192,256]{1,0:T(8,128)(2,1)}, u32[]{:S(2)}) copy-start(bf16[8192,256]{1,0:T(8,128)(2,1)} %copy-done.16) | copy-start | bytes 12582916
  99.9 2.2 %copy-start.11 = (bf16[8192,256]{1,0:T(8,128)(2,1)S(1)}, bf16[8192,256]{1,0:T(8,128)(2,1)}, u32[]{:S(2)}) copy-start(bf16[8192,256]{1,0:T(8,128)(2,1)} %copy-done.10) | copy-start | bytes 12582916
  99.9 3.5 %copy-start.13 = (bf16[8192,256]{1,0:T(8,128)(2,1)S(1)}, bf16[8192,256]{1,0:T(8,128)(2,1)}, u32[]{:S(2)}) copy-start(bf16[8192,256]{1,0:T(8,128)(2,1)} %copy-done.12) | copy-start | bytes 12582916
  103.3 2.2 %copy-start.7 = (bf16[8192,256]{1,0:T(8,128)(2,1)S(1)}, bf16[8192,256]{1,0:T(8,128)(2,1)}, u32[]{:S(2)}) copy-start(bf16[8192,256]{1,0:T(8,128)(2,1)} %copy-done.6) | copy-start | bytes 12582916
  103.3 3.5 %copy-start.9 = (bf16[8192,256]{1,0:T(8,128)(2,1)S(1)}, bf16[8192,256]{1,0:T(8,128)(2,1)}, u32[]{:S(2)}) copy-start(bf16[8192,256]{1,0:T(8,128)(2,1)} %copy-done.8) | copy-start | bytes 12582916
  106.8 11.6 %copy-start.24 = (s32[4,12]{1,0:T(4,128)S(1)}, s32[4,12]{1,0:T(4,128)}, u32[]{:S(2)}) copy-start(s32[4,12]{1,0:T(4,128)} %block_tiles.1) | copy-start | bytes 580
  109.5 8.9 %all-to-all-start.4 = ((f32[8,24,128]{2,1,0:T(8,128)}), f32[8,24,128]{2,1,0:T(8,128)S(1)}, u32[]{:S(2)}, u32[]{:S(2)}) async-start(f32[8,24,128]{2,1,0:T(8,128)} %get-tuple-element.43), calls=%async_computation.4 | async-start | bytes 196608 | tf_op jit(solution)/shard_map/all_to_all | solution.py:291

commit v3 on v2

v3 whole, which is shorter than its diff:
```python
import functools
import math

import jax
import jax.numpy as jnp
from jax import lax
from jax.experimental import pallas as pl
from jax.experimental.pallas import tpu as pltpu
from jax.sharding import PartitionSpec as P

S = 64
SHIFTS = S.bit_length() - 1
SHIFT = 0.1
INV_RADIUS = 4.0
TINY = 1e-12
BOTH = ("gx", "gy")
LARGE = 56
F32, BF16 = jnp.float32, jnp.bfloat16
ANY = pl.BlockSpec(memory_space=pl.ANY)
VMEM = pl.BlockSpec(memory_space=pltpu.VMEM)
SMEM = pl.BlockSpec(memory_space=pltpu.SMEM)
PLAIN = (((1,), (0,)), ((), ()))
LEFT_T = (((0,), (0,)), ((), ()))


def dot(left, right, dims=PLAIN):
    return lax.dot_general(left, right, dims, preferred_element_type=F32)


def split2(value):
    high = value.astype(BF16)
    return high, (value - high.astype(F32)).astype(BF16)


def split3(value):
    high = value.astype(BF16).astype(F32)
    rest = value - high
    middle = rest.astype(BF16).astype(F32)
    return high, middle, rest - middle


def features(points, is_left):
    row = lax.broadcasted_iota(jnp.int32, points.shape, 0)
    is_point = (row >= 4) & (row < 7)
    scaled = jnp.where(is_point, (points - 0.5) * INV_RADIUS, 0.0)
    norm = jnp.sum(scaled * scaled, axis=0, keepdims=True)
    own_row, other_row = (0, 1) if is_left else (1, 0)
    if is_left:
        scaled = -2.0 * scaled
    high, middle, low = split3(scaled)

    def with_norm(part, norm_part):
        return jnp.where(row == own_row, norm_part, jnp.where(row == other_row, 1.0, part))

    norms = split3(norm)
    if is_left:
        parts = [with_norm(high, n) for n in norms] + [middle, middle, low]
    else:
        parts = [with_norm(p, n) for p, n in zip((high, middle, low), norms)] + [high, middle, high]
    return jnp.concatenate(parts, axis=0).astype(BF16)


def quarter_phi(squared):
    squared = jnp.maximum(squared, TINY)
    remain = jnp.maximum(1.0 - squared * lax.rsqrt(squared), 0.0)
    remain2 = remain * remain
    return (remain2 * remain2) * (1.25 - remain)


def pack_kernel(centers, shifts, out, centers_ref, shifts_ref, done):
    copies = [
        pltpu.make_async_copy(centers, centers_ref, done.at[0]),
        pltpu.make_async_copy(shifts, shifts_ref, done.at[1]),
    ]
    for copy in copies:
        copy.start()
    out[...] = jnp.zeros_like(out)
    for copy in copies:
        copy.wait()
    out[:, 0:3, :] = jnp.broadcast_to(shifts_ref[...][None], (out.shape[0],) + shifts.shape)
    out[:, 4:7, :] = jnp.broadcast_to(centers_ref[...][None], (out.shape[0],) + centers.shape)


def lead_rows(value, count):
    row = lax.broadcasted_iota(jnp.int32, value.shape, value.ndim - 2)
    return jnp.where(row < count, value, 0.0)


def flat(ref):
    return jnp.concatenate([ref[part] for part in range(ref.shape[0])], axis=1)


def whole_slice(number, size):
    return pl.ds(pl.multiple_of(number * size, size), size)


def keep_vector(vector, kept_ref):
    both = jnp.concatenate(split2(4.0 * vector), axis=0)
    points = kept_ref.shape[2]
    for number in range(kept_ref.shape[0]):
        kept_ref[number] = both[:, number * points : (number + 1) * points]


def end_sum(both):
    rows = both.shape[0] // 2
    return both[:rows] + both[rows:]


def made_product(right_ref, left_ref, kept_ref, inside, store=None):
    pieces, rows, size = kept_ref.shape
    width = left_ref.shape[1]
    step_columns = math.gcd(width, 256)
    columns = [slice(first, first + step_columns) for first in range(0, width, step_columns)]
    inside = math.gcd(pieces, inside)

    def one_round(turn, sums):
        sums = list(sums)
        for step in range(inside):
            number = turn * inside + step
            for place, piece in enumerate(columns):
                squared = dot(right_ref[whole_slice(number, size), :], left_ref[:, piece])
                weights = split2(quarter_phi(squared))
                if store is not None:
                    for held, part in zip(store, weights):
                        held[whole_slice(number, size), piece] = part
                for part in weights:
                    sums[place] += dot(kept_ref[number], part)
        return tuple(sums)

    start = tuple(jnp.zeros((rows, step_columns), F32) for _ in columns)
    sums = lax.fori_loop(0, pieces // inside, one_round, start)
    return [(piece, end_sum(both)) for piece, both in zip(columns, sums)]


def kept_product(vector, high_ref, low_ref):
    both = jnp.concatenate(split2(4.0 * vector), axis=0)
    return end_sum(dot(both, high_ref[...]) + dot(both, low_ref[...]))


def build_kernel(me, every, right_ref, high_ref, low_ref, applied_out, left_ref, kept_ref):
    everything = flat(every)
    mine = every[me[0]]
    left_ref[...] = features(mine, True)
    right_ref[...] = features(everything, False).T
    keep_vector(lead_rows(everything, 3), kept_ref)
    ((_, product),) = made_product(right_ref, left_ref, kept_ref, 8, (high_ref, low_ref))
    applied = product + SHIFT * lead_rows(mine, 3)
    applied_out[...] = jnp.broadcast_to(applied[0:4][None], applied_out.shape)


def edge_kernel(right_ref, points, pair, out, left_ref, padded_ref, kept_ref):
    padded_ref[...] = jnp.zeros_like(padded_ref)
    padded_ref[4:7, :] = points[...]
    left_ref[...] = features(padded_ref[...], True)
    keep_vector(pair[...], kept_ref)
    for piece, product in made_product(right_ref, left_ref, kept_ref, 4):
        out[:, piece] = product


def lane_sum(value):
    return jnp.sum(value, axis=1, keepdims=True)


def ratio(top, bottom):
    row = lax.broadcasted_iota(jnp.int32, top.shape, 0)
    return jnp.where(row < 3, top / jnp.where(row < 3, bottom, 1.0), 0.0)


def own_part(ref, me, width):
    if width % 128 == 0:
        return ref[:, pl.ds(pl.multiple_of(me * width, 128), width)]
    lane = lax.broadcasted_iota(jnp.int32, (ref.shape[1], width), 0)
    column = lax.broadcasted_iota(jnp.int32, (ref.shape[1], width), 1)
    chosen = jnp.where(lane == me * width + column, 1.0, 0.0)
    return lax.dot_general(ref[...], chosen, PLAIN, precision=lax.Precision.HIGHEST, preferred_element_type=F32)


def turn_one_kernel(me, every, applied, high_ref, low_ref, applied_out, search_out, remain_out, numbers_out):
    width = every.shape[2]
    start = lead_rows(flat(every), 3)[0:4]
    got = flat(applied)
    norm = lane_sum(start * start)
    step = ratio(norm, lane_sum(start * got))
    remain = start - step * got
    following = lane_sum(remain * remain)
    search = remain + ratio(following, norm) * start
    search_out[...] = search
    remain_out[...] = remain
    numbers_out[0] = jnp.broadcast_to(step, numbers_out.shape[1:])
    numbers_out[1] = jnp.broadcast_to(following, numbers_out.shape[1:])
    product = kept_product(jnp.concatenate([search, jnp.zeros_like(search)], axis=0), high_ref, low_ref)
    product = product[0:4] + SHIFT * own_part(search_out, me[0], width)
    applied_out[...] = jnp.broadcast_to(product[None], applied_out.shape)


def turn_two_kernel(me, every, applied, search_in, remain_in, numbers, high_ref, low_ref, partial_out, pair_out, norm_out):
    width = every.shape[2]
    start = lead_rows(flat(every), 3)[0:4]
    got = flat(applied)
    search = search_in[...]
    norm = numbers[1][:, 0:1]
    step = ratio(norm, lane_sum(search * got))
    iterate = numbers[0][:, 0:1] * start + step * search
    remain = remain_in[...] - step * got
    following = lane_sum(remain * remain)
    search = remain + ratio(following, norm) * search
    pair = jnp.concatenate([search, iterate], axis=0)
    pair_out[...] = pair
    norm_out[...] = jnp.broadcast_to(following, norm_out.shape)
    product = kept_product(pair, high_ref, low_ref)
    mine = own_part(pair_out, me[0], width)[0:4]
    product = product[0:4] + SHIFT * mine
    partial_out[...] = jnp.broadcast_to(lane_sum(mine * product)[None], partial_out.shape)


def last_step(partials, norm):
    return ratio(norm[:, 0:1], jnp.sum(partials[...], axis=0)[:, 0:1])


def coefficients_kernel(me, partials, norm, pair, out):
    mine = own_part(pair, me[0], out.shape[1])
    out[...] = (mine[4:8] + last_step(partials, norm) * mine[0:4])[0:3]


def pick_kernel(send_list, partials, norm, motions, tiles_out, edge_ref):
    motion = motions[4:8, :] + last_step(partials, norm) * motions[0:4, :]
    for edge in range(edge_ref.shape[0]):
        edge_ref[edge] = motion[:, edge * S : (edge + 1) * S]
    group, capacity = send_list.shape
    for place in range(group):
        for position in range(0, capacity, 2):
            here = [
                edge_ref[jnp.maximum(send_list[place, number], 0)]
                for number in (position, min(position + 1, capacity - 1))
            ]
            tiles_out[place, 2 * position : 2 * position + 4, :] = jnp.concatenate(here, axis=1)


def blend(index):
    fraction = index.astype(F32) / (S - 1)
    return 1.0 - fraction, fraction


def six_products(left, right):
    lh, lm, ll = split3(left)
    rh, rm, rl = split3(right)
    lefts = jnp.concatenate([lh, lh, lm, lh, ll, lm], axis=0).astype(BF16)
    rights = jnp.concatenate([rh, rm, rh, rl, rh, rm], axis=0).astype(BF16)
    return dot(lefts, rights, LEFT_T)


def block_kernel(block_tiles, count, tiles, out, tile_ref, spread_ref, weight_ref):
    slot, coordinate = pl.program_id(0), pl.program_id(1)
    cells = S * S
    capacity = block_tiles.shape[0] * block_tiles.shape[1] // tiles.shape[0]

    @pl.when((slot == 0) & (coordinate == 0))
    def _():
        index = lax.broadcasted_iota(jnp.int32, (S, 2 * S), 0)
        lane = lax.broadcasted_iota(jnp.int32, (S, 2 * S), 1)
        half = jnp.where(lane < S, 0, 1)
        third = jnp.where(index == lane - S * half, 1.0, 0.0).astype(BF16)
        for first in range(0, cells, 2 * S):
            columns = slice(first, first + 2 * S)
            spread_ref[0:S, columns] = jnp.where(index - first // S == half, 1.0, 0.0).astype(BF16)
            spread_ref[S : 2 * S, columns] = third
        row = lax.broadcasted_iota(jnp.int32, (8, cells), 0)
        cell = lax.broadcasted_iota(jnp.int32, (8, cells), 1)
        j_low, j_high = blend(cell >> SHIFTS)
        k_low, k_high = blend(cell & (S - 1))
        j_weight = jnp.where(row & 1 == 0, j_low, j_high)
        k_weight = jnp.where(row < 2, k_low, k_high)
        weight_ref[0] = jnp.where(row < 4, j_weight * k_weight, 0.0)
        side = row & 2 == 0
        weight_ref[1] = jnp.where(row < 4, jnp.where(side, k_low, k_high), jnp.where(side, j_low, j_high))

    @pl.when((slot < count[0]) & (coordinate == 0))
    def _():
        for edge in range(12):
            place = block_tiles[slot, edge]
            source = lax.div(place, capacity)
            position = place - source * capacity
            group = lax.div(position, 2)
            pair = tiles[source, pl.ds(4 * group, 4), :]
            tile = jnp.where(position == 2 * group, pair[:, 0:S], pair[:, S : 2 * S])
            for row in range(3):
                tile_ref[row, edge : edge + 1, :] = tile[row : row + 1, :]

    @pl.when(slot < count[0])
    def _():
        along_low, along_high = blend(lax.broadcasted_iota(jnp.int32, (8, S), 1))
        row = lax.broadcasted_iota(jnp.int32, (8, S), 0)
        side = jnp.where(row & 1 == 0, along_low, along_high)
        first = tile_ref[coordinate, 0:8, :]
        straight = along_low * first[:, 0:1] + along_high * first[:, S - 1 : S]
        bent = jnp.where(row < 4, first - 2.0 * straight, 0.0)
        others = tile_ref[coordinate, 4:12, :]
        zero = jnp.zeros_like(others)
        placed = jnp.concatenate([jnp.where(row < 4, others, zero), jnp.where(row < 4, zero, others)], axis=1)
        spread = dot(jnp.concatenate(split3(placed), axis=0).astype(BF16), spread_ref[...])
        spread = (spread[0:8] + spread[8:16]) + spread[16:24]
        lefts = jnp.concatenate([bent, side], axis=0)
        rights = jnp.concatenate([weight_ref[0], spread * weight_ref[1]], axis=0)
        out[0, 0] = six_products(lefts, rights)

    @pl.when(slot >= count[0])
    def _():
        out[...] = jnp.zeros_like(out)


def call(kernel, name, outs, specs, scratch=(), megabytes=13, **more):
    shapes = tuple(jax.ShapeDtypeStruct(shape, dtype) for shape, dtype in outs)
    return pl.pallas_call(
        kernel,
        out_shape=shapes,
        in_specs=specs,
        scratch_shapes=scratch,
        compiler_params=pltpu.CompilerParams(vmem_limit_bytes=megabytes << 20),
        cost_estimate=pl.CostEstimate(flops=1, bytes_accessed=1, transcendentals=0),
        name=name,
        **{"out_specs": tuple(VMEM for _ in shapes), **more},
    )


def shards(total, center_points, displacements, edge_points, send_list, block_tiles, block_count):
    width = center_points.shape[1]
    extent = total * width
    edge_width = edge_points.shape[1]
    group, capacity = send_list.shape[1:]
    slots = block_tiles.shape[0]
    me = (lax.axis_index("gx") * lax.axis_size("gy") + lax.axis_index("gy")).reshape(1)

    def spread_out(copies, axes):
        return lax.all_to_all(copies, axes, split_axis=0, concat_axis=0, tiled=True)

    (packed,) = call(
        pack_kernel,
        "pack",
        [((total, 8, width), F32)],
        [ANY] * 2,
        [pltpu.VMEM((3, width), F32)] * 2 + [pltpu.SemaphoreType.DMA((2,))],
        LARGE,
    )(center_points, displacements)
    every = spread_out(packed, BOTH)
    matrix = ((extent, width), BF16)
    thin = ((total, 4, width), F32)
    size = math.gcd(extent, 512)
    kept = pltpu.VMEM((extent // size, 16, size), BF16)
    right, high, low, applied = call(
        build_kernel,
        "build",
        [((extent, 48), BF16), matrix, matrix, thin],
        [SMEM, VMEM],
        [pltpu.VMEM((48, width), BF16), kept],
    )(me, every)
    applied = spread_out(applied, BOTH)
    applied, search, remain, numbers = call(
        turn_one_kernel,
        "turn_one",
        [thin, ((4, extent), F32), ((4, extent), F32), ((2, 4, 128), F32)],
        [SMEM] + [VMEM] * 4,
    )(me, every, applied, high, low)
    applied = spread_out(applied, BOTH)
    partials, pair, norm = call(
        turn_two_kernel,
        "turn_two",
        [((total, 4, 128), F32), ((8, extent), F32), ((4, 128), F32)],
        [SMEM] + [VMEM] * 7,
    )(me, every, applied, search, remain, numbers, high, low)
    partials = spread_out(partials, BOTH)
    (motions,) = call(
        edge_kernel,
        "edges",
        [((8, edge_width), F32)],
        [VMEM] * 3,
        [pltpu.VMEM((48, edge_width), BF16), pltpu.VMEM((8, edge_width), F32), kept],
    )(right, edge_points, pair)
    (tiles,) = call(
        pick_kernel,
        "pick",
        [((group, (capacity + 1) // 2 * 4, 128), F32)],
        [SMEM] + [VMEM] * 3,
        [pltpu.VMEM((edge_width // S, 4, S), F32)],
    )(send_list[0], partials, norm, motions)
    tiles = spread_out(tiles, "gy")
    (coefficients,) = call(coefficients_kernel, "coefficients", [((3, width), F32)], [SMEM] + [VMEM] * 3)(
        me, partials, norm, pair
    )
    (block_motion,) = call(
        block_kernel,
        "blocks",
        [((slots, 3, S, S * S), F32)],
        [SMEM, SMEM, VMEM],
        [
            pltpu.VMEM((3, 12, S), F32),
            pltpu.VMEM((2 * S, S * S), BF16),
            pltpu.VMEM((2, 8, S * S), F32),
        ],
        grid=(slots, 3),
        out_specs=(pl.BlockSpec((1, 1, S, S * S), lambda slot, coordinate: (slot, coordinate, 0, 0)),),
    )(block_tiles, block_count, tiles)
    return coefficients, block_motion


def solution(mesh):
    total = mesh.shape["gx"] * mesh.shape["gy"]
    split = P(None, BOTH)
    return jax.shard_map(
        functools.partial(shards, total),
        mesh=mesh,
        in_specs=(split, split, split, P(BOTH, None, None), P(BOTH, None), P(BOTH)),
        out_specs=(split, P(BOTH, None, None, None)),
        check_vma=False,
    )
```

time: 126 us -> 88.2 us (0.70)
  local copies, waits for them, and re-layouts: 42.8 us -> 0.09 us
  blocking collectives: 0 us -> 20.4 us
  starting transfers between devices: 25.5 us -> 13.7 us
  Pallas kernels: 41.8 us -> 38.8 us
    unnamed x53 -> x7, local copies, waits for them, and re-layouts: 42.8 us -> 0.09 us
    all_to_all x0 -> x2, blocking collectives: none -> 20.4 us  [spread_out(): return lax.all_to_all(copies, axes, split_axis=0, concat_axis=0, tiled=True)]
    all_to_all x5 -> x3, starting transfers between devices: 25.5 us -> 13.7 us  [spread_out(): return lax.all_to_all(copies, axes, split_axis=0, concat_axis=0, tiled=True)]
    pallas_call x1, Pallas kernels: 6.53 us -> 5.12 us  [shards(): call(build_kernel, 'build', [((extent, 48), BF16), matrix, matrix, thin],...]
    pallas_call x11 -> x5, Pallas kernels: 30.7 us -> 29.8 us  [the longest x1 15.4 us: shards(): call(edge_kernel, 'edges', [((8, edge_width), F32)], [VMEM] * 3, [pltpu.V...]
    all_to_all x5 -> x3, waiting for transfers between devices: 14.4 us -> 14.3 us  [spread_out(): return lax.all_to_all(copies, axes, split_axis=0, concat_axis=0, tiled=True)]
  transfers between devices with their start and end apart: 5 -> 3, of which waited for: 2 -> 2; matrix products, arithmetic and copies ran while one was open for 1% -> 0% of each run, Pallas kernels for 17% -> 18%
where the time goes in v3:
time: 88.2 us; the launch traced here: 88.6 us
  Pallas kernels  38.8 us (44%)
  blocking collectives  20.4 us (23%)
  waiting for transfers between devices  14.3 us (16%)
  starting transfers between devices  13.7 us (16%)
  between operations  1.34 us (2%)
    all_to_all x2, blocking collectives, spread_out(): return lax.all_to_all(copies, axes, split_axis=0, concat_axis=0, tiled=True)  20.4 us
    pallas_call x1, Pallas kernels, shards(): call(edge_kernel, 'edges', [((8, edge_width), F32)], [VMEM] * 3, [pltpu.V...  15.4 us
    all_to_all x3, waiting for transfers between devices, spread_out(): return lax.all_to_all(copies, axes, split_axis=0, concat_axis=0, tiled=True)  14.3 us
    all_to_all x3, starting transfers between devices, spread_out(): return lax.all_to_all(copies, axes, split_axis=0, concat_axis=0, tiled=True)  13.7 us
    pallas_call x1, Pallas kernels, shards(): call(block_kernel, 'blocks', [((slots, 3, S, S * S), F32)], [SMEM, SMEM,...  10.7 us
    pallas_call x1, Pallas kernels, shards(): call(build_kernel, 'build', [((extent, 48), BF16), matrix, matrix, thin],...  5.12 us
    pallas_call x1, Pallas kernels, shards(): call(turn_two_kernel, 'turn_two', [((total, 4, 128), F32), ((8, extent),...  2.35 us
  transfers between devices with their start and end apart: 3, of which 2 were waited for; matrix products, arithmetic and copies ran while one was open for 0% of the time, Pallas kernels for 18%

profile of v3, /device:TPU:0, one launch (start us, length us, event | category | flops | bytes accessed | tf_op | source)
XLA Modules:
  0.0 88.6 jit_solution(11822521597686949901)
XLA Ops:
  0.6 1.5 %pack.1 = f32[32,8,256]{2,1,0:T(8,128)} custom-call(f32[3,256]{1,0:T(4,128)} %centers.1, f32[3,256]{1,0:T(4,128)} %shifts.1), custom_call_target="tpu_custom_call" | custom-call | flops 1 | bytes 1 | tf_op jit(solution)/shard_map/pack/pallas_call | solution.py:336
  2.1 7.3 %all-to-all-start = ((f32[32,8,256]{2,1,0:T(8,128)}), f32[32,8,256]{2,1,0:T(8,128)S(1)}, u32[]{:S(2)}, u32[]{:S(2)}) async-start(f32[32,8,256]{2,1,0:T(8,128)} %pack.1), calls=%async_computation | async-start | bytes 524288 | tf_op jit(solution)/shard_map/all_to_all | solution.py:334
  9.4 10.6 %all-to-all-done.every = f32[32,8,256]{2,1,0:T(8,128)S(1)} async-done(((f32[32,8,256]{2,1,0:T(8,128)}), f32[32,8,256]{2,1,0:T(8,128)S(1)}, u32[]{:S(2)}, u32[]{:S(2)}) %all-to-all-start) | async-done | bytes 262176 | tf_op jit(solution)/shard_map/all_to_all | solution.py:334
  20.0 5.1 %build.1 = (bf16[8192,48]{1,0:T(8,128)(2,1)S(1)}, bf16[8192,256]{1,0:T(8,128)(2,1)S(1)}, bf16[8192,256]{1,0:T(8,128)(2,1)S(1)}, f32[32,4,256]{2,1,0:T(4,128)S(1)}) custom-call(s32[1]{0:T(128)} %bitcast.me, f32[32,8,256]{2,1,0:T(8,128)S(1)} %all-to-all-done.every), custom_call_target="tpu_custom_call" | custom-call | flops 1 | bytes 1 | tf_op jit(solution)/shard_map/build/pallas_call | solution.py:349
  25.1 10.4 %all_to_all.25.applied = f32[32,4,256]{2,1,0:T(4,128)S(1)} all-to-all(f32[32,4,256]{2,1,0:T(4,128)S(1)} %get-tuple-element.13), channel_id=1, replica_groups=mesh['gx'=4,'gy'=8] {'gx','gy'}, dimensions={0} | all-to-all | bytes 262144 | tf_op jit(solution)/shard_map/all_to_all | solution.py:334
  35.6 1.5 %turn_one.1 = (f32[32,4,256]{2,1,0:T(4,128)S(1)}, f32[4,8192]{1,0:T(4,128)S(1)}, f32[4,8192]{1,0:T(4,128)S(1)}, f32[2,4,128]{2,1,0:T(4,128)S(1)}) custom-call(s32[1]{0:T(128)} %bitcast.me, f32[32,8,256]{2,1,0:T(8,128)S(1)} %all-to-all-done.every, f32[32,4,256]{2,1,0:T(4,128)S(1)} %all_to_all.25.applied, bf16[8192,256]{1,0:T(8,128)(2,1)S(1)} %get-tuple-element.14.high_ref, ...), custom_call_target="tpu_custom_call" | custom-call | flops 1 | bytes 1 | tf_op jit(solution)/shard_map/turn_one/pallas_call | solution.py:357
  37.1 10.0 %all_to_all.26.applied = f32[32,4,256]{2,1,0:T(4,128)S(1)} all-to-all(f32[32,4,256]{2,1,0:T(4,128)S(1)} %get-tuple-element.16), channel_id=1, replica_groups=mesh['gx'=4,'gy'=8] {'gx','gy'}, dimensions={0} | all-to-all | bytes 262144 | tf_op jit(solution)/shard_map/all_to_all | solution.py:334
  47.1 0.0 copy-start.2
  47.1 0.0 copy-start
  47.1 0.0 copy-start.1
  47.1 2.3 %turn_two.1 = (f32[32,4,128]{2,1,0:T(4,128)}, f32[8,8192]{1,0:T(8,128)S(1)}, f32[4,128]{1,0:T(4,128)S(1)}) custom-call(s32[1]{0:T(128)} %bitcast.me, f32[32,8,256]{2,1,0:T(8,128)S(1)} %all-to-all-done.every, f32[32,4,256]{2,1,0:T(4,128)S(1)} %all_to_all.26.applied, f32[4,8192]{1,0:T(4,128)S(1)} %get-tuple-element.17.search_in, ...), custom_call_target="tpu_custom_call" | custom-call | flops 1 | bytes 1 | tf_op jit(solution)/shard_map/turn_two/pallas_call | solution.py:364
  49.4 2.6 %all-to-all-start.3 = ((f32[32,4,128]{2,1,0:T(4,128)}), f32[32,4,128]{2,1,0:T(4,128)S(1)}, u32[]{:S(2)}, u32[]{:S(2)}) async-start(f32[32,4,128]{2,1,0:T(4,128)} %get-tuple-element.20), calls=%async_computation.3 | async-start | bytes 131072 | tf_op jit(solution)/shard_map/all_to_all | solution.py:334
  52.0 0.0 copy-done.2
  52.0 0.1 copy.8
  52.1 0.0 copy-done
  52.1 15.4 %edges.1.motions = f32[8,1024]{1,0:T(8,128)S(1)} custom-call(bf16[8192,48]{1,0:T(8,128)(2,1)S(1)} %get-tuple-element.23.right_ref, f32[3,1024]{1,0:T(4,128)S(1)} %copy-done, f32[8,8192]{1,0:T(8,128)S(1)} %get-tuple-element.22.pair), custom_call_target="tpu_custom_call" | custom-call | flops 1 | bytes 1 | tf_op jit(solution)/shard_map/edges/pallas_call | solution.py:371
  67.6 0.0 all-to-all-done.3.partials
  67.6 1.5 %pick.1 = f32[8,12,128]{2,1,0:T(8,128)} custom-call(s32[8,6]{1,0:T(8,128)S(1)} %bitcast.2, f32[32,4,128]{2,1,0:T(4,128)S(1)} %all-to-all-done.3.partials, f32[4,128]{1,0:T(4,128)S(1)} %get-tuple-element.21.norm, f32[8,1024]{1,0:T(8,128)S(1)} %edges.1.motions), custom_call_target="tpu_custom_call" | custom-call | flops 1 | bytes 1 | tf_op jit(solution)/shard_map/pick/pallas_call | solution.py:378
  69.1 3.8 %all-to-all-start.4 = ((f32[8,12,128]{2,1,0:T(8,128)}), f32[8,12,128]{2,1,0:T(8,128)S(1)}, u32[]{:S(2)}, u32[]{:S(2)}) async-start(f32[8,12,128]{2,1,0:T(8,128)} %pick.1), calls=%async_computation.4 | async-start | bytes 131072 | tf_op jit(solution)/shard_map/all_to_all | solution.py:334
  73.6 0.7 coefficients.1
  74.3 3.7 %all-to-all-done.4.tiles = f32[8,12,128]{2,1,0:T(8,128)S(1)} async-done(((f32[8,12,128]{2,1,0:T(8,128)}), f32[8,12,128]{2,1,0:T(8,128)S(1)}, u32[]{:S(2)}, u32[]{:S(2)}) %all-to-all-start.4) | async-done | bytes 49184 | tf_op jit(solution)/shard_map/all_to_all | solution.py:334
  78.0 0.0 copy-done.1
  78.0 10.7 %blocks.1 = f32[4,3,64,4096]{3,2,1,0:T(8,128)} custom-call(s32[4,12]{1,0:T(4,128)S(1)} %copy-done.1, s32[1]{0:T(128)S(6)} %copy.9.count, f32[8,12,128]{2,1,0:T(8,128)S(1)} %all-to-all-done.4.tiles), custom_call_target="tpu_custom_call" | custom-call | flops 1 | bytes 1 | tf_op jit(solution)/shard_map/blocks/pallas_call | solution.py:389
Async XLA Ops:
  2.1 17.9 %all-to-all-start = ((f32[32,8,256]{2,1,0:T(8,128)}), f32[32,8,256]{2,1,0:T(8,128)S(1)}, u32[]{:S(2)}, u32[]{:S(2)}) async-start(f32[32,8,256]{2,1,0:T(8,128)} %pack.1), calls=%async_computation | async-start | bytes 524288 | tf_op jit(solution)/shard_map/all_to_all | solution.py:334
  47.1 4.9 %copy-start.2 = (s32[1,8,6]{1,0,2:T(1,128)S(1)}, s32[1,8,6]{1,0,2:T(1,128)}, u32[]{:S(2)}) copy-start(s32[1,8,6]{1,0,2:T(1,128)} %param.9) | copy-start | bytes 580
  47.1 5.0 %copy-start = (f32[3,1024]{1,0:T(4,128)S(1)}, f32[3,1024]{1,0:T(4,128)}, u32[]{:S(2)}) copy-start(f32[3,1024]{1,0:T(4,128)} %points.1) | copy-start | bytes 36868
  47.1 30.9 %copy-start.1 = (s32[4,12]{1,0:T(4,128)S(1)}, s32[4,12]{1,0:T(4,128)}, u32[]{:S(2)}) copy-start(s32[4,12]{1,0:T(4,128)} %block_tiles.1) | copy-start | bytes 580
  49.4 18.1 %all-to-all-start.3 = ((f32[32,4,128]{2,1,0:T(4,128)}), f32[32,4,128]{2,1,0:T(4,128)S(1)}, u32[]{:S(2)}, u32[]{:S(2)}) async-start(f32[32,4,128]{2,1,0:T(4,128)} %get-tuple-element.20), calls=%async_computation.3 | async-start | bytes 131072 | tf_op jit(solution)/shard_map/all_to_all | solution.py:334
  69.1 8.9 %all-to-all-start.4 = ((f32[8,12,128]{2,1,0:T(8,128)}), f32[8,12,128]{2,1,0:T(8,128)S(1)}, u32[]{:S(2)}, u32[]{:S(2)}) async-start(f32[8,12,128]{2,1,0:T(8,128)} %pick.1), calls=%async_computation.4 | async-start | bytes 131072 | tf_op jit(solution)/shard_map/all_to_all | solution.py:334

commit v4 on v3

--- a/solution.py
+++ b/solution.py
@@ -67,6 +67,21 @@
     return (remain2 * remain2) * (1.25 - remain)
 
 
+def write_copies(rows, out, first=0):
+    width = rows.shape[1]
+    for number in range(3):
+        place = (first + number) * width
+        out[:, :, place : place + width] = jnp.broadcast_to(rows[number : number + 1][None], (out.shape[0], 1, width))
+
+
+def read_copies(ref, width, first=0):
+    rows = []
+    for number in range(3):
+        place = (first + number) * width
+        rows.append(jnp.concatenate([ref[part, :, place : place + width] for part in range(ref.shape[0])], axis=1))
+    return jnp.concatenate(rows + [jnp.zeros_like(rows[0])], axis=0)
+
+
 def pack_kernel(centers, shifts, out, centers_ref, shifts_ref, done):
     copies = [
         pltpu.make_async_copy(centers, centers_ref, done.at[0]),
@@ -74,20 +89,10 @@
     ]
     for copy in copies:
         copy.start()
-    out[...] = jnp.zeros_like(out)
     for copy in copies:
         copy.wait()
-    out[:, 0:3, :] = jnp.broadcast_to(shifts_ref[...][None], (out.shape[0],) + shifts.shape)
-    out[:, 4:7, :] = jnp.broadcast_to(centers_ref[...][None], (out.shape[0],) + centers.shape)
-
-
-def lead_rows(value, count):
-    row = lax.broadcasted_iota(jnp.int32, value.shape, value.ndim - 2)
-    return jnp.where(row < count, value, 0.0)
-
-
-def flat(ref):
-    return jnp.concatenate([ref[part] for part in range(ref.shape[0])], axis=1)
+    write_copies(shifts_ref[...], out)
+    write_copies(centers_ref[...], out, 3)
 
 
 def whole_slice(number, size):
@@ -137,15 +142,18 @@
     return end_sum(dot(both, high_ref[...]) + dot(both, low_ref[...]))
 
 
-def build_kernel(me, every, right_ref, high_ref, low_ref, applied_out, left_ref, kept_ref):
-    everything = flat(every)
-    mine = every[me[0]]
+def build_kernel(me, packed, every_out, right_ref, high_ref, low_ref, applied_out, left_ref, kept_ref):
+    width = left_ref.shape[1]
+    shifts = read_copies(packed, width)
+    centers = read_copies(packed, width, 3)
+    every_out[0:4, :] = shifts
+    every_out[4:8, :] = centers
+    mine = own_part(every_out, me[0], width)
     left_ref[...] = features(mine, True)
-    right_ref[...] = features(everything, False).T
-    keep_vector(lead_rows(everything, 3), kept_ref)
+    right_ref[...] = features(every_out[...], False).T
+    keep_vector(jnp.concatenate([shifts, jnp.zeros_like(shifts)], axis=0), kept_ref)
     ((_, product),) = made_product(right_ref, left_ref, kept_ref, 8, (high_ref, low_ref))
-    applied = product + SHIFT * lead_rows(mine, 3)
-    applied_out[...] = jnp.broadcast_to(applied[0:4][None], applied_out.shape)
+    write_copies(product[0:4] + SHIFT * mine[0:4], applied_out)
 
 
 def edge_kernel(right_ref, points, pair, out, left_ref, padded_ref, kept_ref):
@@ -176,9 +184,9 @@
 
 
 def turn_one_kernel(me, every, applied, high_ref, low_ref, applied_out, search_out, remain_out, numbers_out):
-    width = every.shape[2]
-    start = lead_rows(flat(every), 3)[0:4]
-    got = flat(applied)
+    width = high_ref.shape[1]
+    start = every[0:4, :]
+    got = read_copies(applied, width)
     norm = lane_sum(start * start)
     step = ratio(norm, lane_sum(start * got))
     remain = start - step * got
@@ -189,14 +197,13 @@
     numbers_out[0] = jnp.broadcast_to(step, numbers_out.shape[1:])
     numbers_out[1] = jnp.broadcast_to(following, numbers_out.shape[1:])
     product = kept_product(jnp.concatenate([search, jnp.zeros_like(search)], axis=0), high_ref, low_ref)
-    product = product[0:4] + SHIFT * own_part(search_out, me[0], width)
-    applied_out[...] = jnp.broadcast_to(product[None], applied_out.shape)
+    write_copies(product[0:4] + SHIFT * own_part(search_out, me[0], width), applied_out)
 
 
 def turn_two_kernel(me, every, applied, search_in, remain_in, numbers, high_ref, low_ref, partial_out, pair_out, norm_out):
-    width = every.shape[2]
-    start = lead_rows(flat(every), 3)[0:4]
-    got = flat(applied)
+    width = high_ref.shape[1]
+    start = every[0:4, :]
+    got = read_copies(applied, width)
     search = search_in[...]
     norm = numbers[1][:, 0:1]
     step = ratio(norm, lane_sum(search * got))
@@ -241,41 +248,54 @@
     return 1.0 - fraction, fraction
 
 
-def six_products(left, right):
-    lh, lm, ll = split3(left)
-    rh, rm, rl = split3(right)
-    lefts = jnp.concatenate([lh, lh, lm, lh, ll, lm], axis=0).astype(BF16)
-    rights = jnp.concatenate([rh, rm, rh, rl, rh, rm], axis=0).astype(BF16)
+def three_products(left, right):
+    left_high, left_low = split2(left)
+    right_high, right_low = split2(right)
+    lefts = jnp.concatenate([left_high, left_high, left_low], axis=0)
+    rights = jnp.concatenate([right_high, right_low, right_high], axis=0)
     return dot(lefts, rights, LEFT_T)
 
 
-def block_kernel(block_tiles, count, tiles, out, tile_ref, spread_ref, weight_ref):
-    slot, coordinate = pl.program_id(0), pl.program_id(1)
+def block_kernel(block_tiles, count, tiles, out, tile_ref, spread_ref, weight_ref, held_ref, done):
+    slots = out.shape[0]
     cells = S * S
     capacity = block_tiles.shape[0] * block_tiles.shape[1] // tiles.shape[0]
-
-    @pl.when((slot == 0) & (coordinate == 0))
-    def _():
-        index = lax.broadcasted_iota(jnp.int32, (S, 2 * S), 0)
-        lane = lax.broadcasted_iota(jnp.int32, (S, 2 * S), 1)
-        half = jnp.where(lane < S, 0, 1)
-        third = jnp.where(index == lane - S * half, 1.0, 0.0).astype(BF16)
-        for first in range(0, cells, 2 * S):
-            columns = slice(first, first + 2 * S)
-            spread_ref[0:S, columns] = jnp.where(index - first // S == half, 1.0, 0.0).astype(BF16)
-            spread_ref[S : 2 * S, columns] = third
-        row = lax.broadcasted_iota(jnp.int32, (8, cells), 0)
-        cell = lax.broadcasted_iota(jnp.int32, (8, cells), 1)
-        j_low, j_high = blend(cell >> SHIFTS)
-        k_low, k_high = blend(cell & (S - 1))
-        j_weight = jnp.where(row & 1 == 0, j_low, j_high)
-        k_weight = jnp.where(row < 2, k_low, k_high)
-        weight_ref[0] = jnp.where(row < 4, j_weight * k_weight, 0.0)
-        side = row & 2 == 0
-        weight_ref[1] = jnp.where(row < 4, jnp.where(side, k_low, k_high), jnp.where(side, j_low, j_high))
-
-    @pl.when((slot < count[0]) & (coordinate == 0))
-    def _():
+    halves = done.shape[2]
+
+    def copies(slot, coordinate):
+        rows = S // halves
+        return [
+            pltpu.make_async_copy(
+                held_ref.at[slot, coordinate, pl.ds(half * rows, rows), :],
+                out.at[slot, coordinate, pl.ds(half * rows, rows), :],
+                done.at[slot, coordinate, half],
+            )
+            for half in range(halves)
+        ]
+
+    index = lax.broadcasted_iota(jnp.int32, (S, 2 * S), 0)
+    lane = lax.broadcasted_iota(jnp.int32, (S, 2 * S), 1)
+    half = jnp.where(lane < S, 0, 1)
+    third = jnp.where(index == lane - S * half, 1.0, 0.0).astype(BF16)
+    for first in range(0, cells, 2 * S):
+        columns = slice(first, first + 2 * S)
+        spread_ref[0:S, columns] = jnp.where(index - first // S == half, 1.0, 0.0).astype(BF16)
+        spread_ref[S : 2 * S, columns] = third
+    row = lax.broadcasted_iota(jnp.int32, (8, cells), 0)
+    cell = lax.broadcasted_iota(jnp.int32, (8, cells), 1)
+    j_low, j_high = blend(cell >> SHIFTS)
+    k_low, k_high = blend(cell & (S - 1))
+    j_weight = jnp.where(row & 1 == 0, j_low, j_high)
+    k_weight = jnp.where(row < 2, k_low, k_high)
+    weight_ref[0] = jnp.where(row < 4, j_weight * k_weight, 0.0)
+    lower = row & 2 == 0
+    weight_ref[1] = jnp.where(row < 4, jnp.where(lower, k_low, k_high), jnp.where(lower, j_low, j_high))
+
+    along_low, along_high = blend(lax.broadcasted_iota(jnp.int32, (8, S), 1))
+    row = lax.broadcasted_iota(jnp.int32, (8, S), 0)
+    side = jnp.where(row & 1 == 0, along_low, along_high)
+
+    def fill(slot, carry):
         for edge in range(12):
             place = block_tiles[slot, edge]
             source = lax.div(place, capacity)
@@ -283,29 +303,36 @@
             group = lax.div(position, 2)
             pair = tiles[source, pl.ds(4 * group, 4), :]
             tile = jnp.where(position == 2 * group, pair[:, 0:S], pair[:, S : 2 * S])
-            for row in range(3):
-                tile_ref[row, edge : edge + 1, :] = tile[row : row + 1, :]
-
-    @pl.when(slot < count[0])
-    def _():
-        along_low, along_high = blend(lax.broadcasted_iota(jnp.int32, (8, S), 1))
-        row = lax.broadcasted_iota(jnp.int32, (8, S), 0)
-        side = jnp.where(row & 1 == 0, along_low, along_high)
-        first = tile_ref[coordinate, 0:8, :]
-        straight = along_low * first[:, 0:1] + along_high * first[:, S - 1 : S]
-        bent = jnp.where(row < 4, first - 2.0 * straight, 0.0)
-        others = tile_ref[coordinate, 4:12, :]
-        zero = jnp.zeros_like(others)
-        placed = jnp.concatenate([jnp.where(row < 4, others, zero), jnp.where(row < 4, zero, others)], axis=1)
-        spread = dot(jnp.concatenate(split3(placed), axis=0).astype(BF16), spread_ref[...])
-        spread = (spread[0:8] + spread[8:16]) + spread[16:24]
-        lefts = jnp.concatenate([bent, side], axis=0)
-        rights = jnp.concatenate([weight_ref[0], spread * weight_ref[1]], axis=0)
-        out[0, 0] = six_products(lefts, rights)
-
-    @pl.when(slot >= count[0])
-    def _():
-        out[...] = jnp.zeros_like(out)
+            for coordinate in range(3):
+                tile_ref[coordinate, edge : edge + 1, :] = tile[coordinate : coordinate + 1, :]
+        for coordinate in range(3):
+            first = tile_ref[coordinate, 0:8, :]
+            straight = along_low * first[:, 0:1] + along_high * first[:, S - 1 : S]
+            bent = jnp.where(row < 4, first - 2.0 * straight, 0.0)
+            others = tile_ref[coordinate, 4:12, :]
+            zero = jnp.zeros_like(others)
+            placed = jnp.concatenate([jnp.where(row < 4, others, zero), jnp.where(row < 4, zero, others)], axis=1)
+            spread = end_sum(dot(jnp.concatenate(split2(placed), axis=0), spread_ref[...]))
+            lefts = jnp.concatenate([bent, side], axis=0)
+            rights = jnp.concatenate([weight_ref[0], spread * weight_ref[1]], axis=0)
+            held_ref[slot, coordinate] = three_products(lefts, rights)
+            for copy in copies(slot, coordinate):
+                copy.start()
+        return carry
+
+    def clear(slot, carry):
+        held_ref[slot] = jnp.zeros_like(held_ref[slot])
+        for coordinate in range(3):
+            for copy in copies(slot, coordinate):
+                copy.start()
+        return carry
+
+    lax.fori_loop(0, count[0], fill, 0)
+    lax.fori_loop(count[0], slots, clear, 0)
+    for slot in range(slots):
+        for coordinate in range(3):
+            for copy in copies(slot, coordinate):
+                copy.wait()
 
 
 def call(kernel, name, outs, specs, scratch=(), megabytes=13, **more):
@@ -336,23 +363,23 @@
     (packed,) = call(
         pack_kernel,
         "pack",
-        [((total, 8, width), F32)],
+        [((total, 1, 6 * width), F32)],
         [ANY] * 2,
         [pltpu.VMEM((3, width), F32)] * 2 + [pltpu.SemaphoreType.DMA((2,))],
         LARGE,
     )(center_points, displacements)
-    every = spread_out(packed, BOTH)
+    packed = spread_out(packed, BOTH)
     matrix = ((extent, width), BF16)
-    thin = ((total, 4, width), F32)
+    thin = ((total, 1, 3 * width), F32)
     size = math.gcd(extent, 512)
     kept = pltpu.VMEM((extent // size, 16, size), BF16)
-    right, high, low, applied = call(
+    every, right, high, low, applied = call(
         build_kernel,
         "build",
-        [((extent, 48), BF16), matrix, matrix, thin],
+        [((8, extent), F32), ((extent, 48), BF16), matrix, matrix, thin],
         [SMEM, VMEM],
         [pltpu.VMEM((48, width), BF16), kept],
-    )(me, every)
+    )(me, packed)
     applied = spread_out(applied, BOTH)
     applied, search, remain, numbers = call(
         turn_one_kernel,
@@ -395,9 +422,11 @@
             pltpu.VMEM((3, 12, S), F32),
             pltpu.VMEM((2 * S, S * S), BF16),
             pltpu.VMEM((2, 8, S * S), F32),
+            pltpu.VMEM((slots, 3, S, S * S), F32),
+            pltpu.SemaphoreType.DMA((slots, 3, 2)),
         ],
-        grid=(slots, 3),
-        out_specs=(pl.BlockSpec((1, 1, S, S * S), lambda slot, coordinate: (slot, coordinate, 0, 0)),),
+        24,
+        out_specs=(ANY,),
     )(block_tiles, block_count, tiles)
     return coefficients, block_motion
 

time: 88.2 us -> 82.5 us (0.935); the launches traced: 88.6 us -> 82 us
  Pallas kernels: 38.8 us -> 34.4 us
  waiting for transfers between devices: 14.3 us -> 12.5 us
    pallas_call x1, Pallas kernels: 10.7 us -> 6.13 us  [shards(): call(block_kernel, 'blocks', [((slots, 3, S, S * S), F32)], [SMEM, SMEM,...]
    all_to_all x3, waiting for transfers between devices: 14.3 us -> 12.5 us  [spread_out(): return lax.all_to_all(copies, axes, split_axis=0, concat_axis=0, tiled=True)]
  transfers between devices with their start and end apart: 3 -> 3, of which waited for: 2 -> 2; matrix products, arithmetic and copies ran while one was open for 0% -> 0% of each run, Pallas kernels for 18% -> 20%
where the time goes in v4:
time: 82.5 us; the launch traced here: 82 us
  Pallas kernels  34.4 us (42%)
  blocking collectives  19.8 us (24%)
  starting transfers between devices  13.7 us (17%)
  waiting for transfers between devices  12.5 us (15%)
  between operations  1.34 us (2%)
    all_to_all x2, blocking collectives, spread_out(): return lax.all_to_all(copies, axes, split_axis=0, concat_axis=0, tiled=True)  19.8 us
    pallas_call x1, Pallas kernels, shards(): call(edge_kernel, 'edges', [((8, edge_width), F32)], [VMEM] * 3, [pltpu.V...  15.5 us
    all_to_all x3, starting transfers between devices, spread_out(): return lax.all_to_all(copies, axes, split_axis=0, concat_axis=0, tiled=True)  13.7 us
    all_to_all x3, waiting for transfers between devices, spread_out(): return lax.all_to_all(copies, axes, split_axis=0, concat_axis=0, tiled=True)  12.5 us
    pallas_call x1, Pallas kernels, shards(): call(block_kernel, 'blocks', [((slots, 3, S, S * S), F32)], [SMEM, SMEM,...  6.13 us
    pallas_call x1, Pallas kernels, shards(): call(build_kernel, 'build', [((8, extent), F32), ((extent, 48), BF16), ma...  5.22 us
    pallas_call x1, Pallas kernels, shards(): call(turn_two_kernel, 'turn_two', [((total, 4, 128), F32), ((8, extent),...  2.4 us
  transfers between devices with their start and end apart: 3, of which 2 were waited for; matrix products, arithmetic and copies ran while one was open for 0% of the time, Pallas kernels for 20%

profile of v4, /device:TPU:0, one launch (start us, length us, event | category | flops | bytes accessed | tf_op | source)
XLA Modules:
  0.0 82.0 jit_solution(9020183171128173387)
XLA Ops:
  0.6 1.5 %pack.1 = f32[32,1,1536]{2,1,0:T(1,128)} custom-call(f32[3,256]{1,0:T(4,128)} %centers.1, f32[3,256]{1,0:T(4,128)} %shifts.1), custom_call_target="tpu_custom_call" | custom-call | flops 1 | bytes 1 | tf_op jit(solution)/shard_map/pack/pallas_call | solution.py:363
  2.1 7.3 %all-to-all-start = ((f32[32,1,1536]{2,1,0:T(1,128)}), f32[32,1,1536]{2,1,0:T(1,128)S(1)}, u32[]{:S(2)}, u32[]{:S(2)}) async-start(f32[32,1,1536]{2,1,0:T(1,128)} %pack.1), calls=%async_computation | async-start | bytes 393216 | tf_op jit(solution)/shard_map/all_to_all | solution.py:361
  9.4 8.9 %all-to-all-done.packed = f32[32,1,1536]{2,1,0:T(1,128)S(1)} async-done(((f32[32,1,1536]{2,1,0:T(1,128)}), f32[32,1,1536]{2,1,0:T(1,128)S(1)}, u32[]{:S(2)}, u32[]{:S(2)}) %all-to-all-start) | async-done | bytes 196640 | tf_op jit(solution)/shard_map/all_to_all | solution.py:361
  18.3 5.2 %build.1 = (f32[8,8192]{1,0:T(8,128)S(1)}, bf16[8192,48]{1,0:T(8,128)(2,1)S(1)}, bf16[8192,256]{1,0:T(8,128)(2,1)S(1)}, bf16[8192,256]{1,0:T(8,128)(2,1)S(1)}, f32[32,1,768]{2,1,0:T(1,128)S(1)}) custom-call(s32[1]{0:T(128)} %bitcast.me, f32[32,1,1536]{2,1,0:T(1,128)S(1)} %all-to-all-done.packed), custom_call_target="tpu_custom_call" | custom-call | flops 1 | bytes 1 | tf_op jit(solution)/shard_map/build/pallas_call | solution.py:376
  23.5 10.3 %all_to_all.25.applied = f32[32,1,768]{2,1,0:T(1,128)S(1)} all-to-all(f32[32,1,768]{2,1,0:T(1,128)S(1)} %get-tuple-element.15), channel_id=1, replica_groups=mesh['gx'=4,'gy'=8] {'gx','gy'}, dimensions={0} | all-to-all | bytes 196608 | tf_op jit(solution)/shard_map/all_to_all | solution.py:361
  33.8 1.6 %turn_one.1 = (f32[32,1,768]{2,1,0:T(1,128)S(1)}, f32[4,8192]{1,0:T(4,128)S(1)}, f32[4,8192]{1,0:T(4,128)S(1)}, f32[2,4,128]{2,1,0:T(4,128)S(1)}) custom-call(s32[1]{0:T(128)} %bitcast.me, f32[8,8192]{1,0:T(8,128)S(1)} %get-tuple-element.14.every, f32[32,1,768]{2,1,0:T(1,128)S(1)} %all_to_all.25.applied, bf16[8192,256]{1,0:T(8,128)(2,1)S(1)} %get-tuple-element.16.high_ref, ...), custom_call_target="tpu_custom_call" | custom-call | flops 1 | bytes 1 | tf_op jit(solution)/shard_map/turn_one/pallas_call | solution.py:384
  35.4 9.5 %all_to_all.26.applied = f32[32,1,768]{2,1,0:T(1,128)S(1)} all-to-all(f32[32,1,768]{2,1,0:T(1,128)S(1)} %get-tuple-element.18), channel_id=1, replica_groups=mesh['gx'=4,'gy'=8] {'gx','gy'}, dimensions={0} | all-to-all | bytes 196608 | tf_op jit(solution)/shard_map/all_to_all | solution.py:361
  44.9 0.0 copy-start.2
  44.9 0.0 copy-start
  44.9 0.0 copy-start.1
  44.9 2.4 %turn_two.1 = (f32[32,4,128]{2,1,0:T(4,128)}, f32[8,8192]{1,0:T(8,128)S(1)}, f32[4,128]{1,0:T(4,128)S(1)}) custom-call(s32[1]{0:T(128)} %bitcast.me, f32[8,8192]{1,0:T(8,128)S(1)} %get-tuple-element.14.every, f32[32,1,768]{2,1,0:T(1,128)S(1)} %all_to_all.26.applied, f32[4,8192]{1,0:T(4,128)S(1)} %get-tuple-element.19.search_in, ...), custom_call_target="tpu_custom_call" | custom-call | flops 1 | bytes 1 | tf_op jit(solution)/shard_map/turn_two/pallas_call | solution.py:391
  47.3 2.6 %all-to-all-start.3 = ((f32[32,4,128]{2,1,0:T(4,128)}), f32[32,4,128]{2,1,0:T(4,128)S(1)}, u32[]{:S(2)}, u32[]{:S(2)}) async-start(f32[32,4,128]{2,1,0:T(4,128)} %get-tuple-element.22), calls=%async_computation.3 | async-start | bytes 131072 | tf_op jit(solution)/shard_map/all_to_all | solution.py:361
  49.9 0.0 copy-done.2
  49.9 0.1 copy.8
  50.0 0.0 copy-done
  50.0 15.5 %edges.1.motions = f32[8,1024]{1,0:T(8,128)S(1)} custom-call(bf16[8192,48]{1,0:T(8,128)(2,1)S(1)} %get-tuple-element.25.right_ref, f32[3,1024]{1,0:T(4,128)S(1)} %copy-done, f32[8,8192]{1,0:T(8,128)S(1)} %get-tuple-element.24.pair), custom_call_target="tpu_custom_call" | custom-call | flops 1 | bytes 1 | tf_op jit(solution)/shard_map/edges/pallas_call | solution.py:398
  65.5 0.0 all-to-all-done.3.partials
  65.5 1.5 %pick.1 = f32[8,12,128]{2,1,0:T(8,128)} custom-call(s32[8,6]{1,0:T(8,128)S(1)} %bitcast.2, f32[32,4,128]{2,1,0:T(4,128)S(1)} %all-to-all-done.3.partials, f32[4,128]{1,0:T(4,128)S(1)} %get-tuple-element.23.norm, f32[8,1024]{1,0:T(8,128)S(1)} %edges.1.motions), custom_call_target="tpu_custom_call" | custom-call | flops 1 | bytes 1 | tf_op jit(solution)/shard_map/pick/pallas_call | solution.py:405
  67.0 3.8 %all-to-all-start.4 = ((f32[8,12,128]{2,1,0:T(8,128)}), f32[8,12,128]{2,1,0:T(8,128)S(1)}, u32[]{:S(2)}, u32[]{:S(2)}) async-start(f32[8,12,128]{2,1,0:T(8,128)} %pick.1), calls=%async_computation.4 | async-start | bytes 131072 | tf_op jit(solution)/shard_map/all_to_all | solution.py:361
  71.5 0.7 coefficients.1
  72.2 3.7 %all-to-all-done.4.tiles = f32[8,12,128]{2,1,0:T(8,128)S(1)} async-done(((f32[8,12,128]{2,1,0:T(8,128)}), f32[8,12,128]{2,1,0:T(8,128)S(1)}, u32[]{:S(2)}, u32[]{:S(2)}) %all-to-all-start.4) | async-done | bytes 49184 | tf_op jit(solution)/shard_map/all_to_all | solution.py:361
  75.8 0.0 copy-done.1
  75.8 6.1 %blocks.1 = f32[4,3,64,4096]{3,2,1,0:T(8,128)} custom-call(s32[4,12]{1,0:T(4,128)S(1)} %copy-done.1, s32[1]{0:T(128)S(6)} %copy.9.count, f32[8,12,128]{2,1,0:T(8,128)S(1)} %all-to-all-done.4.tiles), custom_call_target="tpu_custom_call" | custom-call | flops 1 | bytes 1 | tf_op jit(solution)/shard_map/blocks/pallas_call | solution.py:416
Async XLA Ops:
  2.1 16.2 %all-to-all-start = ((f32[32,1,1536]{2,1,0:T(1,128)}), f32[32,1,1536]{2,1,0:T(1,128)S(1)}, u32[]{:S(2)}, u32[]{:S(2)}) async-start(f32[32,1,1536]{2,1,0:T(1,128)} %pack.1), calls=%async_computation | async-start | bytes 393216 | tf_op jit(solution)/shard_map/all_to_all | solution.py:361
  44.9 5.0 %copy-start.2 = (s32[1,8,6]{1,0,2:T(1,128)S(1)}, s32[1,8,6]{1,0,2:T(1,128)}, u32[]{:S(2)}) copy-start(s32[1,8,6]{1,0,2:T(1,128)} %param.9) | copy-start | bytes 580
  44.9 5.1 %copy-start = (f32[3,1024]{1,0:T(4,128)S(1)}, f32[3,1024]{1,0:T(4,128)}, u32[]{:S(2)}) copy-start(f32[3,1024]{1,0:T(4,128)} %points.1) | copy-start | bytes 36868
  44.9 30.9 %copy-start.1 = (s32[4,12]{1,0:T(4,128)S(1)}, s32[4,12]{1,0:T(4,128)}, u32[]{:S(2)}) copy-start(s32[4,12]{1,0:T(4,128)} %block_tiles.1) | copy-start | bytes 580
  47.3 18.1 %all-to-all-start.3 = ((f32[32,4,128]{2,1,0:T(4,128)}), f32[32,4,128]{2,1,0:T(4,128)S(1)}, u32[]{:S(2)}, u32[]{:S(2)}) async-start(f32[32,4,128]{2,1,0:T(4,128)} %get-tuple-element.22), calls=%async_computation.3 | async-start | bytes 131072 | tf_op jit(solution)/shard_map/all_to_all | solution.py:361
  67.0 8.9 %all-to-all-start.4 = ((f32[8,12,128]{2,1,0:T(8,128)}), f32[8,12,128]{2,1,0:T(8,128)S(1)}, u32[]{:S(2)}, u32[]{:S(2)}) async-start(f32[8,12,128]{2,1,0:T(8,128)} %pick.1), calls=%async_computation.4 | async-start | bytes 131072 | tf_op jit(solution)/shard_map/all_to_all | solution.py:361

commit v5 on v4

--- a/solution.py
+++ b/solution.py
@@ -62,7 +62,8 @@
 
 def quarter_phi(squared):
     squared = jnp.maximum(squared, TINY)
-    remain = jnp.maximum(1.0 - squared * lax.rsqrt(squared), 0.0)
+    radial = pltpu.reciprocal(lax.rsqrt(squared), approx=True)
+    remain = jnp.maximum(1.0 - radial, 0.0)
     remain2 = remain * remain
     return (remain2 * remain2) * (1.25 - remain)
 
@@ -142,7 +143,7 @@
     return end_sum(dot(both, high_ref[...]) + dot(both, low_ref[...]))
 
 
-def build_kernel(me, packed, every_out, right_ref, high_ref, low_ref, applied_out, left_ref, kept_ref):
+def build_kernel(me, packed, tables, wanted, every_out, right_ref, high_ref, low_ref, applied_out, left_ref, kept_ref):
     width = left_ref.shape[1]
     shifts = read_copies(packed, width)
     centers = read_copies(packed, width, 3)
@@ -217,16 +218,21 @@
     product = kept_product(pair, high_ref, low_ref)
     mine = own_part(pair_out, me[0], width)[0:4]
     product = product[0:4] + SHIFT * mine
-    partial_out[...] = jnp.broadcast_to(lane_sum(mine * product)[None], partial_out.shape)
+    partial = lane_sum(mine * product)
+    lane = lax.broadcasted_iota(jnp.int32, (1, partial_out.shape[2]), 1)
+    row = jnp.zeros(lane.shape, F32)
+    for number in range(3):
+        row = jnp.where(lane == number, partial[number : number + 1], row)
+    partial_out[...] = jnp.broadcast_to(row[None], partial_out.shape)
 
 
 def last_step(partials, norm):
-    return ratio(norm[:, 0:1], jnp.sum(partials[...], axis=0)[:, 0:1])
-
-
-def coefficients_kernel(me, partials, norm, pair, out):
-    mine = own_part(pair, me[0], out.shape[1])
-    out[...] = (mine[4:8] + last_step(partials, norm) * mine[0:4])[0:3]
+    row = jnp.sum(partials[...], axis=0)
+    number = lax.broadcasted_iota(jnp.int32, (4, 1), 0)
+    total = jnp.ones((4, 1), F32)
+    for coordinate in range(3):
+        total = jnp.where(number == coordinate, row[:, coordinate : coordinate + 1], total)
+    return ratio(norm[:, 0:1], total)
 
 
 def pick_kernel(send_list, partials, norm, motions, tiles_out, edge_ref):
@@ -256,10 +262,12 @@
     return dot(lefts, rights, LEFT_T)
 
 
-def block_kernel(block_tiles, count, tiles, out, tile_ref, spread_ref, weight_ref, held_ref, done):
+def block_kernel(me, tables, tiles, partials, norm, pair, out, coefficients_out, *scratch):
+    tile_ref, spread_ref, weight_ref, held_ref, coefficients_ref, done, coefficients_done = scratch
     slots = out.shape[0]
     cells = S * S
-    capacity = block_tiles.shape[0] * block_tiles.shape[1] // tiles.shape[0]
+    capacity = slots * 12 // tiles.shape[0]
+    live = tables[0, 12]
     halves = done.shape[2]
 
     def copies(slot, coordinate):
@@ -297,7 +305,7 @@
 
     def fill(slot, carry):
         for edge in range(12):
-            place = block_tiles[slot, edge]
+            place = tables[slot, edge]
             source = lax.div(place, capacity)
             position = place - source * capacity
             group = lax.div(position, 2)
@@ -327,12 +335,17 @@
                 copy.start()
         return carry
 
-    lax.fori_loop(0, count[0], fill, 0)
-    lax.fori_loop(count[0], slots, clear, 0)
+    lax.fori_loop(0, live, fill, 0)
+    lax.fori_loop(live, slots, clear, 0)
+    mine = own_part(pair, me[0], coefficients_out.shape[1])
+    coefficients_ref[...] = (mine[4:8] + last_step(partials, norm) * mine[0:4])[0:3]
+    last_copy = pltpu.make_async_copy(coefficients_ref, coefficients_out, coefficients_done)
+    last_copy.start()
     for slot in range(slots):
         for coordinate in range(3):
             for copy in copies(slot, coordinate):
                 copy.wait()
+    last_copy.wait()
 
 
 def call(kernel, name, outs, specs, scratch=(), megabytes=13, **more):
@@ -356,6 +369,9 @@
     group, capacity = send_list.shape[1:]
     slots = block_tiles.shape[0]
     me = (lax.axis_index("gx") * lax.axis_size("gy") + lax.axis_index("gy")).reshape(1)
+
+    wanted = send_list[0]
+    tables = jnp.concatenate([block_tiles, jnp.broadcast_to(block_count[:, None], (slots, 1))], axis=1)
 
     def spread_out(copies, axes):
         return lax.all_to_all(copies, axes, split_axis=0, concat_axis=0, tiled=True)
@@ -377,9 +393,9 @@
         build_kernel,
         "build",
         [((8, extent), F32), ((extent, 48), BF16), matrix, matrix, thin],
-        [SMEM, VMEM],
+        [SMEM, VMEM, ANY, ANY],
         [pltpu.VMEM((48, width), BF16), kept],
-    )(me, packed)
+    )(me, packed, tables, wanted)
     applied = spread_out(applied, BOTH)
     applied, search, remain, numbers = call(
         turn_one_kernel,
@@ -391,7 +407,7 @@
     partials, pair, norm = call(
         turn_two_kernel,
         "turn_two",
-        [((total, 4, 128), F32), ((8, extent), F32), ((4, 128), F32)],
+        [((total, 1, 128), F32), ((8, extent), F32), ((4, 128), F32)],
         [SMEM] + [VMEM] * 7,
     )(me, every, applied, search, remain, numbers, high, low)
     partials = spread_out(partials, BOTH)
@@ -408,26 +424,25 @@
         [((group, (capacity + 1) // 2 * 4, 128), F32)],
         [SMEM] + [VMEM] * 3,
         [pltpu.VMEM((edge_width // S, 4, S), F32)],
-    )(send_list[0], partials, norm, motions)
+    )(wanted, partials, norm, motions)
     tiles = spread_out(tiles, "gy")
-    (coefficients,) = call(coefficients_kernel, "coefficients", [((3, width), F32)], [SMEM] + [VMEM] * 3)(
-        me, partials, norm, pair
-    )
-    (block_motion,) = call(
+    block_motion, coefficients = call(
         block_kernel,
         "blocks",
-        [((slots, 3, S, S * S), F32)],
-        [SMEM, SMEM, VMEM],
+        [((slots, 3, S, S * S), F32), ((3, width), F32)],
+        [SMEM] * 2 + [VMEM] * 4,
         [
             pltpu.VMEM((3, 12, S), F32),
             pltpu.VMEM((2 * S, S * S), BF16),
             pltpu.VMEM((2, 8, S * S), F32),
             pltpu.VMEM((slots, 3, S, S * S), F32),
+            pltpu.VMEM((3, width), F32),
             pltpu.SemaphoreType.DMA((slots, 3, 2)),
+            pltpu.SemaphoreType.DMA,
         ],
         24,
-        out_specs=(ANY,),
-    )(block_tiles, block_count, tiles)
+        out_specs=(ANY, ANY),
+    )(me, tables, tiles, partials, norm, pair)
     return coefficients, block_motion
 
 

time: 82.5 us -> 81 us (0.982)
  blocking collectives: 19.8 us -> 28.5 us
  waiting for transfers between devices: 12.5 us -> 6.79 us
  starting transfers between devices: 13.7 us -> 9.85 us
  Pallas kernels: 34.4 us -> 32.7 us
  local copies, waits for them, and re-layouts: 0.09 us -> 1.45 us
    all_to_all x2 -> x3, blocking collectives: 19.8 us -> 28.5 us  [spread_out(): return lax.all_to_all(copies, axes, split_axis=0, concat_axis=0, tiled=True)]
    all_to_all x3 -> x2, waiting for transfers between devices: 12.5 us -> 6.79 us  [spread_out(): return lax.all_to_all(copies, axes, split_axis=0, concat_axis=0, tiled=True)]
    all_to_all x3 -> x2, starting transfers between devices: 13.7 us -> 9.85 us  [spread_out(): return lax.all_to_all(copies, axes, split_axis=0, concat_axis=0, tiled=True)]
    pallas_call x1, Pallas kernels: 15.5 us -> 14.6 us  [shards(): call(edge_kernel, 'edges', [((8, edge_width), F32)], [VMEM] * 3, [pltpu.V...]
    pallas_call x3 -> x2, Pallas kernels: 9.23 us -> 9.07 us  [the longest x1 6.7 us: shards(): call(block_kernel, 'blocks', [((slots, 3, S, S * S), F32), ((3, width), F...]
  transfers between devices with their start and end apart: 3 -> 2, of which waited for: 2 -> 1; matrix products, arithmetic and copies ran while one was open for 0% -> 2% of each run, Pallas kernels for 20% -> 18%
where the time goes in v5:
time: 81 us; the launch traced here: 80.6 us
  Pallas kernels  32.7 us (40%)
  blocking collectives  28.5 us (35%)
  starting transfers between devices  9.85 us (12%)
  waiting for transfers between devices  6.79 us (8%)
  local copies, waits for them, and re-layouts  1.45 us (2%)
  between operations  1.34 us (2%)
    all_to_all x3, blocking collectives, spread_out(): return lax.all_to_all(copies, axes, split_axis=0, concat_axis=0, tiled=True)  28.5 us
    pallas_call x1, Pallas kernels, shards(): call(edge_kernel, 'edges', [((8, edge_width), F32)], [VMEM] * 3, [pltpu.V...  14.6 us
    all_to_all x2, starting transfers between devices, spread_out(): return lax.all_to_all(copies, axes, split_axis=0, concat_axis=0, tiled=True)  9.85 us
    all_to_all x2, waiting for transfers between devices, spread_out(): return lax.all_to_all(copies, axes, split_axis=0, concat_axis=0, tiled=True)  6.79 us
    pallas_call x1, Pallas kernels, shards(): call(block_kernel, 'blocks', [((slots, 3, S, S * S), F32), ((3, width), F...  6.7 us
    pallas_call x1, Pallas kernels, shards(): call(build_kernel, 'build', [((8, extent), F32), ((extent, 48), BF16), ma...  4.92 us
    pallas_call x1, Pallas kernels, shards(): call(turn_two_kernel, 'turn_two', [((total, 1, 128), F32), ((8, extent),...  2.37 us
  transfers between devices with their start and end apart: 2, of which 1 were waited for; matrix products, arithmetic and copies ran while one was open for 2% of the time, Pallas kernels for 18%

profile of v5, /device:TPU:0, one launch (start us, length us, event | category | flops | bytes accessed | tf_op | source)
XLA Modules:
  0.0 80.6 jit_solution(9294434707633556735)
XLA Ops:
  0.6 1.5 %pack.1 = f32[32,1,1536]{2,1,0:T(1,128)} custom-call(f32[3,256]{1,0:T(4,128)} %centers.1, f32[3,256]{1,0:T(4,128)} %shifts.1), custom_call_target="tpu_custom_call" | custom-call | flops 1 | bytes 1 | tf_op jit(solution)/shard_map/pack/pallas_call | solution.py:379
  2.1 7.3 %all-to-all-start = ((f32[32,1,1536]{2,1,0:T(1,128)}), f32[32,1,1536]{2,1,0:T(1,128)S(1)}, u32[]{:S(2)}, u32[]{:S(2)}) async-start(f32[32,1,1536]{2,1,0:T(1,128)} %pack.1), calls=%async_computation | async-start | bytes 393216 | tf_op jit(solution)/shard_map/all_to_all | solution.py:377
  10.1 0.8 copy.8
  10.8 0.7 concatenate.3.tables
  11.5 6.8 %all-to-all-done.packed = f32[32,1,1536]{2,1,0:T(1,128)S(1)} async-done(((f32[32,1,1536]{2,1,0:T(1,128)}), f32[32,1,1536]{2,1,0:T(1,128)S(1)}, u32[]{:S(2)}, u32[]{:S(2)}) %all-to-all-start) | async-done | bytes 196640 | tf_op jit(solution)/shard_map/all_to_all | solution.py:377
  18.3 4.9 %build.1 = (f32[8,8192]{1,0:T(8,128)S(1)}, bf16[8192,48]{1,0:T(8,128)(2,1)S(1)}, bf16[8192,256]{1,0:T(8,128)(2,1)S(1)}, bf16[8192,256]{1,0:T(8,128)(2,1)S(1)}, f32[32,1,768]{2,1,0:T(1,128)S(1)}) custom-call(s32[1]{0:T(128)} %bitcast.me, f32[32,1,1536]{2,1,0:T(1,128)S(1)} %all-to-all-done.packed, s32[4,13]{1,0:T(4,128)S(1)} %concatenate.3.tables, ...), custom_call_target="tpu_custom_call" | custom-call | flops 1 | bytes 1 | tf_op jit(solution)/shard_map/build/pallas_call | solution.py:392
  23.2 10.3 %all_to_all.25.applied = f32[32,1,768]{2,1,0:T(1,128)S(1)} all-to-all(f32[32,1,768]{2,1,0:T(1,128)S(1)} %get-tuple-element.17), channel_id=1, replica_groups=mesh['gx'=4,'gy'=8] {'gx','gy'}, dimensions={0} | all-to-all | bytes 196608 | tf_op jit(solution)/shard_map/all_to_all | solution.py:377
  33.5 1.6 %turn_one.1 = (f32[32,1,768]{2,1,0:T(1,128)S(1)}, f32[4,8192]{1,0:T(4,128)S(1)}, f32[4,8192]{1,0:T(4,128)S(1)}, f32[2,4,128]{2,1,0:T(4,128)S(1)}) custom-call(s32[1]{0:T(128)} %bitcast.me, f32[8,8192]{1,0:T(8,128)S(1)} %get-tuple-element.16.every, f32[32,1,768]{2,1,0:T(1,128)S(1)} %all_to_all.25.applied, bf16[8192,256]{1,0:T(8,128)(2,1)S(1)} %get-tuple-element.18.high_ref, ...), custom_call_target="tpu_custom_call" | custom-call | flops 1 | bytes 1 | tf_op jit(solution)/shard_map/turn_one/pallas_call | solution.py:400
  35.1 9.5 %all_to_all.26.applied = f32[32,1,768]{2,1,0:T(1,128)S(1)} all-to-all(f32[32,1,768]{2,1,0:T(1,128)S(1)} %get-tuple-element.20), channel_id=1, replica_groups=mesh['gx'=4,'gy'=8] {'gx','gy'}, dimensions={0} | all-to-all | bytes 196608 | tf_op jit(solution)/shard_map/all_to_all | solution.py:377
  44.6 0.0 copy-start
  44.7 2.4 %turn_two.1 = (f32[32,1,128]{2,1,0:T(1,128)}, f32[8,8192]{1,0:T(8,128)S(1)}, f32[4,128]{1,0:T(4,128)S(1)}) custom-call(s32[1]{0:T(128)} %bitcast.me, f32[8,8192]{1,0:T(8,128)S(1)} %get-tuple-element.16.every, f32[32,1,768]{2,1,0:T(1,128)S(1)} %all_to_all.26.applied, f32[4,8192]{1,0:T(4,128)S(1)} %get-tuple-element.21.search_in, ...), custom_call_target="tpu_custom_call" | custom-call | flops 1 | bytes 1 | tf_op jit(solution)/shard_map/turn_two/pallas_call | solution.py:407
  47.0 2.5 %all-to-all-start.3 = ((f32[32,1,128]{2,1,0:T(1,128)}), f32[32,1,128]{2,1,0:T(1,128)S(1)}, u32[]{:S(2)}, u32[]{:S(2)}) async-start(f32[32,1,128]{2,1,0:T(1,128)} %get-tuple-element.24), calls=%async_computation.3 | async-start | bytes 32768 | tf_op jit(solution)/shard_map/all_to_all | solution.py:377
  49.6 0.0 copy-done
  49.6 14.6 %edges.1.motions = f32[8,1024]{1,0:T(8,128)S(1)} custom-call(bf16[8192,48]{1,0:T(8,128)(2,1)S(1)} %get-tuple-element.26.right_ref, f32[3,1024]{1,0:T(4,128)S(1)} %copy-done, f32[8,8192]{1,0:T(8,128)S(1)} %get-tuple-element.27.pair), custom_call_target="tpu_custom_call" | custom-call | flops 1 | bytes 1 | tf_op jit(solution)/shard_map/edges/pallas_call | solution.py:414
  64.2 0.0 all-to-all-done.3.partials
  64.2 1.1 %pick.1 = f32[8,12,128]{2,1,0:T(8,128)S(1)} custom-call(s32[8,6]{1,0:T(8,128)S(1)} %bitcast.5, f32[32,1,128]{2,1,0:T(1,128)S(1)} %all-to-all-done.3.partials, f32[4,128]{1,0:T(4,128)S(1)} %get-tuple-element.25.norm, f32[8,1024]{1,0:T(8,128)S(1)} %edges.1.motions), custom_call_target="tpu_custom_call" | custom-call | flops 1 | bytes 1 | tf_op jit(solution)/shard_map/pick/pallas_call | solution.py:421
  65.3 8.7 %all_to_all.27.tiles = f32[8,12,128]{2,1,0:T(8,128)S(1)} all-to-all(f32[8,12,128]{2,1,0:T(8,128)S(1)} %pick.1), channel_id=1, replica_groups=mesh['gx'=4,'gy'=8] {'gy'}, dimensions={0} | all-to-all | bytes 98304 | tf_op jit(solution)/shard_map/all_to_all | solution.py:377
  73.9 6.7 %blocks.1 = (f32[4,3,64,4096]{3,2,1,0:T(8,128)}, f32[3,256]{1,0:T(4,128)}) custom-call(s32[1]{0:T(128)} %bitcast.me, s32[4,13]{1,0:T(4,128)S(1)} %concatenate.3.tables, f32[8,12,128]{2,1,0:T(8,128)S(1)} %all_to_all.27.tiles, f32[32,1,128]{2,1,0:T(1,128)S(1)} %all-to-all-done.3.partials, f32[4,128]{1,0:T(4,128)S(1)} %get-tuple-element.25.norm, ...), custom_call_target="tpu_custom_call" | custom-call | flops 1 | bytes 1 | tf_op jit(solution)/shard_map/blocks/pallas_call | solution.py:429
Async XLA Ops:
  2.1 16.2 %all-to-all-start = ((f32[32,1,1536]{2,1,0:T(1,128)}), f32[32,1,1536]{2,1,0:T(1,128)S(1)}, u32[]{:S(2)}, u32[]{:S(2)}) async-start(f32[32,1,1536]{2,1,0:T(1,128)} %pack.1), calls=%async_computation | async-start | bytes 393216 | tf_op jit(solution)/shard_map/all_to_all | solution.py:377
  44.6 4.9 %copy-start = (f32[3,1024]{1,0:T(4,128)S(1)}, f32[3,1024]{1,0:T(4,128)}, u32[]{:S(2)}) copy-start(f32[3,1024]{1,0:T(4,128)} %points.1) | copy-start | bytes 36868
  47.0 17.2 %all-to-all-start.3 = ((f32[32,1,128]{2,1,0:T(1,128)}), f32[32,1,128]{2,1,0:T(1,128)S(1)}, u32[]{:S(2)}, u32[]{:S(2)}) async-start(f32[32,1,128]{2,1,0:T(1,128)} %get-tuple-element.24), calls=%async_computation.3 | async-start | bytes 32768 | tf_op jit(solution)/shard_map/all_to_all | solution.py:377

commit v6 on v5

--- a/solution.py
+++ b/solution.py
@@ -14,11 +14,9 @@
 INV_RADIUS = 4.0
 TINY = 1e-12
 BOTH = ("gx", "gy")
-LARGE = 56
 F32, BF16 = jnp.float32, jnp.bfloat16
 ANY = pl.BlockSpec(memory_space=pl.ANY)
 VMEM = pl.BlockSpec(memory_space=pltpu.VMEM)
-SMEM = pl.BlockSpec(memory_space=pltpu.SMEM)
 PLAIN = (((1,), (0,)), ((), ()))
 LEFT_T = (((0,), (0,)), ((), ()))
 
@@ -83,17 +81,13 @@
     return jnp.concatenate(rows + [jnp.zeros_like(rows[0])], axis=0)
 
 
-def pack_kernel(centers, shifts, out, centers_ref, shifts_ref, done):
-    copies = [
-        pltpu.make_async_copy(centers, centers_ref, done.at[0]),
-        pltpu.make_async_copy(shifts, shifts_ref, done.at[1]),
-    ]
-    for copy in copies:
-        copy.start()
-    for copy in copies:
-        copy.wait()
-    write_copies(shifts_ref[...], out)
-    write_copies(centers_ref[...], out, 3)
+def pack_kernel(stacked, out):
+    write_copies(stacked[0:3, :], out)
+    write_copies(stacked[3:6, :], out, 3)
+
+
+def own_index():
+    return lax.axis_index("gx") * lax.axis_size("gy") + lax.axis_index("gy")
 
 
 def whole_slice(number, size):
@@ -143,13 +137,13 @@
     return end_sum(dot(both, high_ref[...]) + dot(both, low_ref[...]))
 
 
-def build_kernel(me, packed, tables, wanted, every_out, right_ref, high_ref, low_ref, applied_out, left_ref, kept_ref):
+def build_kernel(packed, chosen, placed, every_out, right_ref, high_ref, low_ref, applied_out, left_ref, kept_ref):
     width = left_ref.shape[1]
     shifts = read_copies(packed, width)
     centers = read_copies(packed, width, 3)
     every_out[0:4, :] = shifts
     every_out[4:8, :] = centers
-    mine = own_part(every_out, me[0], width)
+    mine = own_part(every_out, own_index(), width)
     left_ref[...] = features(mine, True)
     right_ref[...] = features(every_out[...], False).T
     keep_vector(jnp.concatenate([shifts, jnp.zeros_like(shifts)], axis=0), kept_ref)
@@ -184,7 +178,7 @@
     return lax.dot_general(ref[...], chosen, PLAIN, precision=lax.Precision.HIGHEST, preferred_element_type=F32)
 
 
-def turn_one_kernel(me, every, applied, high_ref, low_ref, applied_out, search_out, remain_out, numbers_out):
+def turn_one_kernel(every, applied, high_ref, low_ref, applied_out, search_out, remain_out, numbers_out):
     width = high_ref.shape[1]
     start = every[0:4, :]
     got = read_copies(applied, width)
@@ -198,10 +192,10 @@
     numbers_out[0] = jnp.broadcast_to(step, numbers_out.shape[1:])
     numbers_out[1] = jnp.broadcast_to(following, numbers_out.shape[1:])
     product = kept_product(jnp.concatenate([search, jnp.zeros_like(search)], axis=0), high_ref, low_ref)
-    write_copies(product[0:4] + SHIFT * own_part(search_out, me[0], width), applied_out)
-
-
-def turn_two_kernel(me, every, applied, search_in, remain_in, numbers, high_ref, low_ref, partial_out, pair_out, norm_out):
+    write_copies(product[0:4] + SHIFT * own_part(search_out, own_index(), width), applied_out)
+
+
+def turn_two_kernel(every, applied, search_in, remain_in, numbers, high_ref, low_ref, partial_out, pair_out, norm_out):
     width = high_ref.shape[1]
     start = every[0:4, :]
     got = read_copies(applied, width)
@@ -216,7 +210,7 @@
     pair_out[...] = pair
     norm_out[...] = jnp.broadcast_to(following, norm_out.shape)
     product = kept_product(pair, high_ref, low_ref)
-    mine = own_part(pair_out, me[0], width)[0:4]
+    mine = own_part(pair_out, own_index(), width)[0:4]
     product = product[0:4] + SHIFT * mine
     partial = lane_sum(mine * product)
     lane = lax.broadcasted_iota(jnp.int32, (1, partial_out.shape[2]), 1)
@@ -235,18 +229,21 @@
     return ratio(norm[:, 0:1], total)
 
 
-def pick_kernel(send_list, partials, norm, motions, tiles_out, edge_ref):
+def choose(one_hot, values):
+    width = values.shape[1]
+    parts = dot(one_hot, jnp.concatenate(split3(values), axis=1).astype(BF16))
+    return (parts[:, 0:width] + parts[:, width : 2 * width]) + parts[:, 2 * width :]
+
+
+def pick_kernel(chosen, partials, norm, motions, tiles_out, edge_ref):
     motion = motions[4:8, :] + last_step(partials, norm) * motions[0:4, :]
     for edge in range(edge_ref.shape[0]):
         edge_ref[edge] = motion[:, edge * S : (edge + 1) * S]
-    group, capacity = send_list.shape
+    edges = [edge_ref[:, coordinate, :] for coordinate in range(3)]
+    picked = choose(chosen[...], jnp.concatenate(edges + [jnp.zeros_like(edges[0])], axis=1))
+    group, rows, _ = tiles_out.shape
     for place in range(group):
-        for position in range(0, capacity, 2):
-            here = [
-                edge_ref[jnp.maximum(send_list[place, number], 0)]
-                for number in (position, min(position + 1, capacity - 1))
-            ]
-            tiles_out[place, 2 * position : 2 * position + 4, :] = jnp.concatenate(here, axis=1)
+        tiles_out[place] = picked[place * rows : (place + 1) * rows, :]
 
 
 def blend(index):
@@ -262,13 +259,14 @@
     return dot(lefts, rights, LEFT_T)
 
 
-def block_kernel(me, tables, tiles, partials, norm, pair, out, coefficients_out, *scratch):
+def block_kernel(placed, tiles, partials, norm, pair, out, coefficients_out, *scratch):
     tile_ref, spread_ref, weight_ref, held_ref, coefficients_ref, done, coefficients_done = scratch
     slots = out.shape[0]
     cells = S * S
-    capacity = slots * 12 // tiles.shape[0]
-    live = tables[0, 12]
     halves = done.shape[2]
+    arrived = choose(placed[...], jnp.concatenate([tiles[source] for source in range(tiles.shape[0])], axis=0))
+    for slot in range(slots):
+        tile_ref[slot] = arrived[16 * slot : 16 * slot + 16, :]
 
     def copies(slot, coordinate):
         rows = S // halves
@@ -304,20 +302,11 @@
     side = jnp.where(row & 1 == 0, along_low, along_high)
 
     def fill(slot, carry):
-        for edge in range(12):
-            place = tables[slot, edge]
-            source = lax.div(place, capacity)
-            position = place - source * capacity
-            group = lax.div(position, 2)
-            pair = tiles[source, pl.ds(4 * group, 4), :]
-            tile = jnp.where(position == 2 * group, pair[:, 0:S], pair[:, S : 2 * S])
-            for coordinate in range(3):
-                tile_ref[coordinate, edge : edge + 1, :] = tile[coordinate : coordinate + 1, :]
         for coordinate in range(3):
-            first = tile_ref[coordinate, 0:8, :]
+            tile = tile_ref[slot][:, coordinate * S : (coordinate + 1) * S]
+            first, others = tile[0:8], tile[8:16]
             straight = along_low * first[:, 0:1] + along_high * first[:, S - 1 : S]
             bent = jnp.where(row < 4, first - 2.0 * straight, 0.0)
-            others = tile_ref[coordinate, 4:12, :]
             zero = jnp.zeros_like(others)
             placed = jnp.concatenate([jnp.where(row < 4, others, zero), jnp.where(row < 4, zero, others)], axis=1)
             spread = end_sum(dot(jnp.concatenate(split2(placed), axis=0), spread_ref[...]))
@@ -328,16 +317,8 @@
                 copy.start()
         return carry
 
-    def clear(slot, carry):
-        held_ref[slot] = jnp.zeros_like(held_ref[slot])
-        for coordinate in range(3):
-            for copy in copies(slot, coordinate):
-                copy.start()
-        return carry
-
-    lax.fori_loop(0, live, fill, 0)
-    lax.fori_loop(live, slots, clear, 0)
-    mine = own_part(pair, me[0], coefficients_out.shape[1])
+    lax.fori_loop(0, slots, fill, 0)
+    mine = own_part(pair, own_index(), coefficients_out.shape[1])
     coefficients_ref[...] = (mine[4:8] + last_step(partials, norm) * mine[0:4])[0:3]
     last_copy = pltpu.make_async_copy(coefficients_ref, coefficients_out, coefficients_done)
     last_copy.start()
@@ -368,10 +349,14 @@
     edge_width = edge_points.shape[1]
     group, capacity = send_list.shape[1:]
     slots = block_tiles.shape[0]
-    me = (lax.axis_index("gx") * lax.axis_size("gy") + lax.axis_index("gy")).reshape(1)
-
-    wanted = send_list[0]
-    tables = jnp.concatenate([block_tiles, jnp.broadcast_to(block_count[:, None], (slots, 1))], axis=1)
+    rows = -(-capacity // 8) * 8
+    wanted = jnp.pad(send_list[0], ((0, 0), (0, rows - capacity)), constant_values=-1).reshape(group * rows, 1)
+    chosen = (wanted == jnp.arange(edge_width // S)[None, :]).astype(BF16)
+    tile_rows = block_tiles // capacity * rows + block_tiles % capacity
+    tile_rows = jnp.where(jnp.arange(slots)[:, None] < block_count[0], tile_rows, -1)
+    empty = jnp.full((slots, 4), -1, tile_rows.dtype)
+    tile_rows = jnp.concatenate([tile_rows[:, 0:4], empty, tile_rows[:, 4:12]], axis=1).reshape(slots * 16, 1)
+    placed = (tile_rows == jnp.arange(group * rows)[None, :]).astype(BF16)
 
     def spread_out(copies, axes):
         return lax.all_to_all(copies, axes, split_axis=0, concat_axis=0, tiled=True)
@@ -380,10 +365,8 @@
         pack_kernel,
         "pack",
         [((total, 1, 6 * width), F32)],
-        [ANY] * 2,
-        [pltpu.VMEM((3, width), F32)] * 2 + [pltpu.SemaphoreType.DMA((2,))],
-        LARGE,
-    )(center_points, displacements)
+        [VMEM],
+    )(jnp.concatenate([displacements, center_points], axis=0))
     packed = spread_out(packed, BOTH)
     matrix = ((extent, width), BF16)
     thin = ((total, 1, 3 * width), F32)
@@ -393,23 +376,23 @@
         build_kernel,
         "build",
         [((8, extent), F32), ((extent, 48), BF16), matrix, matrix, thin],
-        [SMEM, VMEM, ANY, ANY],
+        [VMEM, ANY, ANY],
         [pltpu.VMEM((48, width), BF16), kept],
-    )(me, packed, tables, wanted)
+    )(packed, chosen, placed)
     applied = spread_out(applied, BOTH)
     applied, search, remain, numbers = call(
         turn_one_kernel,
         "turn_one",
         [thin, ((4, extent), F32), ((4, extent), F32), ((2, 4, 128), F32)],
-        [SMEM] + [VMEM] * 4,
-    )(me, every, applied, high, low)
+        [VMEM] * 4,
+    )(every, applied, high, low)
     applied = spread_out(applied, BOTH)
     partials, pair, norm = call(
         turn_two_kernel,
         "turn_two",
         [((total, 1, 128), F32), ((8, extent), F32), ((4, 128), F32)],
-        [SMEM] + [VMEM] * 7,
-    )(me, every, applied, search, remain, numbers, high, low)
+        [VMEM] * 7,
+    )(every, applied, search, remain, numbers, high, low)
     partials = spread_out(partials, BOTH)
     (motions,) = call(
         edge_kernel,
@@ -421,18 +404,18 @@
     (tiles,) = call(
         pick_kernel,
         "pick",
-        [((group, (capacity + 1) // 2 * 4, 128), F32)],
-        [SMEM] + [VMEM] * 3,
+        [((group, rows, 4 * S), F32)],
+        [VMEM] * 4,
         [pltpu.VMEM((edge_width // S, 4, S), F32)],
-    )(wanted, partials, norm, motions)
+    )(chosen, partials, norm, motions)
     tiles = spread_out(tiles, "gy")
     block_motion, coefficients = call(
         block_kernel,
         "blocks",
         [((slots, 3, S, S * S), F32), ((3, width), F32)],
-        [SMEM] * 2 + [VMEM] * 4,
+        [VMEM] * 5,
         [
-            pltpu.VMEM((3, 12, S), F32),
+            pltpu.VMEM((slots, 16, 4 * S), F32),
             pltpu.VMEM((2 * S, S * S), BF16),
             pltpu.VMEM((2, 8, S * S), F32),
             pltpu.VMEM((slots, 3, S, S * S), F32),
@@ -442,7 +425,7 @@
         ],
         24,
         out_specs=(ANY, ANY),
-    )(me, tables, tiles, partials, norm, pair)
+    )(placed, tiles, partials, norm, pair)
     return coefficients, block_motion
 
 

time: 81 us -> 79.3 us (0.979)
  Pallas kernels: 32.7 us -> 30.3 us
  other arithmetic: 0 us -> 1.7 us
    pallas_call x2, Pallas kernels: 2.54 us -> 1.36 us  [the longest x1 0.73 us: shards(): call(pack_kernel, 'pack', [((total, 1, 6 * width), F32)], [VMEM])]
    pallas_call x1, Pallas kernels: 6.7 us -> 5.68 us  [shards(): call(block_kernel, 'blocks', [((slots, 3, S, S * S), F32), ((3, width), F...]
  transfers between devices with their start and end apart: 2 -> 2, of which waited for: 1 -> 1; matrix products, arithmetic and copies ran while one was open for 2% -> 3% of each run, Pallas kernels for 18% -> 18%
where the time goes in v6:
time: 79.3 us; the launch traced here: 78.9 us
  Pallas kernels  30.3 us (38%)
  blocking collectives  28.5 us (36%)
  starting transfers between devices  9.84 us (12%)
  waiting for transfers between devices  6.15 us (8%)
  other arithmetic  1.7 us (2%)
  between operations  1.34 us (2%)
  local copies, waits for them, and re-layouts  1.09 us (1%)
    all_to_all x3, blocking collectives, spread_out(): return lax.all_to_all(copies, axes, split_axis=0, concat_axis=0, tiled=True)  28.5 us
    pallas_call x1, Pallas kernels, shards(): call(edge_kernel, 'edges', [((8, edge_width), F32)], [VMEM] * 3, [pltpu.V...  14.4 us
    all_to_all x2, starting transfers between devices, spread_out(): return lax.all_to_all(copies, axes, split_axis=0, concat_axis=0, tiled=True)  9.84 us
    all_to_all x2, waiting for transfers between devices, spread_out(): return lax.all_to_all(copies, axes, split_axis=0, concat_axis=0, tiled=True)  6.15 us
    pallas_call x1, Pallas kernels, shards(): call(block_kernel, 'blocks', [((slots, 3, S, S * S), F32), ((3, width), F...  5.68 us
    pallas_call x1, Pallas kernels, shards(): call(build_kernel, 'build', [((8, extent), F32), ((extent, 48), BF16), ma...  4.89 us
    pallas_call x1, Pallas kernels, shards(): call(turn_two_kernel, 'turn_two', [((total, 1, 128), F32), ((8, extent),...  2.39 us
    pallas_call x1, Pallas kernels, shards(): call(turn_one_kernel, 'turn_one', [thin, ((4, extent), F32), ((4, extent)...  1.59 us
  transfers between devices with their start and end apart: 2, of which 1 were waited for; matrix products, arithmetic and copies ran while one was open for 3% of the time, Pallas kernels for 18%

profile of v6, /device:TPU:0, one launch (start us, length us, event | category | flops | bytes accessed | tf_op | source)
XLA Modules:
  0.0 78.9 jit_solution(8369992679652473518)
XLA Ops:
  0.6 0.7 pad_maximum_fusion.stacked
  1.3 0.7 pack.1
  2.1 7.3 %all-to-all-start = ((f32[32,1,1536]{2,1,0:T(1,128)}), f32[32,1,1536]{2,1,0:T(1,128)S(1)}, u32[]{:S(2)}, u32[]{:S(2)}) async-start(f32[32,1,1536]{2,1,0:T(1,128)} %pack.1), calls=%async_computation | async-start | bytes 393216 | tf_op jit(solution)/shard_map/all_to_all | solution.py:362
  10.0 0.8 fusion.3
  10.8 0.1 slice.7
  10.9 0.1 pad.8.clone
  11.0 0.1 pad_add_fusion
  11.0 0.1 eq.32
  11.1 0.8 copy.8
  11.9 0.1 eq.36
  12.0 0.1 fusion.1.chosen
  12.0 0.1 fusion.placed
  12.1 6.2 %all-to-all-done.packed = f32[32,1,1536]{2,1,0:T(1,128)S(1)} async-done(((f32[32,1,1536]{2,1,0:T(1,128)}), f32[32,1,1536]{2,1,0:T(1,128)S(1)}, u32[]{:S(2)}, u32[]{:S(2)}) %all-to-all-start) | async-done | bytes 196640 | tf_op jit(solution)/shard_map/all_to_all | solution.py:362
  18.3 4.9 %build.1 = (f32[8,8192]{1,0:T(8,128)S(1)}, bf16[8192,48]{1,0:T(8,128)(2,1)S(1)}, bf16[8192,256]{1,0:T(8,128)(2,1)S(1)}, bf16[8192,256]{1,0:T(8,128)(2,1)S(1)}, f32[32,1,768]{2,1,0:T(1,128)S(1)}) custom-call(f32[32,1,1536]{2,1,0:T(1,128)S(1)} %all-to-all-done.packed, bf16[64,16]{1,0:T(8,128)(2,1)S(1)} %fusion.1.chosen, bf16[64,64]{1,0:T(8,128)(2,1)S(1)} %fusion.placed), custom_call_target="tpu_custom_call" | custom-call | flops 1 | bytes 1 | tf_op jit(solution)/shard_map/build/pallas_call | solution.py:375
  23.2 10.3 %all_to_all.25.applied = f32[32,1,768]{2,1,0:T(1,128)S(1)} all-to-all(f32[32,1,768]{2,1,0:T(1,128)S(1)} %get-tuple-element.17), channel_id=1, replica_groups=mesh['gx'=4,'gy'=8] {'gx','gy'}, dimensions={0} | all-to-all | bytes 196608 | tf_op jit(solution)/shard_map/all_to_all | solution.py:362
  33.5 1.6 %turn_one.1 = (f32[32,1,768]{2,1,0:T(1,128)S(1)}, f32[4,8192]{1,0:T(4,128)S(1)}, f32[4,8192]{1,0:T(4,128)S(1)}, f32[2,4,128]{2,1,0:T(4,128)S(1)}) custom-call(f32[8,8192]{1,0:T(8,128)S(1)} %get-tuple-element.16.every, f32[32,1,768]{2,1,0:T(1,128)S(1)} %all_to_all.25.applied, bf16[8192,256]{1,0:T(8,128)(2,1)S(1)} %get-tuple-element.18.high_ref, ...), custom_call_target="tpu_custom_call" | custom-call | flops 1 | bytes 1 | tf_op jit(solution)/shard_map/turn_one/pallas_call | solution.py:383
  35.1 9.5 %all_to_all.26.applied = f32[32,1,768]{2,1,0:T(1,128)S(1)} all-to-all(f32[32,1,768]{2,1,0:T(1,128)S(1)} %get-tuple-element.20), channel_id=1, replica_groups=mesh['gx'=4,'gy'=8] {'gx','gy'}, dimensions={0} | all-to-all | bytes 196608 | tf_op jit(solution)/shard_map/all_to_all | solution.py:362
  44.6 0.0 copy-start
  44.6 2.4 %turn_two.1 = (f32[32,1,128]{2,1,0:T(1,128)}, f32[8,8192]{1,0:T(8,128)S(1)}, f32[4,128]{1,0:T(4,128)S(1)}) custom-call(f32[8,8192]{1,0:T(8,128)S(1)} %get-tuple-element.16.every, f32[32,1,768]{2,1,0:T(1,128)S(1)} %all_to_all.26.applied, f32[4,8192]{1,0:T(4,128)S(1)} %get-tuple-element.21.search_in, f32[4,8192]{1,0:T(4,128)S(1)} %get-tuple-element.22.remain_in, ...), custom_call_target="tpu_custom_call" | custom-call | flops 1 | bytes 1 | tf_op jit(solution)/shard_map/turn_two/pallas_call | solution.py:390
  47.0 2.5 %all-to-all-start.3 = ((f32[32,1,128]{2,1,0:T(1,128)}), f32[32,1,128]{2,1,0:T(1,128)S(1)}, u32[]{:S(2)}, u32[]{:S(2)}) async-start(f32[32,1,128]{2,1,0:T(1,128)} %get-tuple-element.24), calls=%async_computation.3 | async-start | bytes 32768 | tf_op jit(solution)/shard_map/all_to_all | solution.py:362
  49.5 0.0 copy-done
  49.6 14.4 %edges.1.motions = f32[8,1024]{1,0:T(8,128)S(1)} custom-call(bf16[8192,48]{1,0:T(8,128)(2,1)S(1)} %get-tuple-element.26.right_ref, f32[3,1024]{1,0:T(4,128)S(1)} %copy-done, f32[8,8192]{1,0:T(8,128)S(1)} %get-tuple-element.27.pair), custom_call_target="tpu_custom_call" | custom-call | flops 1 | bytes 1 | tf_op jit(solution)/shard_map/edges/pallas_call | solution.py:397
  64.0 0.0 all-to-all-done.3.partials
  64.0 0.6 pick.1
  64.6 8.7 %all_to_all.27.tiles = f32[8,8,256]{2,1,0:T(8,128)S(1)} all-to-all(f32[8,8,256]{2,1,0:T(8,128)S(1)} %pick.1), channel_id=1, replica_groups=mesh['gx'=4,'gy'=8] {'gy'}, dimensions={0} | all-to-all | bytes 131072 | tf_op jit(solution)/shard_map/all_to_all | solution.py:362
  73.3 5.7 %blocks.1 = (f32[4,3,64,4096]{3,2,1,0:T(8,128)}, f32[3,256]{1,0:T(4,128)}) custom-call(bf16[64,64]{1,0:T(8,128)(2,1)S(1)} %fusion.placed, f32[8,8,256]{2,1,0:T(8,128)S(1)} %all_to_all.27.tiles, f32[32,1,128]{2,1,0:T(1,128)S(1)} %all-to-all-done.3.partials, f32[4,128]{1,0:T(4,128)S(1)} %get-tuple-element.25.norm, f32[8,8192]{1,0:T(8,128)S(1)} %get-tuple-element.27.pair), custom_call_target="tpu_custom_call" | custom-call | flops 1 | bytes 1 | tf_op jit(solution)/shard_map/blocks/pallas_call | solution.py:412
  (3 shorter events, 0.0 us)
Async XLA Ops:
  2.1 16.2 %all-to-all-start = ((f32[32,1,1536]{2,1,0:T(1,128)}), f32[32,1,1536]{2,1,0:T(1,128)S(1)}, u32[]{:S(2)}, u32[]{:S(2)}) async-start(f32[32,1,1536]{2,1,0:T(1,128)} %pack.1), calls=%async_computation | async-start | bytes 393216 | tf_op jit(solution)/shard_map/all_to_all | solution.py:362
  44.6 4.9 %copy-start = (f32[3,1024]{1,0:T(4,128)S(1)}, f32[3,1024]{1,0:T(4,128)}, u32[]{:S(2)}) copy-start(f32[3,1024]{1,0:T(4,128)} %points.1) | copy-start | bytes 36868
  47.0 17.0 %all-to-all-start.3 = ((f32[32,1,128]{2,1,0:T(1,128)}), f32[32,1,128]{2,1,0:T(1,128)S(1)}, u32[]{:S(2)}, u32[]{:S(2)}) async-start(f32[32,1,128]{2,1,0:T(1,128)} %get-tuple-element.24), calls=%async_computation.3 | async-start | bytes 32768 | tf_op jit(solution)/shard_map/all_to_all | solution.py:362

commit v7 on v6

--- a/solution.py
+++ b/solution.py
@@ -73,12 +73,22 @@
         out[:, :, place : place + width] = jnp.broadcast_to(rows[number : number + 1][None], (out.shape[0], 1, width))
 
 
-def read_copies(ref, width, first=0):
-    rows = []
-    for number in range(3):
-        place = (first + number) * width
-        rows.append(jnp.concatenate([ref[part, :, place : place + width] for part in range(ref.shape[0])], axis=1))
-    return jnp.concatenate(rows + [jnp.zeros_like(rows[0])], axis=0)
+def read_copies(ref, parts, width, first=0):
+    lanes = ref.shape[-1]
+    pieces = []
+    for part in range(parts):
+        if width % 128:
+            start = first * width
+            row = ref[part]
+            values = [row[:, start + number * width : start + (number + 1) * width] for number in range(3)]
+            pieces.append(jnp.concatenate(values, axis=0))
+            continue
+        step = width // lanes
+        for piece in range(step):
+            start = part * (ref.shape[0] // parts) + first * step + piece
+            pieces.append(ref[pl.ds(start, 3, stride=step), :])
+    rows = jnp.concatenate(pieces, axis=1)
+    return jnp.concatenate([rows, jnp.zeros_like(rows[0:1])], axis=0)
 
 
 def pack_kernel(stacked, out):
@@ -139,8 +149,9 @@
 
 def build_kernel(packed, chosen, placed, every_out, right_ref, high_ref, low_ref, applied_out, left_ref, kept_ref):
     width = left_ref.shape[1]
-    shifts = read_copies(packed, width)
-    centers = read_copies(packed, width, 3)
+    parts = right_ref.shape[0] // width
+    shifts = read_copies(packed, parts, width)
+    centers = read_copies(packed, parts, width, 3)
     every_out[0:4, :] = shifts
     every_out[4:8, :] = centers
     mine = own_part(every_out, own_index(), width)
@@ -156,7 +167,7 @@
     padded_ref[4:7, :] = points[...]
     left_ref[...] = features(padded_ref[...], True)
     keep_vector(pair[...], kept_ref)
-    for piece, product in made_product(right_ref, left_ref, kept_ref, 4):
+    for piece, product in made_product(right_ref, left_ref, kept_ref, 8):
         out[:, piece] = product
 
 
@@ -181,7 +192,7 @@
 def turn_one_kernel(every, applied, high_ref, low_ref, applied_out, search_out, remain_out, numbers_out):
     width = high_ref.shape[1]
     start = every[0:4, :]
-    got = read_copies(applied, width)
+    got = read_copies(applied, every.shape[1] // width, width)
     norm = lane_sum(start * start)
     step = ratio(norm, lane_sum(start * got))
     remain = start - step * got
@@ -198,7 +209,7 @@
 def turn_two_kernel(every, applied, search_in, remain_in, numbers, high_ref, low_ref, partial_out, pair_out, norm_out):
     width = high_ref.shape[1]
     start = every[0:4, :]
-    got = read_copies(applied, width)
+    got = read_copies(applied, every.shape[1] // width, width)
     search = search_in[...]
     norm = numbers[1][:, 0:1]
     step = ratio(norm, lane_sum(search * got))
@@ -361,13 +372,16 @@
     def spread_out(copies, axes):
         return lax.all_to_all(copies, axes, split_axis=0, concat_axis=0, tiled=True)
 
+    def rows_of(array):
+        return array if width % 128 else array.reshape(-1, 128)
+
     (packed,) = call(
         pack_kernel,
         "pack",
         [((total, 1, 6 * width), F32)],
         [VMEM],
     )(jnp.concatenate([displacements, center_points], axis=0))
-    packed = spread_out(packed, BOTH)
+    packed = rows_of(spread_out(packed, BOTH))
     matrix = ((extent, width), BF16)
     thin = ((total, 1, 3 * width), F32)
     size = math.gcd(extent, 512)
@@ -379,14 +393,14 @@
         [VMEM, ANY, ANY],
         [pltpu.VMEM((48, width), BF16), kept],
     )(packed, chosen, placed)
-    applied = spread_out(applied, BOTH)
+    applied = rows_of(spread_out(applied, BOTH))
     applied, search, remain, numbers = call(
         turn_one_kernel,
         "turn_one",
         [thin, ((4, extent), F32), ((4, extent), F32), ((2, 4, 128), F32)],
         [VMEM] * 4,
     )(every, applied, high, low)
-    applied = spread_out(applied, BOTH)
+    applied = rows_of(spread_out(applied, BOTH))
     partials, pair, norm = call(
         turn_two_kernel,
         "turn_two",

time: 79.3 us -> 78.7 us (level)
  Pallas kernels: 30.3 us -> 29.5 us
where the time goes in v7:
time: 78.7 us; the launch traced here: 78.3 us
  Pallas kernels  29.5 us (37%)
  blocking collectives  28.3 us (36%)
  starting transfers between devices  10 us (13%)
  waiting for transfers between devices  6.15 us (8%)
  other arithmetic  1.7 us (2%)
  between operations  1.5 us (2%)
  local copies, waits for them, and re-layouts  1.09 us (1%)
    all_to_all x3, blocking collectives, spread_out(): return lax.all_to_all(copies, axes, split_axis=0, concat_axis=0, tiled=True)  28.3 us
    pallas_call x1, Pallas kernels, shards(): call(edge_kernel, 'edges', [((8, edge_width), F32)], [VMEM] * 3, [pltpu.V...  13.8 us
    all_to_all x2, starting transfers between devices, spread_out(): return lax.all_to_all(copies, axes, split_axis=0, concat_axis=0, tiled=True)  10 us
    all_to_all x2, waiting for transfers between devices, spread_out(): return lax.all_to_all(copies, axes, split_axis=0, concat_axis=0, tiled=True)  6.15 us
    pallas_call x1, Pallas kernels, shards(): call(block_kernel, 'blocks', [((slots, 3, S, S * S), F32), ((3, width), F...  5.67 us
    pallas_call x1, Pallas kernels, shards(): call(build_kernel, 'build', [((8, extent), F32), ((extent, 48), BF16), ma...  4.81 us
    pallas_call x1, Pallas kernels, shards(): call(turn_two_kernel, 'turn_two', [((total, 1, 128), F32), ((8, extent),...  2.33 us
  transfers between devices with their start and end apart: 2, of which 1 were waited for; matrix products, arithmetic and copies ran while one was open for 3% of the time, Pallas kernels for 18%

profile of v7, /device:TPU:0, one launch (start us, length us, event | category | flops | bytes accessed | tf_op | source)
XLA Modules:
  0.0 78.3 jit_solution(4996921759173718856)
XLA Ops:
  0.6 0.7 pad_maximum_fusion.stacked
  1.3 0.7 pack.1
  2.1 7.3 %all-to-all-start = ((f32[32,1,1536]{2,1,0:T(1,128)}), f32[32,1,1536]{2,1,0:T(1,128)S(1)}, u32[]{:S(2)}, u32[]{:S(2)}) async-start(f32[32,1,1536]{2,1,0:T(1,128)} %pack.1), calls=%async_computation | async-start | bytes 393216 | tf_op jit(solution)/shard_map/all_to_all | solution.py:373
  10.0 0.8 fusion.3
  10.8 0.1 slice.7
  10.9 0.1 pad.8.clone
  11.0 0.1 pad_add_fusion
  11.0 0.1 eq.32
  11.1 0.8 copy.8
  11.9 0.1 eq.36
  12.0 0.1 fusion.1.chosen
  12.0 0.1 fusion.placed
  12.1 6.2 %all-to-all-done = f32[32,1,1536]{2,1,0:T(1,128)S(1)} async-done(((f32[32,1,1536]{2,1,0:T(1,128)}), f32[32,1,1536]{2,1,0:T(1,128)S(1)}, u32[]{:S(2)}, u32[]{:S(2)}) %all-to-all-start) | async-done | bytes 196640 | tf_op jit(solution)/shard_map/all_to_all | solution.py:373
  18.3 4.8 %build.1 = (f32[8,8192]{1,0:T(8,128)S(1)}, bf16[8192,48]{1,0:T(8,128)(2,1)S(1)}, bf16[8192,256]{1,0:T(8,128)(2,1)S(1)}, bf16[8192,256]{1,0:T(8,128)(2,1)S(1)}, f32[32,1,768]{2,1,0:T(1,128)S(1)}) custom-call(f32[384,128]{1,0:T(8,128)S(1)} %bitcast.7, bf16[64,16]{1,0:T(8,128)(2,1)S(1)} %fusion.1.chosen, bf16[64,64]{1,0:T(8,128)(2,1)S(1)} %fusion.placed), custom_call_target="tpu_custom_call" | custom-call | flops 1 | bytes 1 | tf_op jit(solution)/shard_map/build/pallas_call | solution.py:389
  23.1 10.3 %all_to_all.25 = f32[32,1,768]{2,1,0:T(1,128)S(1)} all-to-all(f32[32,1,768]{2,1,0:T(1,128)S(1)} %get-tuple-element.17), channel_id=1, replica_groups=mesh['gx'=4,'gy'=8] {'gx','gy'}, dimensions={0} | all-to-all | bytes 196608 | tf_op jit(solution)/shard_map/all_to_all | solution.py:373
  33.4 1.5 %turn_one.1 = (f32[32,1,768]{2,1,0:T(1,128)S(1)}, f32[4,8192]{1,0:T(4,128)S(1)}, f32[4,8192]{1,0:T(4,128)S(1)}, f32[2,4,128]{2,1,0:T(4,128)S(1)}) custom-call(f32[8,8192]{1,0:T(8,128)S(1)} %get-tuple-element.16.every, f32[192,128]{1,0:T(8,128)S(1)} %bitcast.9, bf16[8192,256]{1,0:T(8,128)(2,1)S(1)} %get-tuple-element.18.high_ref, ...), custom_call_target="tpu_custom_call" | custom-call | flops 1 | bytes 1 | tf_op jit(solution)/shard_map/turn_one/pallas_call | solution.py:397
  35.0 9.5 %all_to_all.26 = f32[32,1,768]{2,1,0:T(1,128)S(1)} all-to-all(f32[32,1,768]{2,1,0:T(1,128)S(1)} %get-tuple-element.20), channel_id=1, replica_groups=mesh['gx'=4,'gy'=8] {'gx','gy'}, dimensions={0} | all-to-all | bytes 196608 | tf_op jit(solution)/shard_map/all_to_all | solution.py:373
  44.5 0.0 copy-start
  44.5 2.3 %turn_two.1 = (f32[32,1,128]{2,1,0:T(1,128)}, f32[8,8192]{1,0:T(8,128)S(1)}, f32[4,128]{1,0:T(4,128)S(1)}) custom-call(f32[8,8192]{1,0:T(8,128)S(1)} %get-tuple-element.16.every, f32[192,128]{1,0:T(8,128)S(1)} %bitcast.8, f32[4,8192]{1,0:T(4,128)S(1)} %get-tuple-element.21.search_in, f32[4,8192]{1,0:T(4,128)S(1)} %get-tuple-element.22.remain_in, ...), custom_call_target="tpu_custom_call" | custom-call | flops 1 | bytes 1 | tf_op jit(solution)/shard_map/turn_two/pallas_call | solution.py:404
  46.8 2.7 %all-to-all-start.3 = ((f32[32,1,128]{2,1,0:T(1,128)}), f32[32,1,128]{2,1,0:T(1,128)S(1)}, u32[]{:S(2)}, u32[]{:S(2)}) async-start(f32[32,1,128]{2,1,0:T(1,128)} %get-tuple-element.24), calls=%async_computation.3 | async-start | bytes 32768 | tf_op jit(solution)/shard_map/all_to_all | solution.py:373
  49.5 0.0 copy-done
  49.6 13.8 %edges.1.motions = f32[8,1024]{1,0:T(8,128)S(1)} custom-call(bf16[8192,48]{1,0:T(8,128)(2,1)S(1)} %get-tuple-element.26.right_ref, f32[3,1024]{1,0:T(4,128)S(1)} %copy-done, f32[8,8192]{1,0:T(8,128)S(1)} %get-tuple-element.27.pair), custom_call_target="tpu_custom_call" | custom-call | flops 1 | bytes 1 | tf_op jit(solution)/shard_map/edges/pallas_call | solution.py:411
  63.4 0.0 all-to-all-done.3.partials
  63.4 0.6 pick.1
  64.0 8.5 %all_to_all.27.tiles = f32[8,8,256]{2,1,0:T(8,128)S(1)} all-to-all(f32[8,8,256]{2,1,0:T(8,128)S(1)} %pick.1), channel_id=1, replica_groups=mesh['gx'=4,'gy'=8] {'gy'}, dimensions={0} | all-to-all | bytes 131072 | tf_op jit(solution)/shard_map/all_to_all | solution.py:373
  72.5 5.7 %blocks.1 = (f32[4,3,64,4096]{3,2,1,0:T(8,128)}, f32[3,256]{1,0:T(4,128)}) custom-call(bf16[64,64]{1,0:T(8,128)(2,1)S(1)} %fusion.placed, f32[8,8,256]{2,1,0:T(8,128)S(1)} %all_to_all.27.tiles, f32[32,1,128]{2,1,0:T(1,128)S(1)} %all-to-all-done.3.partials, f32[4,128]{1,0:T(4,128)S(1)} %get-tuple-element.25.norm, f32[8,8192]{1,0:T(8,128)S(1)} %get-tuple-element.27.pair), custom_call_target="tpu_custom_call" | custom-call | flops 1 | bytes 1 | tf_op jit(solution)/shard_map/blocks/pallas_call | solution.py:426
  (3 shorter events, 0.0 us)
Async XLA Ops:
  2.1 16.2 %all-to-all-start = ((f32[32,1,1536]{2,1,0:T(1,128)}), f32[32,1,1536]{2,1,0:T(1,128)S(1)}, u32[]{:S(2)}, u32[]{:S(2)}) async-start(f32[32,1,1536]{2,1,0:T(1,128)} %pack.1), calls=%async_computation | async-start | bytes 393216 | tf_op jit(solution)/shard_map/all_to_all | solution.py:373
  44.5 5.1 %copy-start = (f32[3,1024]{1,0:T(4,128)S(1)}, f32[3,1024]{1,0:T(4,128)}, u32[]{:S(2)}) copy-start(f32[3,1024]{1,0:T(4,128)} %points.1) | copy-start | bytes 36868
  46.8 16.6 %all-to-all-start.3 = ((f32[32,1,128]{2,1,0:T(1,128)}), f32[32,1,128]{2,1,0:T(1,128)S(1)}, u32[]{:S(2)}, u32[]{:S(2)}) async-start(f32[32,1,128]{2,1,0:T(1,128)} %get-tuple-element.24), calls=%async_computation.3 | async-start | bytes 32768 | tf_op jit(solution)/shard_map/all_to_all | solution.py:373

commit v8 on v7

--- a/solution.py
+++ b/solution.py
@@ -206,29 +206,30 @@
     write_copies(product[0:4] + SHIFT * own_part(search_out, own_index(), width), applied_out)
 
 
-def turn_two_kernel(every, applied, search_in, remain_in, numbers, high_ref, low_ref, partial_out, pair_out, norm_out):
+def turn_two_kernel(every, applied, search_in, remain_in, numbers, high_ref, low_ref, *rest):
+    partial_out, pair_out, norm_out, partial_ref, done = rest
     width = high_ref.shape[1]
-    start = every[0:4, :]
     got = read_copies(applied, every.shape[1] // width, width)
     search = search_in[...]
     norm = numbers[1][:, 0:1]
     step = ratio(norm, lane_sum(search * got))
-    iterate = numbers[0][:, 0:1] * start + step * search
     remain = remain_in[...] - step * got
     following = lane_sum(remain * remain)
-    search = remain + ratio(following, norm) * search
-    pair = jnp.concatenate([search, iterate], axis=0)
-    pair_out[...] = pair
-    norm_out[...] = jnp.broadcast_to(following, norm_out.shape)
-    product = kept_product(pair, high_ref, low_ref)
+    new_search = remain + ratio(following, norm) * search
+    pair_out[0:4, :] = new_search
+    product = kept_product(jnp.concatenate([new_search, jnp.zeros_like(new_search)], axis=0), high_ref, low_ref)
     mine = own_part(pair_out, own_index(), width)[0:4]
-    product = product[0:4] + SHIFT * mine
-    partial = lane_sum(mine * product)
-    lane = lax.broadcasted_iota(jnp.int32, (1, partial_out.shape[2]), 1)
+    partial = lane_sum(mine * (product[0:4] + SHIFT * mine))
+    lane = lax.broadcasted_iota(jnp.int32, (1, partial_ref.shape[2]), 1)
     row = jnp.zeros(lane.shape, F32)
     for number in range(3):
         row = jnp.where(lane == number, partial[number : number + 1], row)
-    partial_out[...] = jnp.broadcast_to(row[None], partial_out.shape)
+    partial_ref[...] = jnp.broadcast_to(row[None], partial_ref.shape)
+    copy = pltpu.make_async_copy(partial_ref, partial_out, done)
+    copy.start()
+    pair_out[4:8, :] = numbers[0][:, 0:1] * every[0:4, :] + step * search
+    norm_out[...] = jnp.broadcast_to(following, norm_out.shape)
+    copy.wait()
 
 
 def last_step(partials, norm):
@@ -406,6 +407,8 @@
         "turn_two",
         [((total, 1, 128), F32), ((8, extent), F32), ((4, 128), F32)],
         [VMEM] * 7,
+        [pltpu.VMEM((total, 1, 128), F32), pltpu.SemaphoreType.DMA],
+        out_specs=(ANY, VMEM, VMEM),
     )(every, applied, search, remain, numbers, high, low)
     partials = spread_out(partials, BOTH)
     (motions,) = call(
@@ -434,7 +437,7 @@
             pltpu.VMEM((2, 8, S * S), F32),
             pltpu.VMEM((slots, 3, S, S * S), F32),
             pltpu.VMEM((3, width), F32),
-            pltpu.SemaphoreType.DMA((slots, 3, 2)),
+            pltpu.SemaphoreType.DMA((slots, 3, 1)),
             pltpu.SemaphoreType.DMA,
         ],
         24,

time: 78.7 us -> 78.7 us (level)
  no operation moved by 1% of the time
where the time goes in v8:
time: 78.7 us; the launch traced here: 78.3 us
  Pallas kernels  29.5 us (37%)
  blocking collectives  28.3 us (36%)
  starting transfers between devices  10 us (13%)
  waiting for transfers between devices  6.15 us (8%)
  other arithmetic  1.7 us (2%)
  between operations  1.51 us (2%)
  local copies, waits for them, and re-layouts  1.09 us (1%)
    all_to_all x3, blocking collectives, spread_out(): return lax.all_to_all(copies, axes, split_axis=0, concat_axis=0, tiled=True)  28.3 us
    pallas_call x1, Pallas kernels, shards(): call(edge_kernel, 'edges', [((8, edge_width), F32)], [VMEM] * 3, [pltpu.V...  13.8 us
    all_to_all x2, starting transfers between devices, spread_out(): return lax.all_to_all(copies, axes, split_axis=0, concat_axis=0, tiled=True)  10 us
    all_to_all x2, waiting for transfers between devices, spread_out(): return lax.all_to_all(copies, axes, split_axis=0, concat_axis=0, tiled=True)  6.15 us
    pallas_call x1, Pallas kernels, shards(): call(block_kernel, 'blocks', [((slots, 3, S, S * S), F32), ((3, width), F...  5.58 us
    pallas_call x1, Pallas kernels, shards(): call(build_kernel, 'build', [((8, extent), F32), ((extent, 48), BF16), ma...  4.81 us
    pallas_call x1, Pallas kernels, shards(): call(turn_two_kernel, 'turn_two', [((total, 1, 128), F32), ((8, extent),...  2.39 us
  transfers between devices with their start and end apart: 2, of which 1 were waited for; matrix products, arithmetic and copies ran while one was open for 3% of the time, Pallas kernels for 18%

profile of v8, /device:TPU:0, one launch (start us, length us, event | category | flops | bytes accessed | tf_op | source)
XLA Modules:
  0.0 78.3 jit_solution(12323574923816286766)
XLA Ops:
  0.6 0.7 pad_maximum_fusion.stacked
  1.3 0.7 pack.1
  2.1 7.3 %all-to-all-start = ((f32[32,1,1536]{2,1,0:T(1,128)}), f32[32,1,1536]{2,1,0:T(1,128)S(1)}, u32[]{:S(2)}, u32[]{:S(2)}) async-start(f32[32,1,1536]{2,1,0:T(1,128)} %pack.1), calls=%async_computation | async-start | bytes 393216 | tf_op jit(solution)/shard_map/all_to_all | solution.py:374
  10.0 0.8 fusion.3
  10.8 0.1 slice.7
  10.9 0.1 pad.8.clone
  11.0 0.1 pad_add_fusion
  11.0 0.1 eq.32
  11.1 0.8 copy.8
  11.9 0.1 eq.36
  12.0 0.1 fusion.1.chosen
  12.0 0.1 fusion.placed
  12.1 6.2 %all-to-all-done = f32[32,1,1536]{2,1,0:T(1,128)S(1)} async-done(((f32[32,1,1536]{2,1,0:T(1,128)}), f32[32,1,1536]{2,1,0:T(1,128)S(1)}, u32[]{:S(2)}, u32[]{:S(2)}) %all-to-all-start) | async-done | bytes 196640 | tf_op jit(solution)/shard_map/all_to_all | solution.py:374
  18.3 4.8 %build.1 = (f32[8,8192]{1,0:T(8,128)S(1)}, bf16[8192,48]{1,0:T(8,128)(2,1)S(1)}, bf16[8192,256]{1,0:T(8,128)(2,1)S(1)}, bf16[8192,256]{1,0:T(8,128)(2,1)S(1)}, f32[32,1,768]{2,1,0:T(1,128)S(1)}) custom-call(f32[384,128]{1,0:T(8,128)S(1)} %bitcast.7, bf16[64,16]{1,0:T(8,128)(2,1)S(1)} %fusion.1.chosen, bf16[64,64]{1,0:T(8,128)(2,1)S(1)} %fusion.placed), custom_call_target="tpu_custom_call" | custom-call | flops 1 | bytes 1 | tf_op jit(solution)/shard_map/build/pallas_call | solution.py:390
  23.1 10.3 %all_to_all.25 = f32[32,1,768]{2,1,0:T(1,128)S(1)} all-to-all(f32[32,1,768]{2,1,0:T(1,128)S(1)} %get-tuple-element.17), channel_id=1, replica_groups=mesh['gx'=4,'gy'=8] {'gx','gy'}, dimensions={0} | all-to-all | bytes 196608 | tf_op jit(solution)/shard_map/all_to_all | solution.py:374
  33.4 1.5 %turn_one.1 = (f32[32,1,768]{2,1,0:T(1,128)S(1)}, f32[4,8192]{1,0:T(4,128)S(1)}, f32[4,8192]{1,0:T(4,128)S(1)}, f32[2,4,128]{2,1,0:T(4,128)S(1)}) custom-call(f32[8,8192]{1,0:T(8,128)S(1)} %get-tuple-element.16.every, f32[192,128]{1,0:T(8,128)S(1)} %bitcast.9, bf16[8192,256]{1,0:T(8,128)(2,1)S(1)} %get-tuple-element.18.high_ref, ...), custom_call_target="tpu_custom_call" | custom-call | flops 1 | bytes 1 | tf_op jit(solution)/shard_map/turn_one/pallas_call | solution.py:398
  35.0 9.5 %all_to_all.26 = f32[32,1,768]{2,1,0:T(1,128)S(1)} all-to-all(f32[32,1,768]{2,1,0:T(1,128)S(1)} %get-tuple-element.20), channel_id=1, replica_groups=mesh['gx'=4,'gy'=8] {'gx','gy'}, dimensions={0} | all-to-all | bytes 196608 | tf_op jit(solution)/shard_map/all_to_all | solution.py:374
  44.5 0.0 copy-start
  44.5 2.4 %turn_two.1 = (f32[32,1,128]{2,1,0:T(1,128)}, f32[8,8192]{1,0:T(8,128)S(1)}, f32[4,128]{1,0:T(4,128)S(1)}) custom-call(f32[8,8192]{1,0:T(8,128)S(1)} %get-tuple-element.16.every, f32[192,128]{1,0:T(8,128)S(1)} %bitcast.8, f32[4,8192]{1,0:T(4,128)S(1)} %get-tuple-element.21.search_in, f32[4,8192]{1,0:T(4,128)S(1)} %get-tuple-element.22.remain_in, ...), custom_call_target="tpu_custom_call" | custom-call | flops 1 | bytes 1 | tf_op jit(solution)/shard_map/turn_two/pallas_call | solution.py:405
  46.9 2.7 %all-to-all-start.3 = ((f32[32,1,128]{2,1,0:T(1,128)}), f32[32,1,128]{2,1,0:T(1,128)S(1)}, u32[]{:S(2)}, u32[]{:S(2)}) async-start(f32[32,1,128]{2,1,0:T(1,128)} %get-tuple-element.24), calls=%async_computation.3 | async-start | bytes 32768 | tf_op jit(solution)/shard_map/all_to_all | solution.py:374
  49.6 0.0 copy-done
  49.6 13.8 %edges.1.motions = f32[8,1024]{1,0:T(8,128)S(1)} custom-call(bf16[8192,48]{1,0:T(8,128)(2,1)S(1)} %get-tuple-element.26.right_ref, f32[3,1024]{1,0:T(4,128)S(1)} %copy-done, f32[8,8192]{1,0:T(8,128)S(1)} %get-tuple-element.27.pair), custom_call_target="tpu_custom_call" | custom-call | flops 1 | bytes 1 | tf_op jit(solution)/shard_map/edges/pallas_call | solution.py:414
  63.5 0.0 all-to-all-done.3.partials
  63.5 0.6 pick.1
  64.1 8.5 %all_to_all.27.tiles = f32[8,8,256]{2,1,0:T(8,128)S(1)} all-to-all(f32[8,8,256]{2,1,0:T(8,128)S(1)} %pick.1), channel_id=1, replica_groups=mesh['gx'=4,'gy'=8] {'gy'}, dimensions={0} | all-to-all | bytes 131072 | tf_op jit(solution)/shard_map/all_to_all | solution.py:374
  72.6 5.6 %blocks.1 = (f32[4,3,64,4096]{3,2,1,0:T(8,128)}, f32[3,256]{1,0:T(4,128)}) custom-call(bf16[64,64]{1,0:T(8,128)(2,1)S(1)} %fusion.placed, f32[8,8,256]{2,1,0:T(8,128)S(1)} %all_to_all.27.tiles, f32[32,1,128]{2,1,0:T(1,128)S(1)} %all-to-all-done.3.partials, f32[4,128]{1,0:T(4,128)S(1)} %get-tuple-element.25.norm, f32[8,8192]{1,0:T(8,128)S(1)} %get-tuple-element.27.pair), custom_call_target="tpu_custom_call" | custom-call | flops 1 | bytes 1 | tf_op jit(solution)/shard_map/blocks/pallas_call | solution.py:429
  (3 shorter events, 0.0 us)
Async XLA Ops:
  2.1 16.2 %all-to-all-start = ((f32[32,1,1536]{2,1,0:T(1,128)}), f32[32,1,1536]{2,1,0:T(1,128)S(1)}, u32[]{:S(2)}, u32[]{:S(2)}) async-start(f32[32,1,1536]{2,1,0:T(1,128)} %pack.1), calls=%async_computation | async-start | bytes 393216 | tf_op jit(solution)/shard_map/all_to_all | solution.py:374
  44.5 5.2 %copy-start = (f32[3,1024]{1,0:T(4,128)S(1)}, f32[3,1024]{1,0:T(4,128)}, u32[]{:S(2)}) copy-start(f32[3,1024]{1,0:T(4,128)} %points.1) | copy-start | bytes 36868
  46.9 16.6 %all-to-all-start.3 = ((f32[32,1,128]{2,1,0:T(1,128)}), f32[32,1,128]{2,1,0:T(1,128)S(1)}, u32[]{:S(2)}, u32[]{:S(2)}) async-start(f32[32,1,128]{2,1,0:T(1,128)} %get-tuple-element.24), calls=%async_computation.3 | async-start | bytes 32768 | tf_op jit(solution)/shard_map/all_to_all | solution.py:374
